TPU v7x, 128 devices: a whole 4x4x4 slice. The times are simulated.
128 devices in a mesh: ty: 8 (over x_hi, y), tx: 16 (over z, x_lo, core).
Axes of the slice: x: 4 (x_hi: 2, x_lo: 2; x = x_hi * 2 + x_lo), y: 4, z: 4, core: 2. Of those that a mesh axis runs over, the one named last changes fastest.
Arguments:
- region_state: bfloat16 [8, 16, 256, 1024], P('ty', 'tx'), may hold values from -6 to 6
- global_latent: bfloat16 [65536, 1024], P(('ty', 'tx')), may hold values from -6 to 6
- send_rows: int32 [128, 1024], P(('ty', 'tx')), may hold values from 0 to 511, as said below
- recv_slots: int32 [8, 16, 1024], P('ty', 'tx'), may hold values from 0 to 1023, as said below
- regrid_weight: float32 [8, 16, 256, 4], P('ty', 'tx'), may hold values from 0.2 to 1
- window_mask: int32 [8, 16, 5], P('ty', 'tx'), may hold values from 0 to 1, as said below
- norm_gain: bfloat16 [1024], replicated, may hold values from 0.25 to 1.75
- w_query: bfloat16 [1024, 1024], replicated, may hold values from -0.1875 to 0.1875
- w_key: bfloat16 [1024, 1024], replicated, may hold values from -0.1875 to 0.1875
- w_value: bfloat16 [1024, 1024], replicated, may hold values from -0.1875 to 0.1875
- w_out: bfloat16 [1024, 1024], replicated, may hold values from -0.1875 to 0.1875
- out_grad: bfloat16 [8, 16, 256, 1024], P('ty', 'tx'), may hold values from -6 to 6
Outputs:
- updated: bfloat16 [8, 16, 256, 1024], P('ty', 'tx')
- state_grad: bfloat16 [8, 16, 256, 1024], P('ty', 'tx')
- global_grad: bfloat16 [65536, 1024], P(('ty', 'tx'))
- weight_grads: float32 [4, 1024, 1024], P(None, ('ty', 'tx'))
Inputs may be any that keep to these rules, and one draw needn't show every extreme that they name: `send_rows`: each device's list names each of its 512 global rows equally often. `recv_slots`: on every tile each of the 1024 received slots is read, all about equally often. `window_mask`: entry 0 is 1; a flag is 0 where the tile named lies outside the grid; two neighbouring tiles flag each other alike.
All inputs are finite; a program needn't handle non-finite values.
Results may differ from a plain program's by a relative error of at most 0.015.
Values may be sent and summed in bfloat16 or wider, within the bound.
No kernel may reach another device: no remote copies, remote signals or barrier semaphores. Data moves between devices by JAX's collectives and lax.ppermute only.
A program may use at most 128 MiB of HBM per device.

v0:
```python
import functools
import jax
import jax.numpy as jnp
from jax import lax
from jax.experimental import pallas as pl
from jax.experimental.pallas import tpu as pltpu
from jax.sharding import PartitionSpec as P

HEADS = 8
HEAD_SIZE = 128
EPSILON = 1e-05
LOG2_E = 1.4426950408889634
BF16 = jnp.bfloat16
F32 = jnp.float32
NN = (((1,), (0,)), ((), ()))
NT = (((1,), (1,)), ((), ()))
TN = (((0,), (0,)), ((), ()))


def mm(left, right, dims=NN):
    return lax.dot_general(left, right, dims, preferred_element_type=F32)


def params(mib):
    return pltpu.CompilerParams(vmem_limit_bytes=mib * 1024 * 1024)


def pick_kernel(rows_ref, table_ref, out_ref):
    table_rows = table_ref.shape[0]
    hit = lax.broadcasted_iota(jnp.int32, (table_rows, rows_ref.shape[1]), 0) == rows_ref[...]
    out_ref[...] = mm(hit.astype(F32).astype(BF16), table_ref[...], TN).astype(BF16)


def pick_rows(rows, table):
    count, width, step = rows.shape[1], table.shape[1], 256
    return pl.pallas_call(
        pick_kernel,
        grid=(count // step,),
        in_specs=[
            pl.BlockSpec((1, step), lambda i: (0, i)),
            pl.BlockSpec(table.shape, lambda i: (0, 0)),
        ],
        out_specs=pl.BlockSpec((step, width), lambda i: (i, 0)),
        out_shape=jax.ShapeDtypeStruct((count, width), BF16),
        compiler_params=params(60),
        name="pick_rows",
    )(rows, table)


def add_kernel(rows_ref, sent_ref, out_ref):
    step = out_ref.shape[0]
    ids = lax.broadcasted_iota(jnp.int32, (step, rows_ref.shape[1]), 0) + pl.program_id(0) * step
    hit = (ids == rows_ref[...]).astype(F32).astype(BF16)
    out_ref[...] = mm(hit, sent_ref[...]).astype(BF16)


def add_rows(rows, sent, table_rows):
    step = 256
    return pl.pallas_call(
        add_kernel,
        grid=(table_rows // step,),
        in_specs=[
            pl.BlockSpec(rows.shape, lambda i: (0, 0)),
            pl.BlockSpec(sent.shape, lambda i: (0, 0)),
        ],
        out_specs=pl.BlockSpec((step, sent.shape[1]), lambda i: (i, 0)),
        out_shape=jax.ShapeDtypeStruct((table_rows, sent.shape[1]), BF16),
        compiler_params=params(14),
        name="add_rows",
    )(rows, sent)


def blend_kernel(slots_ref, blend_ref, incoming_ref, state_ref, gain_ref, in_ref, normed_ref, inverse_ref, high_ref, low_ref):
    rows, slots = blend_ref.shape[0], incoming_ref.shape[0]
    lanes = lax.broadcasted_iota(jnp.int32, (rows, slots), 1)
    spread = jnp.zeros((rows, slots), F32)
    for k in range(blend_ref.shape[1]):
        spread = spread + jnp.where(lanes == slots_ref[:, k : k + 1], blend_ref[:, k : k + 1], 0.0)
    high = spread.astype(BF16)
    low = (spread - high.astype(F32)).astype(BF16)
    high_ref[...] = high
    low_ref[...] = low
    incoming = incoming_ref[...]
    pre = state_ref[...].astype(F32) + (mm(high, incoming) + mm(low, incoming))
    inverse = lax.rsqrt(jnp.mean(pre * pre, axis=-1, keepdims=True) + EPSILON)
    normed = pre * inverse
    normed_ref[...] = normed
    inverse_ref[...] = jnp.broadcast_to(inverse, inverse_ref.shape)
    in_ref[...] = (normed * gain_ref[...].astype(F32)).astype(BF16)


def blend_norm(slots, blend, incoming, state, gain):
    rows, width = state.shape
    spread = jax.ShapeDtypeStruct((rows, incoming.shape[0]), BF16)
    return pl.pallas_call(
        blend_kernel,
        out_shape=(
            jax.ShapeDtypeStruct((rows, width), BF16),
            jax.ShapeDtypeStruct((rows, width), F32),
            jax.ShapeDtypeStruct((rows, 128), F32),
            spread,
            spread,
        ),
        compiler_params=params(60),
        name="blend_norm",
    )(slots, blend, incoming, state, gain)


def attend_kernel(
    core_ref, mask_ref, own_ref, up_ref, down_ref, left_ref, right_ref, grad_ref, wq_ref, wk_ref, wv_ref, wo_ref,
    keep_y, send_y, keep_z, send_z, attended_ref, up_grad, down_grad, left_grad, right_grad, own_grad, x_all, x_turned, grads,
):
    step = pl.program_id(0)
    rows = own_ref.shape[0]
    blocks = x_all.shape[0] // rows
    ys, _, _, _, lanes = keep_y.shape
    zs, _, _, piece, _ = keep_z.shape

    @pl.when(step == 0)
    def _():
        for b, ref in enumerate((own_ref, up_ref, down_ref, left_ref, right_ref)):
            x_all[b * rows : (b + 1) * rows] = ref[...]
            x_turned[:, b * rows : (b + 1) * rows] = ref[...].T
        grads[...] = jnp.zeros_like(grads)

    grad_out = grad_ref[...]
    width = grad_out.shape[1]
    scale = HEAD_SIZE ** (-0.5)
    query = mm(own_ref[...], wq_ref[...]).astype(BF16)
    g = mm(grad_out, wo_ref[...], NT).astype(BF16)
    key = mm(x_all[...], wk_ref[...]).astype(BF16)
    value = mm(x_all[...], wv_ref[...]).astype(BF16)
    query_t, g_t = query.T, g.T
    attended_t, dquery_t, dkey, dvalue = [], [], [], []
    for h in range(lanes // HEAD_SIZE):
        at = slice(h * HEAD_SIZE, (h + 1) * HEAD_SIZE)
        raw = mm(key[:, at], query_t[at])
        scores = jnp.concatenate(
            [
                raw[b * rows : (b + 1) * rows] * (scale * LOG2_E) + jnp.where(mask_ref[0, b] > 0, 0.0, -1e30)
                for b in range(blocks)
            ],
            axis=0,
        )
        highest = jnp.max(scores, axis=0, keepdims=True)
        raised = jnp.exp2(scores - highest)
        prob = raised * (1.0 / jnp.sum(raised, axis=0, keepdims=True))
        weights = prob.astype(BF16)
        att = mm(value[:, at], weights, TN).astype(BF16)
        delta = jnp.sum(g_t[at].astype(F32) * att.astype(F32), axis=0, keepdims=True)
        dscore = (prob * (mm(value[:, at], g_t[at]) - delta) * scale).astype(BF16)
        attended_t.append(att)
        dquery_t.append(mm(key[:, at], dscore, TN).astype(BF16))
        dkey.append(mm(dscore, query[:, at]).astype(BF16))
        dvalue.append(mm(weights, g[:, at]).astype(BF16))
    attended_t = jnp.concatenate(attended_t, axis=0)
    dquery = jnp.concatenate(dquery_t, axis=0).T
    dkey = jnp.concatenate(dkey, axis=1)
    dvalue = jnp.concatenate(dvalue, axis=1)
    attended_ref[...] = attended_t.T
    grads[...] += mm(jnp.concatenate([dkey, dvalue], axis=1), jnp.concatenate([wk_ref[...], wv_ref[...]], axis=1), NT)
    grads[:rows] += mm(dquery, wq_ref[...], NT)
    first = core_ref[0] == 0

    def place(keep_ref, send_ref, at, m, where, halves):
        low, high = (half.reshape(-1, lanes) for half in halves)
        keep_ref[at, m, 0, where] = jnp.where(first, low, high).astype(BF16)
        send_ref[at, m, 0, where] = jnp.where(first, high, low).astype(BF16)

    chunk = piece // 16
    every = slice(None)
    for m, part in enumerate((mm(x_turned[:, :rows], dquery), mm(x_turned[...], dkey))):
        part = part.reshape(2, ys, zs, 2, 2, chunk, lanes)
        for y in range(ys):
            place(keep_y, send_y, y, m, every, [part[:, y, :, :, c] for c in range(2)])
    part = mm(x_turned[...], dvalue).reshape(2 * ys, zs, 2, 2, chunk, lanes)
    for z in range(zs):
        place(keep_z, send_z, z, 0, every, [part[:, z, :, c] for c in range(2)])
    part = mm(attended_t, grad_out).reshape(2, zs, 2, 2, chunk, width)
    for z in range(zs):
        for q in range(4):
            columns = slice(q * lanes, (q + 1) * lanes)
            rows_of = slice(q * piece // 4, (q + 1) * piece // 4)
            place(keep_z, send_z, z, 1, rows_of, [part[:, z, :, c, :, columns] for c in range(2)])

    @pl.when(step == pl.num_programs(0) - 1)
    def _():
        own_grad[...] = grads[:rows]
        for b, ref in enumerate((up_grad, down_grad, left_grad, right_grad), 1):
            ref[...] = grads[b * rows : (b + 1) * rows].astype(BF16)


def attend(core, mask, tiles, grad_out, w_query, w_key, w_value, w_out, ys, zs):
    rows, width = grad_out.shape
    near, lanes = len(tiles), 2 * HEAD_SIZE
    steps = width // lanes
    whole = lambda: pl.BlockSpec((rows, width), lambda h: (0, 0), pipeline_mode=pl.Buffered(1))
    columns = lambda: pl.BlockSpec((width, lanes), lambda h: (0, h))
    flags = lambda: pl.BlockSpec(memory_space=pltpu.SMEM)
    parts = lambda n: pl.BlockSpec((n, 2, 1, width // 2 // n, lanes), lambda h: (0, 0, h, 0, 0))
    out = lambda n: pl.BlockSpec((n, lanes), lambda h: (0, h))
    part = lambda n: jax.ShapeDtypeStruct((n, 2, steps, width // 2 // n, lanes), BF16)
    small = jax.ShapeDtypeStruct((rows, width), BF16)
    return pl.pallas_call(
        attend_kernel,
        grid=(steps,),
        in_specs=[flags(), flags()]
        + [whole() for _ in range(near + 1)]
        + [columns(), columns(), columns(), pl.BlockSpec((lanes, width), lambda h: (h, 0))],
        out_specs=[parts(ys), parts(ys), parts(zs), parts(zs), out(rows)]
        + [whole() for _ in range(near)],
        out_shape=(part(ys), part(ys), part(zs), part(zs)) + (small,) * near + (jax.ShapeDtypeStruct((rows, width), F32),),
        scratch_shapes=[
            pltpu.VMEM((near * rows, width), BF16),
            pltpu.VMEM((width, near * rows), BF16),
            pltpu.VMEM((near * rows, width), F32),
        ],
        compiler_params=params(60),
        cost_estimate=pl.CostEstimate(flops=34 * 10**9, bytes_accessed=32 * 10**6, transcendentals=10**6),
        name="attend",
    )(core, mask, *tiles, grad_out, w_query, w_key, w_value, w_out)


def split_kernel(here_ref, keep_ref, came_ref, *out_refs):
    count = len(out_refs)
    for step, ref in enumerate(out_refs):
        at = (here_ref[0] + step) % count
        ref[...] = (keep_ref[at].astype(F32) + came_ref[at].astype(F32)).astype(BF16)


def split_sum(here, keep, came):
    count, mats, steps, *rest = keep.shape
    whole = lambda: pl.BlockSpec((count, mats, 1, *rest), lambda s: (0, 0, s, 0, 0))
    return pl.pallas_call(
        split_kernel,
        grid=(steps,),
        in_specs=[pl.BlockSpec(memory_space=pltpu.SMEM), whole(), whole()],
        out_specs=[pl.BlockSpec((mats, 1, *rest), lambda s: (0, s, 0, 0)) for _ in range(count)],
        out_shape=tuple(jax.ShapeDtypeStruct((mats, steps, *rest), BF16) for _ in range(count)),
        compiler_params=params(60),
        cost_estimate=pl.CostEstimate(flops=10**6, bytes_accessed=6 * 10**6, transcendentals=0),
        name="split_sum",
    )(here, keep, came)


def join_kernel(pieces, out_matrix, here_ref, *refs):
    in_refs, out_refs, table = refs[:pieces], refs[pieces:-1], refs[-1]
    count = len(out_refs)
    chunk = out_refs[0].shape[3]

    def totals():
        for s in range(in_refs[0].shape[1]):
            total = in_refs[0][0, s].astype(F32)
            for ref in in_refs[1:]:
                total = total + ref[0, s].astype(F32)
            yield s, total

    @pl.when(pl.program_id(0) != out_matrix)
    def _():
        for s, total in totals():
            lanes = total.shape[1]
            total = total.reshape(2, count, 2, chunk, lanes)
            for n in range(count):
                table[n, :, :, :, s * lanes : (s + 1) * lanes] = total[:, n]

    if out_matrix >= 0:

        @pl.when(pl.program_id(0) == out_matrix)
        def _():
            for s, total in totals():
                lanes = total.shape[1]
                total = total.reshape(4, 2, 2, chunk, lanes)
                for q in range(4):
                    for y in range(2):
                        table[s % 2 * 2 + y, s // 2, :, :, q * lanes : (q + 1) * lanes] = total[q, y]

    for step, ref in enumerate(out_refs):
        ref[:, :, 0] = table[(here_ref[0] + step) % count].astype(BF16)


def join_sum(here, parts, count, out_matrix, chunk):
    mats, steps, piece, lanes = parts[0].shape
    width = steps * lanes
    return pl.pallas_call(
        functools.partial(join_kernel, len(parts), out_matrix),
        grid=(mats,),
        in_specs=[pl.BlockSpec(memory_space=pltpu.SMEM)]
        + [pl.BlockSpec((1, steps, piece, lanes), lambda m: (m, 0, 0, 0)) for _ in parts],
        out_specs=[pl.BlockSpec((2, 2, 1, chunk, width), lambda m: (0, 0, m, 0, 0)) for _ in range(count)],
        out_shape=tuple(jax.ShapeDtypeStruct((2, 2, mats, chunk, width), BF16) for _ in range(count)),
        scratch_shapes=[pltpu.VMEM((count, 2, 2, chunk, width), F32)],
        compiler_params=params(60),
        cost_estimate=pl.CostEstimate(flops=10**6, bytes_accessed=6 * 10**6, transcendentals=0),
        name="join_sum",
    )(here, *parts)


def finish_kernel(own_ref, up_ref, down_ref, left_ref, right_ref, normed_ref, inverse_ref, gain_ref, grad_ref, high_ref, low_ref, state_grad_ref, slot_ref):
    total = own_ref[...]
    for ref in (up_ref, down_ref, left_ref, right_ref):
        total = total + ref[...].astype(F32)
    grad = total * gain_ref[...].astype(F32)
    normed = normed_ref[...]
    grad = inverse_ref[:, :1] * (grad - normed * jnp.mean(grad * normed, axis=-1, keepdims=True))
    state_grad_ref[...] = (grad_ref[...].astype(F32) + grad).astype(BF16)
    top = grad.astype(BF16)
    rest = (grad - top.astype(F32)).astype(BF16)
    slot_ref[...] = (mm(high_ref[...], top, TN) + (mm(high_ref[...], rest, TN) + mm(low_ref[...], top, TN))).astype(BF16)


def finish(own, near, normed, inverse, gain, grad_out, high, low):
    rows, width = own.shape
    return pl.pallas_call(
        finish_kernel,
        out_shape=(
            jax.ShapeDtypeStruct((rows, width), BF16),
            jax.ShapeDtypeStruct((high.shape[1], width), BF16),
        ),
        compiler_params=params(60),
        name="finish",
    )(own, *near, normed, inverse, gain, grad_out, high, low)


def after(value, others):
    return lax.optimization_barrier((value, others))[0]


def shifted(block, axis, step):
    count = lax.axis_size(axis)
    return lax.ppermute(block, axis, [(i, (i + step) % count) for i in range(count)])


def swapped(chunks, axis):
    return [chunks[0]] + [shifted(chunk, axis, step) for step, chunk in enumerate(chunks) if step]


def passed_along(block, axis, distance):
    count = lax.axis_size(axis)
    route = [(i, i + distance) for i in range(count) if 0 <= i + distance < count]
    return lax.ppermute(block, axis, route)


TY = ("x_hi", "y")
TX = ("z", "x_lo", "core")
X = ("x_hi", "x_lo")


def body(
    region_state,
    global_latent,
    send_rows,
    recv_slots,
    regrid_weight,
    window_mask,
    norm_gain,
    w_query,
    w_key,
    w_value,
    w_out,
    out_grad,
):
    state, grad_out = region_state[0, 0], out_grad[0, 0]
    rows, width = state.shape
    gain = norm_gain[None]
    devices = lax.axis_size(TY + TX)
    outgoing = pick_rows(send_rows, global_latent)
    incoming = lax.all_to_all(outgoing, TY + TX, split_axis=0, concat_axis=0, tiled=True)
    normed_in, normed, inverse, high, low = blend_norm(
        recv_slots.reshape(rows, -1), regrid_weight[0, 0], incoming, state, gain
    )
    tiles = (
        normed_in,
        passed_along(normed_in, TY, 1),
        passed_along(normed_in, TY, -1),
        passed_along(normed_in, TX, 1),
        passed_along(normed_in, TX, -1),
    )
    here = {axis: lax.axis_index(axis).reshape(1) for axis in ("z", "y", "core", "x_hi", "x_lo")}
    chunk = width // devices
    ys, zs = lax.axis_size("y"), lax.axis_size("z")
    keep_y, send_y, keep_z, send_z, attended, *near, own = attend(
        here["core"], window_mask[0], tiles, grad_out, w_query, w_key, w_value, w_out, ys, zs
    )
    came_y, came_z = shifted(send_y, "core", 1), shifted(send_z, "core", 1)
    returned = (
        passed_along(near[0], TY, -1),
        passed_along(near[1], TY, 1),
        passed_along(near[2], TX, -1),
        passed_along(near[3], TX, 1),
    )
    along_z = swapped(split_sum(here["z"], keep_z, came_z), "z")
    along_y = swapped(split_sum(here["y"], keep_y, came_y), "y")
    own = after(own, (along_z[0], along_y[0]))
    state_grad, slots = finish(own, returned, normed, inverse, gain, grad_out, high, low)
    sent_back = lax.all_to_all(after(slots, (along_z, along_y)), TY + TX, split_axis=0, concat_axis=0, tiled=True)
    global_grad = add_rows(send_rows, sent_back, global_latent.shape[0])
    here_y, here_z = after((here["y"], here["z"]), slots)
    second_z = swapped(join_sum(here_z, along_y, zs, -1, chunk), "z")
    second_y = swapped(join_sum(here_y, along_z, ys, 1, chunk), "y")
    total = jnp.concatenate([sum(piece.astype(F32) for piece in group) for group in (second_z, second_y)], axis=2)
    total = total.astype(BF16).reshape(-1, 4, chunk, width)
    term = jnp.dot(attended, w_out, preferred_element_type=F32)
    updated = (state.astype(F32) + term).astype(BF16)
    total = after(total, updated)
    place = lax.axis_index(X)
    along_x = swapped([lax.dynamic_index_in_dim(total, (place + k) % total.shape[0], 0, keepdims=False) for k in range(total.shape[0])], X)
    weight_grads = sum(piece.astype(F32) for piece in after(along_x[:1], global_grad) + along_x[1:])
    return (updated[None, None], state_grad[None, None], global_grad, weight_grads)


def solution(mesh):
    ty, tx = mesh.devices.shape
    y, z = max(ty // 2, 1), tx // 4
    fine = jax.sharding.Mesh(mesh.devices.reshape(ty // y, y, z, 2, 2), TY + TX)
    tiles = P(TY, TX)
    flat = P(TY + TX)
    return jax.shard_map(
        body,
        mesh=fine,
        in_specs=(tiles, flat, flat, tiles, tiles, tiles, P(), P(), P(), P(), P(), tiles),
        out_specs=(tiles, tiles, flat, P(None, TY + TX)),
        check_vma=False,
    )
```

profile of v0, /device:TPU:0, one launch (start us, length us, event | category | flops | bytes accessed | tf_op | source)
XLA Modules:
  0.0 239.6 jit_solution(13816562127926864915)
XLA Ops:
  0.6 4.5 %pick_rows.1 = bf16[1024,1024]{1,0:T(8,128)(2,1)} custom-call(s32[1,1024]{1,0:T(1,128)} %rows_ref.3, bf16[512,1024]{1,0:T(8,128)(2,1)} %table_ref.1), custom_call_target="tpu_custom_call" | custom-call | tf_op jit(solution)/shard_map/pick_rows/pallas_call | solution.py:36
  5.1 11.1 %all-to-all-start = ((bf16[128,8,1024]{2,1,0:T(8,128)(2,1)}), bf16[128,8,1024]{2,1,0:T(8,128)(2,1)S(1)}, u32[]{:S(2)}, u32[]{:S(2)}) async-start(bf16[128,8,1024]{2,1,0:T(8,128)(2,1)} %bitcast.28), calls=%async_computation | async-start | bytes 4194304 | tf_op jit(solution)/shard_map/all_to_all | solution.py:367
  19.6 27.1 %all-to-all-done = bf16[128,8,1024]{2,1,0:T(8,128)(2,1)S(1)} async-done(((bf16[128,8,1024]{2,1,0:T(8,128)(2,1)}), bf16[128,8,1024]{2,1,0:T(8,128)(2,1)S(1)}, u32[]{:S(2)}, u32[]{:S(2)}) %all-to-all-start) | async-done | bytes 2097184 | tf_op jit(solution)/shard_map/all_to_all | solution.py:367
  48.0 5.0 %blend_norm.1 = (bf16[256,1024]{1,0:T(8,128)(2,1)}, f32[256,1024]{1,0:T(8,128)}, f32[256,128]{1,0:T(8,128)}, bf16[256,1024]{1,0:T(8,128)(2,1)}, bf16[256,1024]{1,0:T(8,128)(2,1)}) custom-call(s32[256,4]{1,0:T(8,128)} %reshape.30.slots_ref, f32[256,4]{1,0:T(8,128)} %bitcast.32, bf16[1024,1024]{1,0:T(8,128)(2,1)} %bitcast.27, bf16[256,1024]{1,0:T(8,128)(2,1)} %bitcast.35, ...), custom_call_target="tpu_custom_call" | custom-call | tf_op jit(solution)/shard_map/blend_norm/pallas_call | solution.py:95
  58.5 7.2 %collective-permute-done.up_ref = bf16[256,1024]{1,0:T(8,128)(2,1)S(1)} collective-permute-done((bf16[256,1024]{1,0:T(8,128)(2,1)}, bf16[256,1024]{1,0:T(8,128)(2,1)S(1)}, u32[]{:S(2)}, u32[]{:S(2)}) %collective-permute-start) | collective-permute-done | bytes 524320 | tf_op jit(solution)/shard_map/ppermute | solution.py:340
  65.7 4.0 %collective-permute-done.1.down_ref = bf16[256,1024]{1,0:T(8,128)(2,1)S(1)} collective-permute-done((bf16[256,1024]{1,0:T(8,128)(2,1)}, bf16[256,1024]{1,0:T(8,128)(2,1)S(1)}, u32[]{:S(2)}, u32[]{:S(2)}) %collective-permute-start.1) | collective-permute-done | bytes 524320 | tf_op jit(solution)/shard_map/ppermute | solution.py:340
  70.9 41.0 %attend.1 = (bf16[4,2,4,128,256]{4,3,2,1,0:T(8,128)(2,1)}, bf16[4,2,4,128,256]{4,3,2,1,0:T(8,128)(2,1)}, bf16[4,2,4,128,256]{4,3,2,1,0:T(8,128)(2,1)}, bf16[4,2,...) custom-call(s32[1]{0:T(128)} %bitcast.1.core_ref, ...), custom_call_target="tpu_custom_call" | custom-call | flops 33999998976 | bytes 32000000 | tf_op jit(solution)/shard_map/attend/pallas_call | solution.py:204
  114.5 6.0 %collective-permute-start.7 = (bf16[256,1024]{1,0:T(8,128)(2,1)}, bf16[256,1024]{1,0:T(8,128)(2,1)}, u32[]{:S(2)}, u32[]{:S(2)}) collective-permute-start(bf16[256,1024]{1,0:T(8,128)(2,1)} %get-tuple-element.54), channel_id=1, source_target_pairs={{0,16},{16,32},{32,48},{48,64},{64,80},{80,96},{96,112},{1,17},{17... | collective-permute-start | bytes 1572872 | tf_op jit(solution)/shard_map/ppermute | solution.py:340
  121.8 3.9 %collective-permute-start.9 = (bf16[256,1024]{1,0:T(8,128)(2,1)}, bf16[256,1024]{1,0:T(8,128)(2,1)}, u32[]{:S(2)}, u32[]{:S(2)}) collective-permute-start(bf16[256,1024]{1,0:T(8,128)(2,1)} %get-tuple-element.56), channel_id=1, source_target_pairs={{0,1},{1,2},{2,3},{3,4},{4,5},{5,6},{6,7},{7,8},{8,9},{9,10},{10,1... | collective-permute-start | bytes 1572872 | tf_op jit(solution)/shard_map/ppermute | solution.py:340
  125.7 4.3 %split_sum.3 = (bf16[2,4,128,256]{3,2,1,0:T(8,128)(2,1)}, bf16[2,4,128,256]{3,2,1,0:T(8,128)(2,1)}, bf16[2,4,128,256]{3,2,1,0:T(8,128)(2,1)}, bf16[2,4,128,256]{3,2,1,0:T(8,128)(2,1)}) custom-call(s32[1]{0:T(128)} %bitcast.9.here_ref, bf16[4,2,4,128,256]{4,3,2,1,0:T(8,128)(2,1)} %get-tuple-element.49.keep_ref, ...), custom_call_target="tpu_custom_call" | custom-call | flops 1000000 | bytes 6000000 | tf_op jit(solution)/shard_map/split_sum/pallas_call | solution.py:234
  131.3 4.3 %split_sum.2 = (bf16[2,4,128,256]{3,2,1,0:T(8,128)(2,1)}, bf16[2,4,128,256]{3,2,1,0:T(8,128)(2,1)}, bf16[2,4,128,256]{3,2,1,0:T(8,128)(2,1)}, bf16[2,4,128,256]{3,2,1,0:T(8,128)(2,1)}) custom-call(s32[1]{0:T(128)} %bitcast.8.here_ref, bf16[4,2,4,128,256]{4,3,2,1,0:T(8,128)(2,1)} %get-tuple-element.46.keep_ref, bf16[4,2,4,128,256]{4,3,2,1,0:T(8,128)(2,1)} %copy-done.2), custom_call_target="tpu_custom_call" | custom-call | flops 1000000 | bytes 6000000 | tf_op jit(solution)/shard_map/split_sum/pallas_call | solution.py:234
  135.7 15.5 %collective-permute-start.14 = (bf16[2,4,128,256]{3,2,1,0:T(8,128)(2,1)}, bf16[2,4,128,256]{3,2,1,0:T(8,128)(2,1)S(1)}, u32[]{:S(2)}, u32[]{:S(2)}) collective-permute-start(bf16[2,4,128,256]{3,2,1,0:T(8,128)(2,1)} %get-tuple-element.67), channel_id=1, source_target_pairs={{0,32},{16,48},{32,0},{48,16},{1,33},{17,49},{33,1},{49,17},{2,34}... | collective-permute-start | bytes 1572872 | tf_op jit(solution)/shard_map/ppermute | solution.py:330
  154.0 4.1 %collective-permute-done.13.refs_1_ = bf16[2,4,128,256]{3,2,1,0:T(8,128)(2,1)S(1)} collective-permute-done((bf16[2,4,128,256]{3,2,1,0:T(8,128)(2,1)}, bf16[2,4,128,256]{3,2,1,0:T(8,128)(2,1)S(1)}, u32[]{:S(2)}, u32[]{:S(2)}) %collective-permute-start.13) | collective-permute-done | bytes 524320 | tf_op jit(solution)/shard_map/ppermute | solution.py:330
  159.1 6.5 %finish.1 = (bf16[256,1024]{1,0:T(8,128)(2,1)}, bf16[1024,1024]{1,0:T(8,128)(2,1)}) custom-call(f32[256,1024]{1,0:T(8,128)} %get-tuple-element.52.own_ref, bf16[256,1024]{1,0:T(8,128)(2,1)} %copy-done.7, bf16[256,1024]{1,0:T(8,128)(2,1)} %collective-permute-done.7.down_ref, bf16[256,1024]{1,0:T(8,128)(2,1)} %collective-permute-done.8.left_ref, ...), custom_call_target="tpu_custom_call" | custom-call | tf_op jit(solution)/shard_map/finish/pallas_call | solution.py:313
  165.5 5.0 %collective-permute-done.14.refs_2_ = bf16[2,4,128,256]{3,2,1,0:T(8,128)(2,1)S(1)} collective-permute-done((bf16[2,4,128,256]{3,2,1,0:T(8,128)(2,1)}, bf16[2,4,128,256]{3,2,1,0:T(8,128)(2,1)S(1)}, u32[]{:S(2)}, u32[]{:S(2)}) %collective-permute-start.14) | collective-permute-done | bytes 524320 | tf_op jit(solution)/shard_map/ppermute | solution.py:330
  170.6 5.1 %collective-permute-done.15.refs_3_ = bf16[2,4,128,256]{3,2,1,0:T(8,128)(2,1)S(1)} collective-permute-done((bf16[2,4,128,256]{3,2,1,0:T(8,128)(2,1)}, bf16[2,4,128,256]{3,2,1,0:T(8,128)(2,1)S(1)}, u32[]{:S(2)}, u32[]{:S(2)}) %collective-permute-start.15) | collective-permute-done | bytes 524320 | tf_op jit(solution)/shard_map/ppermute | solution.py:330
  178.8 13.2 %all-to-all-start.1 = ((bf16[128,8,1024]{2,1,0:T(8,128)(2,1)}), bf16[128,8,1024]{2,1,0:T(8,128)(2,1)S(1)}, u32[]{:S(2)}, u32[]{:S(2)}) async-start(bf16[128,8,1024]{2,1,0:T(8,128)(2,1)} %bitcast.29), calls=%async_computation.1 | async-start | bytes 4194304 | tf_op jit(solution)/shard_map/all_to_all | solution.py:395
  192.0 2.5 %join_sum.2 = (bf16[2,2,2,8,1024]{4,3,2,1,0:T(8,128)(2,1)}, bf16[2,2,2,8,1024]{4,3,2,1,0:T(8,128)(2,1)}, bf16[2,2,2,8,1024]{4,3,2,1,0:T(8,128)(2,1)}, bf16[2,2,2,8,1024]{4,3,2,1,0:T(8,128)(2,1)}) custom-call(s32[1]{0:T(128)} %bitcast.8.here_ref, bf16[2,4,128,256]{3,2,1,0:T(8,128)(2,1)} %get-tuple-element.51.refs_0_, bf16[2,4,128,256]{3,2,1,0:T(8,128)(2,1)} %copy-done.3, ...), custom_call_target="tpu_custom_call" | custom-call | flops 1000000 | bytes 6000000 | tf_op jit(solution)/shard_map/join_sum/pallas_call | solution.py:284
  195.6 3.2 %collective-permute-start.17 = (bf16[2,2,2,8,1024]{4,3,2,1,0:T(8,128)(2,1)}, bf16[2,2,2,8,1024]{4,3,2,1,0:T(8,128)(2,1)S(1)}, u32[]{:S(2)}, u32[]{:S(2)}) collective-permute-start(bf16[2,2,2,8,1024]{4,3,2,1,0:T(8,128)(2,1)} %get-tuple-element.73), channel_id=1, source_target_pairs={{0,8},{4,12},{8,0},{12,4},{1,9},{5,13},{9,1},{13,5},{2,10},{6,14},... | collective-permute-start | bytes 393224 | tf_op jit(solution)/shard_map/ppermute | solution.py:330
  200.0 3.1 %fusion = bf16[256,1024]{1,0:T(8,128)(2,1)} fusion(bf16[256,1024]{1,0:T(8,128)(2,1)S(1)} %copy-done.17, bf16[1024,1024]{1,0:T(8,128)(2,1)} %wo_ref.1, bf16[1,1,256,1024]{3,2,1,0:T(8,128)(2,1)S(1)} %copy-done.8), kind=kOutput, calls=%fused_computation.1 | convolution fusion | flops 537657344 | bytes 3670016 | tf_op jit(solution)/shard_map/dot_general | solution.py:402
  207.1 2.8 %collective-permute-start.20 = (bf16[2,2,2,8,1024]{4,3,2,1,0:T(8,128)(2,1)}, bf16[2,2,2,8,1024]{4,3,2,1,0:T(8,128)(2,1)S(1)}, u32[]{:S(2)}, u32[]{:S(2)}) collective-permute-start(bf16[2,2,2,8,1024]{4,3,2,1,0:T(8,128)(2,1)} %get-tuple-element.78), channel_id=1, source_target_pairs={{0,32},{16,48},{32,0},{48,16},{1,33},{17,49},{33,1},{49,17},{2,34}... | collective-permute-start | bytes 393224 | tf_op jit(solution)/shard_map/ppermute | solution.py:330
  209.9 11.1 %collective-permute-done.16 = bf16[2,2,2,8,1024]{4,3,2,1,0:T(8,128)(2,1)S(1)} collective-permute-done((bf16[2,2,2,8,1024]{4,3,2,1,0:T(8,128)(2,1)}, bf16[2,2,2,8,1024]{4,3,2,1,0:T(8,128)(2,1)S(1)}, u32[]{:S(2)}, u32[]{:S(2)}) %collective-permute-start.16) | collective-permute-done | bytes 131104 | tf_op jit(solution)/shard_map/ppermute | solution.py:330
  221.0 5.2 %collective-permute-start.21 = (bf16[2,2,2,8,1024]{4,3,2,1,0:T(8,128)(2,1)}, bf16[2,2,2,8,1024]{4,3,2,1,0:T(8,128)(2,1)S(1)}, u32[]{:S(2)}, u32[]{:S(2)}) collective-permute-start(bf16[2,2,2,8,1024]{4,3,2,1,0:T(8,128)(2,1)} %get-tuple-element.79), channel_id=1, source_target_pairs={{0,48},{16,0},{32,16},{48,32},{1,49},{17,1},{33,17},{49,33},{2,50}... | collective-permute-start | bytes 393224 | tf_op jit(solution)/shard_map/ppermute | solution.py:330
  226.4 2.7 %collective-permute-done.21 = bf16[2,2,2,8,1024]{4,3,2,1,0:T(8,128)(2,1)S(1)} collective-permute-done((bf16[2,2,2,8,1024]{4,3,2,1,0:T(8,128)(2,1)}, bf16[2,2,2,8,1024]{4,3,2,1,0:T(8,128)(2,1)S(1)}, u32[]{:S(2)}, u32[]{:S(2)}) %collective-permute-start.21) | collective-permute-done | bytes 131104 | tf_op jit(solution)/shard_map/ppermute | solution.py:330
  (86 shorter events, 40.1 us)
Async XLA Ops:
  5.1 41.6 %all-to-all-start = ((bf16[128,8,1024]{2,1,0:T(8,128)(2,1)}), bf16[128,8,1024]{2,1,0:T(8,128)(2,1)S(1)}, u32[]{:S(2)}, u32[]{:S(2)}) async-start(bf16[128,8,1024]{2,1,0:T(8,128)(2,1)} %bitcast.28), calls=%async_computation | async-start | bytes 4194304 | tf_op jit(solution)/shard_map/all_to_all | solution.py:367
  53.0 12.6 %collective-permute-start = (bf16[256,1024]{1,0:T(8,128)(2,1)}, bf16[256,1024]{1,0:T(8,128)(2,1)S(1)}, u32[]{:S(2)}, u32[]{:S(2)}) collective-permute-start(bf16[256,1024]{1,0:T(8,128)(2,1)} %get-tuple-element.43.own_ref), channel_id=1, source_target_pairs={{0,16},{16,32},{32,48},{48,64},{64,80},{80,96},{96,112},{1,17},{17... | collective-permute-start | bytes 1572872 | tf_op jit(solution)/shard_map/ppermute | solution.py:340
  54.4 15.3 %collective-permute-start.1 = (bf16[256,1024]{1,0:T(8,128)(2,1)}, bf16[256,1024]{1,0:T(8,128)(2,1)S(1)}, u32[]{:S(2)}, u32[]{:S(2)}) collective-permute-start(bf16[256,1024]{1,0:T(8,128)(2,1)} %get-tuple-element.43.own_ref), channel_id=1, source_target_pairs={{16,0},{32,16},{48,32},{64,48},{80,64},{96,80},{112,96},{17,1},{33... | collective-permute-start | bytes 1572872 | tf_op jit(solution)/shard_map/ppermute | solution.py:340
  55.7 14.1 %collective-permute-start.2 = (bf16[256,1024]{1,0:T(8,128)(2,1)}, bf16[256,1024]{1,0:T(8,128)(2,1)S(1)}, u32[]{:S(2)}, u32[]{:S(2)}) collective-permute-start(bf16[256,1024]{1,0:T(8,128)(2,1)} %get-tuple-element.43.own_ref), channel_id=1, source_target_pairs={{0,1},{1,2},{2,3},{3,4},{4,5},{5,6},{6,7},{7,8},{8,9},{9,10},{10,1... | collective-permute-start | bytes 1572872 | tf_op jit(solution)/shard_map/ppermute | solution.py:340
  57.0 12.7 %collective-permute-start.3 = (bf16[256,1024]{1,0:T(8,128)(2,1)}, bf16[256,1024]{1,0:T(8,128)(2,1)S(1)}, u32[]{:S(2)}, u32[]{:S(2)}) collective-permute-start(bf16[256,1024]{1,0:T(8,128)(2,1)} %get-tuple-element.43.own_ref), channel_id=1, source_target_pairs={{1,0},{2,1},{3,2},{4,3},{5,4},{6,5},{7,6},{8,7},{9,8},{10,9},{11,1... | collective-permute-start | bytes 1572872 | tf_op jit(solution)/shard_map/ppermute | solution.py:340
  111.9 9.9 %collective-permute-start.5 = (bf16[4,2,4,128,256]{4,3,2,1,0:T(8,128)(2,1)}, bf16[4,2,4,128,256]{4,3,2,1,0:T(8,128)(2,1)}, u32[]{:S(2)}, u32[]{:S(2)}) collective-permute-start(bf16[4,2,4,128,256]{4,3,2,1,0:T(8,128)(2,1)} %get-tuple-element.50), channel_id=1, source_target_pairs={{0,1},{1,0},{2,3},{3,2},{4,5},{5,4},{6,7},{7,6},{8,9},{9,8},{10,11... | collective-permute-start | bytes 6291464 | tf_op jit(solution)/shard_map/ppermute | solution.py:330
  113.1 16.9 %collective-permute-start.4 = (bf16[4,2,4,128,256]{4,3,2,1,0:T(8,128)(2,1)}, bf16[4,2,4,128,256]{4,3,2,1,0:T(8,128)(2,1)S(1)}, u32[]{:S(2)}, u32[]{:S(2)}) collective-permute-start(bf16[4,2,4,128,256]{4,3,2,1,0:T(8,128)(2,1)} %get-tuple-element.47), channel_id=1, source_target_pairs={{0,1},{1,0},{2,3},{3,2},{4,5},{5,4},{6,7},{7,6},{8,9},{9,8},{10,11... | collective-permute-start | bytes 6291464 | tf_op jit(solution)/shard_map/ppermute | solution.py:330
  113.2 22.4 %collective-permute-start.6 = (bf16[256,1024]{1,0:T(8,128)(2,1)}, bf16[256,1024]{1,0:T(8,128)(2,1)S(1)}, u32[]{:S(2)}, u32[]{:S(2)}) collective-permute-start(bf16[256,1024]{1,0:T(8,128)(2,1)} %get-tuple-element.53), channel_id=1, source_target_pairs={{16,0},{32,16},{48,32},{64,48},{80,64},{96,80},{112,96},{17,1},{33... | collective-permute-start | bytes 1572872 | tf_op jit(solution)/shard_map/ppermute | solution.py:340
  114.5 36.7 %collective-permute-start.7 = (bf16[256,1024]{1,0:T(8,128)(2,1)}, bf16[256,1024]{1,0:T(8,128)(2,1)}, u32[]{:S(2)}, u32[]{:S(2)}) collective-permute-start(bf16[256,1024]{1,0:T(8,128)(2,1)} %get-tuple-element.54), channel_id=1, source_target_pairs={{0,16},{16,32},{32,48},{48,64},{64,80},{80,96},{96,112},{1,17},{17... | collective-permute-start | bytes 1572872 | tf_op jit(solution)/shard_map/ppermute | solution.py:340
  120.5 30.7 %collective-permute-start.8 = (bf16[256,1024]{1,0:T(8,128)(2,1)}, bf16[256,1024]{1,0:T(8,128)(2,1)}, u32[]{:S(2)}, u32[]{:S(2)}) collective-permute-start(bf16[256,1024]{1,0:T(8,128)(2,1)} %get-tuple-element.55), channel_id=1, source_target_pairs={{1,0},{2,1},{3,2},{4,3},{5,4},{6,5},{7,6},{8,7},{9,8},{10,9},{11,1... | collective-permute-start | bytes 1572872 | tf_op jit(solution)/shard_map/ppermute | solution.py:340
  121.8 29.7 %collective-permute-start.9 = (bf16[256,1024]{1,0:T(8,128)(2,1)}, bf16[256,1024]{1,0:T(8,128)(2,1)}, u32[]{:S(2)}, u32[]{:S(2)}) collective-permute-start(bf16[256,1024]{1,0:T(8,128)(2,1)} %get-tuple-element.56), channel_id=1, source_target_pairs={{0,1},{1,2},{2,3},{3,4},{4,5},{5,6},{6,7},{7,8},{8,9},{9,10},{10,1... | collective-permute-start | bytes 1572872 | tf_op jit(solution)/shard_map/ppermute | solution.py:340
  130.0 28.1 %collective-permute-start.13 = (bf16[2,4,128,256]{3,2,1,0:T(8,128)(2,1)}, bf16[2,4,128,256]{3,2,1,0:T(8,128)(2,1)S(1)}, u32[]{:S(2)}, u32[]{:S(2)}) collective-permute-start(bf16[2,4,128,256]{3,2,1,0:T(8,128)(2,1)} %get-tuple-element.66), channel_id=1, source_target_pairs={{0,16},{16,32},{32,48},{48,0},{1,17},{17,33},{33,49},{49,1},{2,18}... | collective-permute-start | bytes 1572872 | tf_op jit(solution)/shard_map/ppermute | solution.py:330
  135.7 34.9 %collective-permute-start.14 = (bf16[2,4,128,256]{3,2,1,0:T(8,128)(2,1)}, bf16[2,4,128,256]{3,2,1,0:T(8,128)(2,1)S(1)}, u32[]{:S(2)}, u32[]{:S(2)}) collective-permute-start(bf16[2,4,128,256]{3,2,1,0:T(8,128)(2,1)} %get-tuple-element.67), channel_id=1, source_target_pairs={{0,32},{16,48},{32,0},{48,16},{1,33},{17,49},{33,1},{49,17},{2,34}... | collective-permute-start | bytes 1572872 | tf_op jit(solution)/shard_map/ppermute | solution.py:330
  151.2 24.5 %collective-permute-start.15 = (bf16[2,4,128,256]{3,2,1,0:T(8,128)(2,1)}, bf16[2,4,128,256]{3,2,1,0:T(8,128)(2,1)S(1)}, u32[]{:S(2)}, u32[]{:S(2)}) collective-permute-start(bf16[2,4,128,256]{3,2,1,0:T(8,128)(2,1)} %get-tuple-element.68), channel_id=1, source_target_pairs={{0,48},{16,0},{32,16},{48,32},{1,49},{17,1},{33,17},{49,33},{2,50}... | collective-permute-start | bytes 1572872 | tf_op jit(solution)/shard_map/ppermute | solution.py:330
  151.2 26.8 %collective-permute-start.10 = (bf16[2,4,128,256]{3,2,1,0:T(8,128)(2,1)}, bf16[2,4,128,256]{3,2,1,0:T(8,128)(2,1)S(1)}, u32[]{:S(2)}, u32[]{:S(2)}) collective-permute-start(bf16[2,4,128,256]{3,2,1,0:T(8,128)(2,1)} %get-tuple-element.63), channel_id=1, source_target_pairs={{0,4},{4,8},{8,12},{12,0},{1,5},{5,9},{9,13},{13,1},{2,6},{6,10},{... | collective-permute-start | bytes 1572872 | tf_op jit(solution)/shard_map/ppermute | solution.py:330
  151.5 26.5 %collective-permute-start.11 = (bf16[2,4,128,256]{3,2,1,0:T(8,128)(2,1)}, bf16[2,4,128,256]{3,2,1,0:T(8,128)(2,1)}, u32[]{:S(2)}, u32[]{:S(2)}) collective-permute-start(bf16[2,4,128,256]{3,2,1,0:T(8,128)(2,1)} %get-tuple-element.64), channel_id=1, source_target_pairs={{0,8},{4,12},{8,0},{12,4},{1,9},{5,13},{9,1},{13,5},{2,10},{6,14},... | collective-permute-start | bytes 1572872 | tf_op jit(solution)/shard_map/ppermute | solution.py:330
  158.1 20.6 %collective-permute-start.12 = (bf16[2,4,128,256]{3,2,1,0:T(8,128)(2,1)}, bf16[2,4,128,256]{3,2,1,0:T(8,128)(2,1)}, u32[]{:S(2)}, u32[]{:S(2)}) collective-permute-start(bf16[2,4,128,256]{3,2,1,0:T(8,128)(2,1)} %get-tuple-element.65), channel_id=1, source_target_pairs={{0,12},{4,0},{8,4},{12,8},{1,13},{5,1},{9,5},{13,9},{2,14},{6,2},{... | collective-permute-start | bytes 1572872 | tf_op jit(solution)/shard_map/ppermute | solution.py:330
  178.8 57.0 %all-to-all-start.1 = ((bf16[128,8,1024]{2,1,0:T(8,128)(2,1)}), bf16[128,8,1024]{2,1,0:T(8,128)(2,1)S(1)}, u32[]{:S(2)}, u32[]{:S(2)}) async-start(bf16[128,8,1024]{2,1,0:T(8,128)(2,1)} %bitcast.29), calls=%async_computation.1 | async-start | bytes 4194304 | tf_op jit(solution)/shard_map/all_to_all | solution.py:395
  194.5 26.5 %collective-permute-start.16 = (bf16[2,2,2,8,1024]{4,3,2,1,0:T(8,128)(2,1)}, bf16[2,2,2,8,1024]{4,3,2,1,0:T(8,128)(2,1)S(1)}, u32[]{:S(2)}, u32[]{:S(2)}) collective-permute-start(bf16[2,2,2,8,1024]{4,3,2,1,0:T(8,128)(2,1)} %get-tuple-element.72), channel_id=1, source_target_pairs={{0,4},{4,8},{8,12},{12,0},{1,5},{5,9},{9,13},{13,1},{2,6},{6,10},{... | collective-permute-start | bytes 393224 | tf_op jit(solution)/shard_map/ppermute | solution.py:330
  195.6 30.6 %collective-permute-start.17 = (bf16[2,2,2,8,1024]{4,3,2,1,0:T(8,128)(2,1)}, bf16[2,2,2,8,1024]{4,3,2,1,0:T(8,128)(2,1)S(1)}, u32[]{:S(2)}, u32[]{:S(2)}) collective-permute-start(bf16[2,2,2,8,1024]{4,3,2,1,0:T(8,128)(2,1)} %get-tuple-element.73), channel_id=1, source_target_pairs={{0,8},{4,12},{8,0},{12,4},{1,9},{5,13},{9,1},{13,5},{2,10},{6,14},... | collective-permute-start | bytes 393224 | tf_op jit(solution)/shard_map/ppermute | solution.py:330
  198.8 27.4 %collective-permute-start.18 = (bf16[2,2,2,8,1024]{4,3,2,1,0:T(8,128)(2,1)}, bf16[2,2,2,8,1024]{4,3,2,1,0:T(8,128)(2,1)S(1)}, u32[]{:S(2)}, u32[]{:S(2)}) collective-permute-start(bf16[2,2,2,8,1024]{4,3,2,1,0:T(8,128)(2,1)} %get-tuple-element.74), channel_id=1, source_target_pairs={{0,12},{4,0},{8,4},{12,8},{1,13},{5,1},{9,5},{13,9},{2,14},{6,2},{... | collective-permute-start | bytes 393224 | tf_op jit(solution)/shard_map/ppermute | solution.py:330
  205.5 20.8 %collective-permute-start.19 = (bf16[2,2,2,8,1024]{4,3,2,1,0:T(8,128)(2,1)}, bf16[2,2,2,8,1024]{4,3,2,1,0:T(8,128)(2,1)S(1)}, u32[]{:S(2)}, u32[]{:S(2)}) collective-permute-start(bf16[2,2,2,8,1024]{4,3,2,1,0:T(8,128)(2,1)} %get-tuple-element.77), channel_id=1, source_target_pairs={{0,16},{16,32},{32,48},{48,0},{1,17},{17,33},{33,49},{49,1},{2,18}... | collective-permute-start | bytes 393224 | tf_op jit(solution)/shard_map/ppermute | solution.py:330
  207.1 19.2 %collective-permute-start.20 = (bf16[2,2,2,8,1024]{4,3,2,1,0:T(8,128)(2,1)}, bf16[2,2,2,8,1024]{4,3,2,1,0:T(8,128)(2,1)S(1)}, u32[]{:S(2)}, u32[]{:S(2)}) collective-permute-start(bf16[2,2,2,8,1024]{4,3,2,1,0:T(8,128)(2,1)} %get-tuple-element.78), channel_id=1, source_target_pairs={{0,32},{16,48},{32,0},{48,16},{1,33},{17,49},{33,1},{49,17},{2,34}... | collective-permute-start | bytes 393224 | tf_op jit(solution)/shard_map/ppermute | solution.py:330
  221.0 8.0 %collective-permute-start.21 = (bf16[2,2,2,8,1024]{4,3,2,1,0:T(8,128)(2,1)}, bf16[2,2,2,8,1024]{4,3,2,1,0:T(8,128)(2,1)S(1)}, u32[]{:S(2)}, u32[]{:S(2)}) collective-permute-start(bf16[2,2,2,8,1024]{4,3,2,1,0:T(8,128)(2,1)} %get-tuple-element.79), channel_id=1, source_target_pairs={{0,48},{16,0},{32,16},{48,32},{1,49},{17,1},{33,17},{49,33},{2,50}... | collective-permute-start | bytes 393224 | tf_op jit(solution)/shard_map/ppermute | solution.py:330
  (21 other events, 173.4 us)
where the time goes:
time: 240 us
  starting transfers between devices  84.7 us (35%)
  Pallas kernels  72.7 us (30%)
  waiting for transfers between devices  70.3 us (29%)
  local copies, waits for them, and re-layouts  5.33 us (2%)
  matrix products  3.13 us (1%)
  other arithmetic  2.43 us (1%)
    ppermute x17, starting transfers between devices, shifted(): lax.ppermute(block, axis, [(i, (i + step) % count) for i in range(count)])  42.6 us
    pallas_call x1, Pallas kernels, attend(): pl.pallas_call(attend_kernel, grid=(steps,), in_specs=[flags(), flags()]...  41 us
    ppermute x17, waiting for transfers between devices, shifted(): lax.ppermute(block, axis, [(i, (i + step) % count) for i in range(count)])  32 us
    all_to_all x1, waiting for transfers between devices, body(): lax.all_to_all(outgoing, TY + TX, split_axis=0, concat_axis=0, tiled=True)  27.1 us
    ppermute x8, starting transfers between devices, passed_along(): return lax.ppermute(block, axis, route)  17.9 us
    all_to_all x1, starting transfers between devices, body(): lax.all_to_all(after(slots, (along_z, along_y)), TY + TX, split_axis=0, c...  13.2 us
    ppermute x8, waiting for transfers between devices, passed_along(): return lax.ppermute(block, axis, route)  11.2 us
    all_to_all x1, starting transfers between devices, body(): lax.all_to_all(outgoing, TY + TX, split_axis=0, concat_axis=0, tiled=True)  11.1 us
  transfers between devices with their start and end apart: 27, of which 11 were waited for; matrix products, arithmetic and copies ran while one was open for 3% of the time, Pallas kernels for 9%

commit v1 on v0

--- a/solution.py
+++ b/solution.py
@@ -70,16 +70,18 @@
     )(rows, sent)
 
 
-def blend_kernel(slots_ref, blend_ref, incoming_ref, state_ref, gain_ref, in_ref, normed_ref, inverse_ref, high_ref, low_ref):
-    rows, slots = blend_ref.shape[0], incoming_ref.shape[0]
-    lanes = lax.broadcasted_iota(jnp.int32, (rows, slots), 1)
-    spread = jnp.zeros((rows, slots), F32)
+def spread_weights(slots_ref, blend_ref, count):
+    rows = blend_ref.shape[0]
+    lanes = lax.broadcasted_iota(jnp.int32, (rows, count), 1)
+    spread = jnp.zeros((rows, count), F32)
     for k in range(blend_ref.shape[1]):
         spread = spread + jnp.where(lanes == slots_ref[:, k : k + 1], blend_ref[:, k : k + 1], 0.0)
     high = spread.astype(BF16)
-    low = (spread - high.astype(F32)).astype(BF16)
-    high_ref[...] = high
-    low_ref[...] = low
+    return high, (spread - high.astype(F32)).astype(BF16)
+
+
+def blend_kernel(slots_ref, blend_ref, incoming_ref, state_ref, gain_ref, in_ref, normed_ref, inverse_ref):
+    high, low = spread_weights(slots_ref, blend_ref, incoming_ref.shape[0])
     incoming = incoming_ref[...]
     pre = state_ref[...].astype(F32) + (mm(high, incoming) + mm(low, incoming))
     inverse = lax.rsqrt(jnp.mean(pre * pre, axis=-1, keepdims=True) + EPSILON)
@@ -91,23 +93,46 @@
 
 def blend_norm(slots, blend, incoming, state, gain):
     rows, width = state.shape
-    spread = jax.ShapeDtypeStruct((rows, incoming.shape[0]), BF16)
     return pl.pallas_call(
         blend_kernel,
         out_shape=(
             jax.ShapeDtypeStruct((rows, width), BF16),
             jax.ShapeDtypeStruct((rows, width), F32),
             jax.ShapeDtypeStruct((rows, 128), F32),
-            spread,
-            spread,
         ),
-        compiler_params=params(60),
+        compiler_params=params(30),
         name="blend_norm",
     )(slots, blend, incoming, state, gain)
 
 
+def project_kernel(in_ref, grad_ref, wq_ref, wk_ref, wv_ref, wo_ref, query_ref, key_ref, value_ref, g_ref):
+    normed_in = in_ref[...]
+    query_ref[...] = mm(normed_in, wq_ref[...]).astype(BF16)
+    key_ref[...] = mm(normed_in, wk_ref[...]).astype(BF16)
+    value_ref[...] = mm(normed_in, wv_ref[...]).astype(BF16)
+    g_ref[...] = mm(grad_ref[...], wo_ref[...], NT).astype(BF16)
+
+
+def project(normed_in, grad_out, w_query, w_key, w_value, w_out):
+    rows, width = normed_in.shape
+    lanes = 2 * HEAD_SIZE
+    whole = lambda: pl.BlockSpec((rows, width), lambda h: (0, 0), pipeline_mode=pl.Buffered(1))
+    columns = lambda n: pl.BlockSpec((n, lanes), lambda h: (0, h))
+    return pl.pallas_call(
+        project_kernel,
+        grid=(width // lanes,),
+        in_specs=[whole(), whole()] + [columns(width)] * 3 + [pl.BlockSpec((lanes, width), lambda h: (h, 0))],
+        out_specs=[columns(rows)] * 4,
+        out_shape=(jax.ShapeDtypeStruct((rows, width), BF16),) * 4,
+        compiler_params=params(60),
+        cost_estimate=pl.CostEstimate(flops=21 * 10**8, bytes_accessed=11 * 10**6, transcendentals=0),
+        name="project",
+    )(normed_in, grad_out, w_query, w_key, w_value, w_out)
+
+
 def attend_kernel(
-    core_ref, mask_ref, own_ref, up_ref, down_ref, left_ref, right_ref, grad_ref, wq_ref, wk_ref, wv_ref, wo_ref,
+    core_ref, mask_ref, own_ref, up_ref, down_ref, left_ref, right_ref, grad_ref,
+    query_ref, own_key_ref, own_value_ref, g_ref, wq_ref, wk_ref, wv_ref,
     keep_y, send_y, keep_z, send_z, attended_ref, up_grad, down_grad, left_grad, right_grad, own_grad, x_all, x_turned, grads,
 ):
     step = pl.program_id(0)
@@ -126,10 +151,10 @@
     grad_out = grad_ref[...]
     width = grad_out.shape[1]
     scale = HEAD_SIZE ** (-0.5)
-    query = mm(own_ref[...], wq_ref[...]).astype(BF16)
-    g = mm(grad_out, wo_ref[...], NT).astype(BF16)
-    key = mm(x_all[...], wk_ref[...]).astype(BF16)
-    value = mm(x_all[...], wv_ref[...]).astype(BF16)
+    query, g = query_ref[...], g_ref[...]
+    near = x_all[rows:]
+    key = jnp.concatenate([own_key_ref[...], mm(near, wk_ref[...]).astype(BF16)], axis=0)
+    value = jnp.concatenate([own_value_ref[...], mm(near, wv_ref[...]).astype(BF16)], axis=0)
     query_t, g_t = query.T, g.T
     attended_t, dquery_t, dkey, dvalue = [], [], [], []
     for h in range(lanes // HEAD_SIZE):
@@ -190,7 +215,7 @@
             ref[...] = grads[b * rows : (b + 1) * rows].astype(BF16)
 
 
-def attend(core, mask, tiles, grad_out, w_query, w_key, w_value, w_out, ys, zs):
+def attend(core, mask, tiles, grad_out, projected, w_query, w_key, w_value, ys, zs):
     rows, width = grad_out.shape
     near, lanes = len(tiles), 2 * HEAD_SIZE
     steps = width // lanes
@@ -206,7 +231,8 @@
         grid=(steps,),
         in_specs=[flags(), flags()]
         + [whole() for _ in range(near + 1)]
-        + [columns(), columns(), columns(), pl.BlockSpec((lanes, width), lambda h: (h, 0))],
+        + [out(rows)] * 4
+        + [columns()] * 3,
         out_specs=[parts(ys), parts(ys), parts(zs), parts(zs), out(rows)]
         + [whole() for _ in range(near)],
         out_shape=(part(ys), part(ys), part(zs), part(zs)) + (small,) * near + (jax.ShapeDtypeStruct((rows, width), F32),),
@@ -218,29 +244,35 @@
         compiler_params=params(60),
         cost_estimate=pl.CostEstimate(flops=34 * 10**9, bytes_accessed=32 * 10**6, transcendentals=10**6),
         name="attend",
-    )(core, mask, *tiles, grad_out, w_query, w_key, w_value, w_out)
-
-
-def split_kernel(here_ref, keep_ref, came_ref, *out_refs):
-    count = len(out_refs)
-    for step, ref in enumerate(out_refs):
-        at = (here_ref[0] + step) % count
-        ref[...] = (keep_ref[at].astype(F32) + came_ref[at].astype(F32)).astype(BF16)
-
-
-def split_sum(here, keep, came):
-    count, mats, steps, *rest = keep.shape
-    whole = lambda: pl.BlockSpec((count, mats, 1, *rest), lambda s: (0, 0, s, 0, 0))
-    return pl.pallas_call(
-        split_kernel,
+    )(core, mask, *tiles, grad_out, *projected, w_query, w_key, w_value)
+
+
+def split_kernel(counts, *refs):
+    heres, refs = refs[: len(counts)], refs[len(counts) :]
+    in_refs, out_refs = refs[: 2 * len(counts)], list(refs[2 * len(counts) :])
+    for group, count in enumerate(counts):
+        keep_ref, came_ref = in_refs[2 * group : 2 * group + 2]
+        for step in range(count):
+            at = (heres[group][0] + step) % count
+            out_refs.pop(0)[...] = (keep_ref[at].astype(F32) + came_ref[at].astype(F32)).astype(BF16)
+
+
+def split_sum(heres, groups):
+    counts = tuple(keep.shape[0] for keep, _ in groups)
+    steps = groups[0][0].shape[2]
+    block = lambda a: pl.BlockSpec((*a.shape[:2], 1, *a.shape[3:]), lambda s: (0, 0, s, 0, 0))
+    chunks = [keep.shape[1:] for keep, _ in groups for _ in range(keep.shape[0])]
+    out = pl.pallas_call(
+        functools.partial(split_kernel, counts),
         grid=(steps,),
-        in_specs=[pl.BlockSpec(memory_space=pltpu.SMEM), whole(), whole()],
-        out_specs=[pl.BlockSpec((mats, 1, *rest), lambda s: (0, s, 0, 0)) for _ in range(count)],
-        out_shape=tuple(jax.ShapeDtypeStruct((mats, steps, *rest), BF16) for _ in range(count)),
-        compiler_params=params(60),
-        cost_estimate=pl.CostEstimate(flops=10**6, bytes_accessed=6 * 10**6, transcendentals=0),
+        in_specs=[pl.BlockSpec(memory_space=pltpu.SMEM) for _ in heres] + [block(a) for pair in groups for a in pair],
+        out_specs=[pl.BlockSpec((c[0], 1, *c[2:]), lambda s: (0, s, 0, 0)) for c in chunks],
+        out_shape=tuple(jax.ShapeDtypeStruct(c, BF16) for c in chunks),
+        compiler_params=params(60),
+        cost_estimate=pl.CostEstimate(flops=10**6, bytes_accessed=12 * 10**6, transcendentals=0),
         name="split_sum",
-    )(here, keep, came)
+    )(*heres, *(a for pair in groups for a in pair))
+    return out[: counts[0]], out[counts[0] :]
 
 
 def join_kernel(pieces, out_matrix, here_ref, *refs):
@@ -295,7 +327,7 @@
     )(here, *parts)
 
 
-def finish_kernel(own_ref, up_ref, down_ref, left_ref, right_ref, normed_ref, inverse_ref, gain_ref, grad_ref, high_ref, low_ref, state_grad_ref, slot_ref):
+def finish_kernel(own_ref, up_ref, down_ref, left_ref, right_ref, normed_ref, inverse_ref, gain_ref, grad_ref, slots_ref, blend_ref, state_grad_ref, slot_ref):
     total = own_ref[...]
     for ref in (up_ref, down_ref, left_ref, right_ref):
         total = total + ref[...].astype(F32)
@@ -305,20 +337,21 @@
     state_grad_ref[...] = (grad_ref[...].astype(F32) + grad).astype(BF16)
     top = grad.astype(BF16)
     rest = (grad - top.astype(F32)).astype(BF16)
-    slot_ref[...] = (mm(high_ref[...], top, TN) + (mm(high_ref[...], rest, TN) + mm(low_ref[...], top, TN))).astype(BF16)
-
-
-def finish(own, near, normed, inverse, gain, grad_out, high, low):
+    high, low = spread_weights(slots_ref, blend_ref, slot_ref.shape[0])
+    slot_ref[...] = (mm(high, top, TN) + (mm(high, rest, TN) + mm(low, top, TN))).astype(BF16)
+
+
+def finish(own, near, normed, inverse, gain, grad_out, slots, blend, count):
     rows, width = own.shape
     return pl.pallas_call(
         finish_kernel,
         out_shape=(
             jax.ShapeDtypeStruct((rows, width), BF16),
-            jax.ShapeDtypeStruct((high.shape[1], width), BF16),
+            jax.ShapeDtypeStruct((count, width), BF16),
         ),
         compiler_params=params(60),
         name="finish",
-    )(own, *near, normed, inverse, gain, grad_out, high, low)
+    )(own, *near, normed, inverse, gain, grad_out, slots, blend)
 
 
 def after(value, others):
@@ -365,9 +398,8 @@
     devices = lax.axis_size(TY + TX)
     outgoing = pick_rows(send_rows, global_latent)
     incoming = lax.all_to_all(outgoing, TY + TX, split_axis=0, concat_axis=0, tiled=True)
-    normed_in, normed, inverse, high, low = blend_norm(
-        recv_slots.reshape(rows, -1), regrid_weight[0, 0], incoming, state, gain
-    )
+    slot_ids, blend = recv_slots.reshape(rows, -1), regrid_weight[0, 0]
+    normed_in, normed, inverse = blend_norm(slot_ids, blend, incoming, state, gain)
     tiles = (
         normed_in,
         passed_along(normed_in, TY, 1),
@@ -375,11 +407,12 @@
         passed_along(normed_in, TX, 1),
         passed_along(normed_in, TX, -1),
     )
+    projected = project(normed_in, grad_out, w_query, w_key, w_value, w_out)
     here = {axis: lax.axis_index(axis).reshape(1) for axis in ("z", "y", "core", "x_hi", "x_lo")}
     chunk = width // devices
     ys, zs = lax.axis_size("y"), lax.axis_size("z")
     keep_y, send_y, keep_z, send_z, attended, *near, own = attend(
-        here["core"], window_mask[0], tiles, grad_out, w_query, w_key, w_value, w_out, ys, zs
+        here["core"], window_mask[0], tiles, grad_out, projected, w_query, w_key, w_value, ys, zs
     )
     came_y, came_z = shifted(send_y, "core", 1), shifted(send_z, "core", 1)
     returned = (
@@ -388,20 +421,19 @@
         passed_along(near[2], TX, -1),
         passed_along(near[3], TX, 1),
     )
-    along_z = swapped(split_sum(here["z"], keep_z, came_z), "z")
-    along_y = swapped(split_sum(here["y"], keep_y, came_y), "y")
+    chunks_y, chunks_z = split_sum((here["y"], here["z"]), ((keep_y, came_y), (keep_z, came_z)))
+    along_y, along_z = swapped(chunks_y, "y"), swapped(chunks_z, "z")
     own = after(own, (along_z[0], along_y[0]))
-    state_grad, slots = finish(own, returned, normed, inverse, gain, grad_out, high, low)
-    sent_back = lax.all_to_all(after(slots, (along_z, along_y)), TY + TX, split_axis=0, concat_axis=0, tiled=True)
+    state_grad, slots = finish(own, returned, normed, inverse, gain, grad_out, slot_ids, blend, incoming.shape[0])
+    term = jnp.dot(after(attended, slots), w_out, preferred_element_type=F32)
+    updated = (state.astype(F32) + term).astype(BF16)
+    sent_back = lax.all_to_all(after(slots, (along_z, along_y, updated)), TY + TX, split_axis=0, concat_axis=0, tiled=True)
     global_grad = add_rows(send_rows, sent_back, global_latent.shape[0])
     here_y, here_z = after((here["y"], here["z"]), slots)
     second_z = swapped(join_sum(here_z, along_y, zs, -1, chunk), "z")
     second_y = swapped(join_sum(here_y, along_z, ys, 1, chunk), "y")
     total = jnp.concatenate([sum(piece.astype(F32) for piece in group) for group in (second_z, second_y)], axis=2)
     total = total.astype(BF16).reshape(-1, 4, chunk, width)
-    term = jnp.dot(attended, w_out, preferred_element_type=F32)
-    updated = (state.astype(F32) + term).astype(BF16)
-    total = after(total, updated)
     place = lax.axis_index(X)
     along_x = swapped([lax.dynamic_index_in_dim(total, (place + k) % total.shape[0], 0, keepdims=False) for k in range(total.shape[0])], X)
     weight_grads = sum(piece.astype(F32) for piece in after(along_x[:1], global_grad) + along_x[1:])

time: 240 us -> 232 us (0.967)
  waiting for transfers between devices: 70.3 us -> 55.6 us
  starting transfers between devices: 84.7 us -> 93.9 us
    ppermute x17, starting transfers between devices: 42.6 us -> 53.9 us  [shifted(): lax.ppermute(block, axis, [(i, (i + step) % count) for i in range(count)])]
    ppermute x17, waiting for transfers between devices: 32 us -> 22.7 us  [shifted(): lax.ppermute(block, axis, [(i, (i + step) % count) for i in range(count)])]
    ppermute x8, waiting for transfers between devices: 11.2 us -> 3.98 us  [passed_along(): return lax.ppermute(block, axis, route)]
    pallas_call x2, Pallas kernels: 8.63 us -> 12.9 us  [the longest x1 6.97 us: project(): pl.pallas_call(project_kernel, grid=(width // lanes,), in_specs=[whole(),...]
    pallas_call x1, Pallas kernels: 5.02 us -> 1.98 us  [blend_norm(): pl.pallas_call(blend_kernel, out_shape=(jax.ShapeDtypeStruct((rows, width...]
  transfers between devices with their start and end apart: 27 -> 27, of which waited for: 11 -> 7; matrix products, arithmetic and copies ran while one was open for 3% -> 2% of each run, Pallas kernels for 9% -> 12%
where the time goes in v1:
time: 232 us; the launch traced here: 231 us
  starting transfers between devices  93.9 us (40%)
  Pallas kernels  72.4 us (31%)
  waiting for transfers between devices  55.6 us (24%)
  local copies, waits for them, and re-layouts  3.59 us (2%)
  matrix products  2.55 us (1%)
  other arithmetic  2.44 us (1%)
    ppermute x17, starting transfers between devices, shifted(): lax.ppermute(block, axis, [(i, (i + step) % count) for i in range(count)])  53.9 us
    pallas_call x1, Pallas kernels, attend(): pl.pallas_call(attend_kernel, grid=(steps,), in_specs=[flags(), flags()]...  39 us
    all_to_all x1, waiting for transfers between devices, body(): lax.all_to_all(outgoing, TY + TX, split_axis=0, concat_axis=0, tiled=True)  28.9 us
    ppermute x17, waiting for transfers between devices, shifted(): lax.ppermute(block, axis, [(i, (i + step) % count) for i in range(count)])  22.7 us
    ppermute x8, starting transfers between devices, passed_along(): return lax.ppermute(block, axis, route)  17.1 us
    all_to_all x1, starting transfers between devices, body(): lax.all_to_all(after(slots, (along_z, along_y, updated)), TY + TX, split_...  11.8 us
    all_to_all x1, starting transfers between devices, body(): lax.all_to_all(outgoing, TY + TX, split_axis=0, concat_axis=0, tiled=True)  11.1 us
    pallas_call x1, Pallas kernels, finish(): pl.pallas_call(finish_kernel, out_shape=(jax.ShapeDtypeStruct((rows, widt...  7.02 us
  transfers between devices with their start and end apart: 27, of which 7 were waited for; matrix products, arithmetic and copies ran while one was open for 2% of the time, Pallas kernels for 12%

profile of v1, /device:TPU:0, one launch (start us, length us, event | category | flops | bytes accessed | tf_op | source)
XLA Modules:
  0.0 231.4 jit_solution(8121954284438894899)
XLA Ops:
  0.6 4.5 %pick_rows.1 = bf16[1024,1024]{1,0:T(8,128)(2,1)} custom-call(s32[1,1024]{1,0:T(1,128)} %rows_ref.3, bf16[512,1024]{1,0:T(8,128)(2,1)} %table_ref.1), custom_call_target="tpu_custom_call" | custom-call | tf_op jit(solution)/shard_map/pick_rows/pallas_call | solution.py:36
  5.1 11.1 %all-to-all-start = ((bf16[128,8,1024]{2,1,0:T(8,128)(2,1)}), bf16[128,8,1024]{2,1,0:T(8,128)(2,1)S(1)}, u32[]{:S(2)}, u32[]{:S(2)}) async-start(bf16[128,8,1024]{2,1,0:T(8,128)(2,1)} %bitcast.31), calls=%async_computation | async-start | bytes 4194304 | tf_op jit(solution)/shard_map/all_to_all | solution.py:400
  17.8 28.9 %all-to-all-done = bf16[128,8,1024]{2,1,0:T(8,128)(2,1)S(1)} async-done(((bf16[128,8,1024]{2,1,0:T(8,128)(2,1)}), bf16[128,8,1024]{2,1,0:T(8,128)(2,1)S(1)}, u32[]{:S(2)}, u32[]{:S(2)}) %all-to-all-start) | async-done | bytes 2097184 | tf_op jit(solution)/shard_map/all_to_all | solution.py:400
  55.8 7.0 %project.1 = (bf16[256,1024]{1,0:T(8,128)(2,1)}, bf16[256,1024]{1,0:T(8,128)(2,1)}, bf16[256,1024]{1,0:T(8,128)(2,1)}, bf16[256,1024]{1,0:T(8,128)(2,1)}) custom-call(bf16[256,1024]{1,0:T(8,128)(2,1)} %copy-done.3, bf16[256,1024]{1,0:T(8,128)(2,1)} %bitcast.32, bf16[1024,1024]{1,0:T(8,128)(2,1)} %wq_ref.3, bf16[1024,1024]{1,0:T(8,128)(2,1)} %wk_ref.3, ...), custom_call_target="tpu_custom_call" | custom-call | flops 2100000000 | bytes 11000000 | tf_op jit(solution)/shard_map/project/pallas_call | solution.py:121
  62.8 4.0 %collective-permute-done.1.down_ref = bf16[256,1024]{1,0:T(8,128)(2,1)S(1)} collective-permute-done((bf16[256,1024]{1,0:T(8,128)(2,1)S(1)}, bf16[256,1024]{1,0:T(8,128)(2,1)S(1)}, u32[]{:S(2)}, u32[]{:S(2)}) %collective-permute-start.1) | collective-permute-done | bytes 524320 | tf_op jit(solution)/shard_map/ppermute | solution.py:373
  67.9 39.0 %attend.1 = (bf16[4,2,4,128,256]{4,3,2,1,0:T(8,128)(2,1)}, bf16[4,2,4,128,256]{4,3,2,1,0:T(8,128)(2,1)}, bf16[4,2,4,128,256]{4,3,2,1,0:T(8,128)(2,1)}, bf16[4,2,...) custom-call(s32[1]{0:T(128)} %bitcast.1.core_ref, ...), custom_call_target="tpu_custom_call" | custom-call | flops 33999998976 | bytes 32000000 | tf_op jit(solution)/shard_map/attend/pallas_call | solution.py:229
  109.6 5.2 %collective-permute-start.7 = (bf16[256,1024]{1,0:T(8,128)(2,1)}, bf16[256,1024]{1,0:T(8,128)(2,1)S(1)}, u32[]{:S(2)}, u32[]{:S(2)}) collective-permute-start(bf16[256,1024]{1,0:T(8,128)(2,1)} %get-tuple-element.60), channel_id=1, source_target_pairs={{0,16},{16,32},{32,48},{48,64},{64,80},{80,96},{96,112},{1,17},{17... | collective-permute-start | bytes 1572872 | tf_op jit(solution)/shard_map/ppermute | solution.py:373
  116.1 3.9 %collective-permute-start.9 = (bf16[256,1024]{1,0:T(8,128)(2,1)}, bf16[256,1024]{1,0:T(8,128)(2,1)}, u32[]{:S(2)}, u32[]{:S(2)}) collective-permute-start(bf16[256,1024]{1,0:T(8,128)(2,1)} %get-tuple-element.62), channel_id=1, source_target_pairs={{0,1},{1,2},{2,3},{3,4},{4,5},{5,6},{6,7},{7,8},{8,9},{9,10},{10,1... | collective-permute-start | bytes 1572872 | tf_op jit(solution)/shard_map/ppermute | solution.py:373
  120.0 6.0 %split_sum.1 = (bf16[2,4,128,256]{3,2,1,0:T(8,128)(2,1)}, bf16[2,4,128,256]{3,2,1,0:T(8,128)(2,1)}, bf16[2,4,128,256]{3,2,1,0:T(8,128)(2,1)}, bf16[2,4,128,256]{...) custom-call(s32[1]{0:T(128)} %bitcast.7.refs_0_.here_ref, ...), custom_call_target="tpu_custom_call" | custom-call | flops 1000000 | bytes 12000000 | tf_op jit(solution)/shard_map/split_sum/pallas_call | solution.py:265
  126.7 2.4 %collective-permute-start.11 = (bf16[2,4,128,256]{3,2,1,0:T(8,128)(2,1)}, bf16[2,4,128,256]{3,2,1,0:T(8,128)(2,1)}, u32[]{:S(2)}, u32[]{:S(2)}) collective-permute-start(bf16[2,4,128,256]{3,2,1,0:T(8,128)(2,1)} %get-tuple-element.69), channel_id=1, source_target_pairs={{0,8},{4,12},{8,0},{12,4},{1,9},{5,13},{9,1},{13,5},{2,10},{6,14},... | collective-permute-start | bytes 1572872 | tf_op jit(solution)/shard_map/ppermute | solution.py:363
  132.0 15.1 %collective-permute-start.14 = (bf16[2,4,128,256]{3,2,1,0:T(8,128)(2,1)}, bf16[2,4,128,256]{3,2,1,0:T(8,128)(2,1)}, u32[]{:S(2)}, u32[]{:S(2)}) collective-permute-start(bf16[2,4,128,256]{3,2,1,0:T(8,128)(2,1)} %get-tuple-element.72), channel_id=1, source_target_pairs={{0,32},{16,48},{32,0},{48,16},{1,33},{17,49},{33,1},{49,17},{2,34}... | collective-permute-start | bytes 1572872 | tf_op jit(solution)/shard_map/ppermute | solution.py:363
  147.2 12.2 %collective-permute-start.15 = (bf16[2,4,128,256]{3,2,1,0:T(8,128)(2,1)}, bf16[2,4,128,256]{3,2,1,0:T(8,128)(2,1)}, u32[]{:S(2)}, u32[]{:S(2)}) collective-permute-start(bf16[2,4,128,256]{3,2,1,0:T(8,128)(2,1)} %get-tuple-element.73), channel_id=1, source_target_pairs={{0,48},{16,0},{32,16},{48,32},{1,49},{17,1},{33,17},{49,33},{2,50}... | collective-permute-start | bytes 1572872 | tf_op jit(solution)/shard_map/ppermute | solution.py:363
  159.4 7.0 %finish.1 = (bf16[256,1024]{1,0:T(8,128)(2,1)}, bf16[1024,1024]{1,0:T(8,128)(2,1)}) custom-call(f32[256,1024]{1,0:T(8,128)} %get-tuple-element.58.own_ref, bf16[256,1024]{1,0:T(8,128)(2,1)} %copy-done.12, bf16[256,1024]{1,0:T(8,128)(2,1)} %copy-done.13, bf16[256,1024]{1,0:T(8,128)(2,1)} %collective-permute-done.8.left_ref, ...), custom_call_target="tpu_custom_call" | custom-call | tf_op jit(solution)/shard_map/finish/pallas_call | solution.py:346
  166.4 2.5 %fusion = bf16[256,1024]{1,0:T(8,128)(2,1)} fusion(bf16[256,1024]{1,0:T(8,128)(2,1)} %get-tuple-element.66, bf16[1024,1024]{1,0:T(8,128)(2,1)S(1)} %copy-done.9, bf16[1,1,256,1024]{3,2,1,0:T(8,128)(2,1)S(1)} %copy-done.4), kind=kOutput, calls=%fused_computation.1 | convolution fusion | flops 537657344 | bytes 3670016 | tf_op jit(solution)/shard_map/dot_general | solution.py:428
  169.0 5.8 %collective-permute-done.15.refs_3_ = bf16[2,4,128,256]{3,2,1,0:T(8,128)(2,1)} collective-permute-done((bf16[2,4,128,256]{3,2,1,0:T(8,128)(2,1)}, bf16[2,4,128,256]{3,2,1,0:T(8,128)(2,1)}, u32[]{:S(2)}, u32[]{:S(2)}) %collective-permute-start.15) | collective-permute-done | bytes 524320 | tf_op jit(solution)/shard_map/ppermute | solution.py:363
  174.8 11.8 %all-to-all-start.1 = ((bf16[128,8,1024]{2,1,0:T(8,128)(2,1)}), bf16[128,8,1024]{2,1,0:T(8,128)(2,1)S(1)}, u32[]{:S(2)}, u32[]{:S(2)}) async-start(bf16[128,8,1024]{2,1,0:T(8,128)(2,1)} %bitcast.35), calls=%async_computation.1 | async-start | bytes 4194304 | tf_op jit(solution)/shard_map/all_to_all | solution.py:430
  186.6 2.4 %join_sum.3 = (bf16[2,2,2,8,1024]{4,3,2,1,0:T(8,128)(2,1)}, bf16[2,2,2,8,1024]{4,3,2,1,0:T(8,128)(2,1)}, bf16[2,2,2,8,1024]{4,3,2,1,0:T(8,128)(2,1)}, bf16[2,2,2,8,1024]{4,3,2,1,0:T(8,128)(2,1)}) custom-call(s32[1]{0:T(128)} %bitcast.7.refs_0_.here_ref, bf16[2,4,128,256]{3,2,1,0:T(8,128)(2,1)} %get-tuple-element.56.refs_0_, ...), custom_call_target="tpu_custom_call" | custom-call | flops 1000000 | bytes 6000000 | tf_op jit(solution)/shard_map/join_sum/pallas_call | solution.py:316
  190.1 2.7 %collective-permute-start.20 = (bf16[2,2,2,8,1024]{4,3,2,1,0:T(8,128)(2,1)}, bf16[2,2,2,8,1024]{4,3,2,1,0:T(8,128)(2,1)S(1)}, u32[]{:S(2)}, u32[]{:S(2)}) collective-permute-start(bf16[2,2,2,8,1024]{4,3,2,1,0:T(8,128)(2,1)} %get-tuple-element.83), channel_id=1, source_target_pairs={{0,32},{16,48},{32,0},{48,16},{1,33},{17,49},{33,1},{49,17},{2,34}... | collective-permute-start | bytes 393224 | tf_op jit(solution)/shard_map/ppermute | solution.py:363
  194.2 2.4 %join_sum.2 = (bf16[2,2,2,8,1024]{4,3,2,1,0:T(8,128)(2,1)}, bf16[2,2,2,8,1024]{4,3,2,1,0:T(8,128)(2,1)}, bf16[2,2,2,8,1024]{4,3,2,1,0:T(8,128)(2,1)}, bf16[2,2,2,8,1024]{4,3,2,1,0:T(8,128)(2,1)}) custom-call(s32[1]{0:T(128)} %bitcast.8.refs_1_.here_ref, bf16[2,4,128,256]{3,2,1,0:T(8,128)(2,1)} %get-tuple-element.57.refs_0_, ...), custom_call_target="tpu_custom_call" | custom-call | flops 1000000 | bytes 6000000 | tf_op jit(solution)/shard_map/join_sum/pallas_call | solution.py:316
  198.3 3.2 %collective-permute-start.17 = (bf16[2,2,2,8,1024]{4,3,2,1,0:T(8,128)(2,1)}, bf16[2,2,2,8,1024]{4,3,2,1,0:T(8,128)(2,1)S(1)}, u32[]{:S(2)}, u32[]{:S(2)}) collective-permute-start(bf16[2,2,2,8,1024]{4,3,2,1,0:T(8,128)(2,1)} %get-tuple-element.78), channel_id=1, source_target_pairs={{0,8},{4,12},{8,0},{12,4},{1,9},{5,13},{9,1},{13,5},{2,10},{6,14},... | collective-permute-start | bytes 393224 | tf_op jit(solution)/shard_map/ppermute | solution.py:363
  201.5 13.3 %collective-permute-done.19 = bf16[2,2,2,8,1024]{4,3,2,1,0:T(8,128)(2,1)S(1)} collective-permute-done((bf16[2,2,2,8,1024]{4,3,2,1,0:T(8,128)(2,1)}, bf16[2,2,2,8,1024]{4,3,2,1,0:T(8,128)(2,1)S(1)}, u32[]{:S(2)}, u32[]{:S(2)}) %collective-permute-start.19) | collective-permute-done | bytes 131104 | tf_op jit(solution)/shard_map/ppermute | solution.py:363
  214.8 3.3 %collective-permute-start.18 = (bf16[2,2,2,8,1024]{4,3,2,1,0:T(8,128)(2,1)}, bf16[2,2,2,8,1024]{4,3,2,1,0:T(8,128)(2,1)S(1)}, u32[]{:S(2)}, u32[]{:S(2)}) collective-permute-start(bf16[2,2,2,8,1024]{4,3,2,1,0:T(8,128)(2,1)} %get-tuple-element.79), channel_id=1, source_target_pairs={{0,12},{4,0},{8,4},{12,8},{1,13},{5,1},{9,5},{13,9},{2,14},{6,2},{... | collective-permute-start | bytes 393224 | tf_op jit(solution)/shard_map/ppermute | solution.py:363
  223.6 2.9 %collective-permute-start.23 = (bf16[4,8,1024]{2,1,0:T(8,128)(2,1)S(1)}, bf16[4,8,1024]{2,1,0:T(8,128)(2,1)S(1)}, u32[]{:S(2)}, u32[]{:S(2)}) collective-permute-start(bf16[4,8,1024]{2,1,0:T(8,128)(2,1)S(1)} %get-tuple-element.88), channel_id=1, source_target_pairs={{0,64},{2,66},{64,0},{66,2},{1,65},{3,67},{65,1},{67,3},{4,68},{6,... | collective-permute-start | bytes 196616 | tf_op jit(solution)/shard_map/ppermute | solution.py:363
  227.7 2.2 add_rows.1
  (93 shorter events, 31.6 us)
Async XLA Ops:
  5.1 41.6 %all-to-all-start = ((bf16[128,8,1024]{2,1,0:T(8,128)(2,1)}), bf16[128,8,1024]{2,1,0:T(8,128)(2,1)S(1)}, u32[]{:S(2)}, u32[]{:S(2)}) async-start(bf16[128,8,1024]{2,1,0:T(8,128)(2,1)} %bitcast.31), calls=%async_computation | async-start | bytes 4194304 | tf_op jit(solution)/shard_map/all_to_all | solution.py:400
  50.3 12.5 %collective-permute-start = (bf16[256,1024]{1,0:T(8,128)(2,1)S(1)}, bf16[256,1024]{1,0:T(8,128)(2,1)S(1)}, u32[]{:S(2)}, u32[]{:S(2)}) collective-permute-start(bf16[256,1024]{1,0:T(8,128)(2,1)S(1)} %get-tuple-element.45.in_ref.own_ref), channel_id=1, source_target_pairs={{0,16},{16,32},{32,48},{48,64},{64,80},{80,96},{96,112},{1,17},{17... | collective-permute-start | bytes 1572872 | tf_op jit(solution)/shard_map/ppermute | solution.py:373
  51.6 15.1 %collective-permute-start.1 = (bf16[256,1024]{1,0:T(8,128)(2,1)S(1)}, bf16[256,1024]{1,0:T(8,128)(2,1)S(1)}, u32[]{:S(2)}, u32[]{:S(2)}) collective-permute-start(bf16[256,1024]{1,0:T(8,128)(2,1)S(1)} %get-tuple-element.45.in_ref.own_ref), channel_id=1, source_target_pairs={{16,0},{32,16},{48,32},{64,48},{80,64},{96,80},{112,96},{17,1},{33... | collective-permute-start | bytes 1572872 | tf_op jit(solution)/shard_map/ppermute | solution.py:373
  52.9 13.8 %collective-permute-start.2 = (bf16[256,1024]{1,0:T(8,128)(2,1)S(1)}, bf16[256,1024]{1,0:T(8,128)(2,1)S(1)}, u32[]{:S(2)}, u32[]{:S(2)}) collective-permute-start(bf16[256,1024]{1,0:T(8,128)(2,1)S(1)} %get-tuple-element.45.in_ref.own_ref), channel_id=1, source_target_pairs={{0,1},{1,2},{2,3},{3,4},{4,5},{5,6},{6,7},{7,8},{8,9},{9,10},{10,1... | collective-permute-start | bytes 1572872 | tf_op jit(solution)/shard_map/ppermute | solution.py:373
  54.3 12.5 %collective-permute-start.3 = (bf16[256,1024]{1,0:T(8,128)(2,1)S(1)}, bf16[256,1024]{1,0:T(8,128)(2,1)S(1)}, u32[]{:S(2)}, u32[]{:S(2)}) collective-permute-start(bf16[256,1024]{1,0:T(8,128)(2,1)S(1)} %get-tuple-element.45.in_ref.own_ref), channel_id=1, source_target_pairs={{1,0},{2,1},{3,2},{4,3},{5,4},{6,5},{7,6},{8,7},{9,8},{10,9},{11,1... | collective-permute-start | bytes 1572872 | tf_op jit(solution)/shard_map/ppermute | solution.py:373
  106.9 9.1 %collective-permute-start.4 = (bf16[4,2,4,128,256]{4,3,2,1,0:T(8,128)(2,1)}, bf16[4,2,4,128,256]{4,3,2,1,0:T(8,128)(2,1)S(1)}, u32[]{:S(2)}, u32[]{:S(2)}) collective-permute-start(bf16[4,2,4,128,256]{4,3,2,1,0:T(8,128)(2,1)} %get-tuple-element.53), channel_id=1, source_target_pairs={{0,1},{1,0},{2,3},{3,2},{4,5},{5,4},{6,7},{7,6},{8,9},{9,8},{10,11... | collective-permute-start | bytes 6291464 | tf_op jit(solution)/shard_map/ppermute | solution.py:363
  108.2 11.8 %collective-permute-start.5 = (bf16[4,2,4,128,256]{4,3,2,1,0:T(8,128)(2,1)}, bf16[4,2,4,128,256]{4,3,2,1,0:T(8,128)(2,1)}, u32[]{:S(2)}, u32[]{:S(2)}) collective-permute-start(bf16[4,2,4,128,256]{4,3,2,1,0:T(8,128)(2,1)} %get-tuple-element.55), channel_id=1, source_target_pairs={{0,1},{1,0},{2,3},{3,2},{4,5},{5,4},{6,7},{7,6},{8,9},{9,8},{10,11... | collective-permute-start | bytes 6291464 | tf_op jit(solution)/shard_map/ppermute | solution.py:363
  108.3 18.4 %collective-permute-start.6 = (bf16[256,1024]{1,0:T(8,128)(2,1)}, bf16[256,1024]{1,0:T(8,128)(2,1)S(1)}, u32[]{:S(2)}, u32[]{:S(2)}) collective-permute-start(bf16[256,1024]{1,0:T(8,128)(2,1)} %get-tuple-element.59), channel_id=1, source_target_pairs={{16,0},{32,16},{48,32},{64,48},{80,64},{96,80},{112,96},{17,1},{33... | collective-permute-start | bytes 1572872 | tf_op jit(solution)/shard_map/ppermute | solution.py:373
  109.6 19.5 %collective-permute-start.7 = (bf16[256,1024]{1,0:T(8,128)(2,1)}, bf16[256,1024]{1,0:T(8,128)(2,1)S(1)}, u32[]{:S(2)}, u32[]{:S(2)}) collective-permute-start(bf16[256,1024]{1,0:T(8,128)(2,1)} %get-tuple-element.60), channel_id=1, source_target_pairs={{0,16},{16,32},{32,48},{48,64},{64,80},{80,96},{96,112},{1,17},{17... | collective-permute-start | bytes 1572872 | tf_op jit(solution)/shard_map/ppermute | solution.py:373
  114.8 15.5 %collective-permute-start.8 = (bf16[256,1024]{1,0:T(8,128)(2,1)}, bf16[256,1024]{1,0:T(8,128)(2,1)}, u32[]{:S(2)}, u32[]{:S(2)}) collective-permute-start(bf16[256,1024]{1,0:T(8,128)(2,1)} %get-tuple-element.61), channel_id=1, source_target_pairs={{1,0},{2,1},{3,2},{4,3},{5,4},{6,5},{7,6},{8,7},{9,8},{10,9},{11,1... | collective-permute-start | bytes 1572872 | tf_op jit(solution)/shard_map/ppermute | solution.py:373
  116.1 15.9 %collective-permute-start.9 = (bf16[256,1024]{1,0:T(8,128)(2,1)}, bf16[256,1024]{1,0:T(8,128)(2,1)}, u32[]{:S(2)}, u32[]{:S(2)}) collective-permute-start(bf16[256,1024]{1,0:T(8,128)(2,1)} %get-tuple-element.62), channel_id=1, source_target_pairs={{0,1},{1,2},{2,3},{3,4},{4,5},{5,6},{6,7},{7,8},{8,9},{9,10},{10,1... | collective-permute-start | bytes 1572872 | tf_op jit(solution)/shard_map/ppermute | solution.py:373
  125.9 21.2 %collective-permute-start.10 = (bf16[2,4,128,256]{3,2,1,0:T(8,128)(2,1)}, bf16[2,4,128,256]{3,2,1,0:T(8,128)(2,1)S(1)}, u32[]{:S(2)}, u32[]{:S(2)}) collective-permute-start(bf16[2,4,128,256]{3,2,1,0:T(8,128)(2,1)} %get-tuple-element.68), channel_id=1, source_target_pairs={{0,4},{4,8},{8,12},{12,0},{1,5},{5,9},{9,13},{13,1},{2,6},{6,10},{... | collective-permute-start | bytes 1572872 | tf_op jit(solution)/shard_map/ppermute | solution.py:363
  126.7 42.3 %collective-permute-start.11 = (bf16[2,4,128,256]{3,2,1,0:T(8,128)(2,1)}, bf16[2,4,128,256]{3,2,1,0:T(8,128)(2,1)}, u32[]{:S(2)}, u32[]{:S(2)}) collective-permute-start(bf16[2,4,128,256]{3,2,1,0:T(8,128)(2,1)} %get-tuple-element.69), channel_id=1, source_target_pairs={{0,8},{4,12},{8,0},{12,4},{1,9},{5,13},{9,1},{13,5},{2,10},{6,14},... | collective-permute-start | bytes 1572872 | tf_op jit(solution)/shard_map/ppermute | solution.py:363
  129.0 39.9 %collective-permute-start.12 = (bf16[2,4,128,256]{3,2,1,0:T(8,128)(2,1)}, bf16[2,4,128,256]{3,2,1,0:T(8,128)(2,1)}, u32[]{:S(2)}, u32[]{:S(2)}) collective-permute-start(bf16[2,4,128,256]{3,2,1,0:T(8,128)(2,1)} %get-tuple-element.70), channel_id=1, source_target_pairs={{0,12},{4,0},{8,4},{12,8},{1,13},{5,1},{9,5},{13,9},{2,14},{6,2},{... | collective-permute-start | bytes 1572872 | tf_op jit(solution)/shard_map/ppermute | solution.py:363
  130.3 38.7 %collective-permute-start.13 = (bf16[2,4,128,256]{3,2,1,0:T(8,128)(2,1)}, bf16[2,4,128,256]{3,2,1,0:T(8,128)(2,1)S(1)}, u32[]{:S(2)}, u32[]{:S(2)}) collective-permute-start(bf16[2,4,128,256]{3,2,1,0:T(8,128)(2,1)} %get-tuple-element.71), channel_id=1, source_target_pairs={{0,16},{16,32},{32,48},{48,0},{1,17},{17,33},{33,49},{49,1},{2,18}... | collective-permute-start | bytes 1572872 | tf_op jit(solution)/shard_map/ppermute | solution.py:363
  132.0 37.0 %collective-permute-start.14 = (bf16[2,4,128,256]{3,2,1,0:T(8,128)(2,1)}, bf16[2,4,128,256]{3,2,1,0:T(8,128)(2,1)}, u32[]{:S(2)}, u32[]{:S(2)}) collective-permute-start(bf16[2,4,128,256]{3,2,1,0:T(8,128)(2,1)} %get-tuple-element.72), channel_id=1, source_target_pairs={{0,32},{16,48},{32,0},{48,16},{1,33},{17,49},{33,1},{49,17},{2,34}... | collective-permute-start | bytes 1572872 | tf_op jit(solution)/shard_map/ppermute | solution.py:363
  147.2 27.7 %collective-permute-start.15 = (bf16[2,4,128,256]{3,2,1,0:T(8,128)(2,1)}, bf16[2,4,128,256]{3,2,1,0:T(8,128)(2,1)}, u32[]{:S(2)}, u32[]{:S(2)}) collective-permute-start(bf16[2,4,128,256]{3,2,1,0:T(8,128)(2,1)} %get-tuple-element.73), channel_id=1, source_target_pairs={{0,48},{16,0},{32,16},{48,32},{1,49},{17,1},{33,17},{49,33},{2,50}... | collective-permute-start | bytes 1572872 | tf_op jit(solution)/shard_map/ppermute | solution.py:363
  174.8 52.9 %all-to-all-start.1 = ((bf16[128,8,1024]{2,1,0:T(8,128)(2,1)}), bf16[128,8,1024]{2,1,0:T(8,128)(2,1)S(1)}, u32[]{:S(2)}, u32[]{:S(2)}) async-start(bf16[128,8,1024]{2,1,0:T(8,128)(2,1)} %bitcast.35), calls=%async_computation.1 | async-start | bytes 4194304 | tf_op jit(solution)/shard_map/all_to_all | solution.py:430
  189.0 25.8 %collective-permute-start.19 = (bf16[2,2,2,8,1024]{4,3,2,1,0:T(8,128)(2,1)}, bf16[2,2,2,8,1024]{4,3,2,1,0:T(8,128)(2,1)S(1)}, u32[]{:S(2)}, u32[]{:S(2)}) collective-permute-start(bf16[2,2,2,8,1024]{4,3,2,1,0:T(8,128)(2,1)} %get-tuple-element.82), channel_id=1, source_target_pairs={{0,16},{16,32},{32,48},{48,0},{1,17},{17,33},{33,49},{49,1},{2,18}... | collective-permute-start | bytes 393224 | tf_op jit(solution)/shard_map/ppermute | solution.py:363
  190.1 28.1 %collective-permute-start.20 = (bf16[2,2,2,8,1024]{4,3,2,1,0:T(8,128)(2,1)}, bf16[2,2,2,8,1024]{4,3,2,1,0:T(8,128)(2,1)S(1)}, u32[]{:S(2)}, u32[]{:S(2)}) collective-permute-start(bf16[2,2,2,8,1024]{4,3,2,1,0:T(8,128)(2,1)} %get-tuple-element.83), channel_id=1, source_target_pairs={{0,32},{16,48},{32,0},{48,16},{1,33},{17,49},{33,1},{49,17},{2,34}... | collective-permute-start | bytes 393224 | tf_op jit(solution)/shard_map/ppermute | solution.py:363
  192.8 25.3 %collective-permute-start.21 = (bf16[2,2,2,8,1024]{4,3,2,1,0:T(8,128)(2,1)}, bf16[2,2,2,8,1024]{4,3,2,1,0:T(8,128)(2,1)S(1)}, u32[]{:S(2)}, u32[]{:S(2)}) collective-permute-start(bf16[2,2,2,8,1024]{4,3,2,1,0:T(8,128)(2,1)} %get-tuple-element.84), channel_id=1, source_target_pairs={{0,48},{16,0},{32,16},{48,32},{1,49},{17,1},{33,17},{49,33},{2,50}... | collective-permute-start | bytes 393224 | tf_op jit(solution)/shard_map/ppermute | solution.py:363
  196.6 23.4 %collective-permute-start.16 = (bf16[2,2,2,8,1024]{4,3,2,1,0:T(8,128)(2,1)}, bf16[2,2,2,8,1024]{4,3,2,1,0:T(8,128)(2,1)S(1)}, u32[]{:S(2)}, u32[]{:S(2)}) collective-permute-start(bf16[2,2,2,8,1024]{4,3,2,1,0:T(8,128)(2,1)} %get-tuple-element.77), channel_id=1, source_target_pairs={{0,4},{4,8},{8,12},{12,0},{1,5},{5,9},{9,13},{13,1},{2,6},{6,10},{... | collective-permute-start | bytes 393224 | tf_op jit(solution)/shard_map/ppermute | solution.py:363
  198.3 21.7 %collective-permute-start.17 = (bf16[2,2,2,8,1024]{4,3,2,1,0:T(8,128)(2,1)}, bf16[2,2,2,8,1024]{4,3,2,1,0:T(8,128)(2,1)S(1)}, u32[]{:S(2)}, u32[]{:S(2)}) collective-permute-start(bf16[2,2,2,8,1024]{4,3,2,1,0:T(8,128)(2,1)} %get-tuple-element.78), channel_id=1, source_target_pairs={{0,8},{4,12},{8,0},{12,4},{1,9},{5,13},{9,1},{13,5},{2,10},{6,14},... | collective-permute-start | bytes 393224 | tf_op jit(solution)/shard_map/ppermute | solution.py:363
  222.1 7.9 %collective-permute-start.22 = (bf16[4,8,1024]{2,1,0:T(8,128)(2,1)S(1)}, bf16[4,8,1024]{2,1,0:T(8,128)(2,1)S(1)}, u32[]{:S(2)}, u32[]{:S(2)}) collective-permute-start(bf16[4,8,1024]{2,1,0:T(8,128)(2,1)S(1)} %get-tuple-element.87), channel_id=1, source_target_pairs={{0,2},{2,64},{64,66},{66,0},{1,3},{3,65},{65,67},{67,1},{4,6},{6,6... | collective-permute-start | bytes 196616 | tf_op jit(solution)/shard_map/ppermute | solution.py:363
  (25 other events, 375.2 us)

commit v2 on v1

--- a/solution.py
+++ b/solution.py
@@ -131,7 +131,7 @@
 
 
 def attend_kernel(
-    core_ref, mask_ref, own_ref, up_ref, down_ref, left_ref, right_ref, grad_ref,
+    core_ref, mask_ref, own_ref, left_ref, right_ref, up_ref, down_ref, grad_ref,
     query_ref, own_key_ref, own_value_ref, g_ref, wq_ref, wk_ref, wv_ref,
     keep_y, send_y, keep_z, send_z, attended_ref, up_grad, down_grad, left_grad, right_grad, own_grad, x_all, x_turned, grads,
 ):
@@ -218,6 +218,7 @@
 def attend(core, mask, tiles, grad_out, projected, w_query, w_key, w_value, ys, zs):
     rows, width = grad_out.shape
     near, lanes = len(tiles), 2 * HEAD_SIZE
+    own, up, down, left, right = tiles
     steps = width // lanes
     whole = lambda: pl.BlockSpec((rows, width), lambda h: (0, 0), pipeline_mode=pl.Buffered(1))
     columns = lambda: pl.BlockSpec((width, lanes), lambda h: (0, h))
@@ -244,7 +245,7 @@
         compiler_params=params(60),
         cost_estimate=pl.CostEstimate(flops=34 * 10**9, bytes_accessed=32 * 10**6, transcendentals=10**6),
         name="attend",
-    )(core, mask, *tiles, grad_out, *projected, w_query, w_key, w_value)
+    )(core, mask, own, left, right, up, down, grad_out, *projected, w_query, w_key, w_value)
 
 
 def split_kernel(counts, *refs):
@@ -427,11 +428,12 @@
     state_grad, slots = finish(own, returned, normed, inverse, gain, grad_out, slot_ids, blend, incoming.shape[0])
     term = jnp.dot(after(attended, slots), w_out, preferred_element_type=F32)
     updated = (state.astype(F32) + term).astype(BF16)
-    sent_back = lax.all_to_all(after(slots, (along_z, along_y, updated)), TY + TX, split_axis=0, concat_axis=0, tiled=True)
+    here_y, here_z = after((here["y"], here["z"]), slots)
+    second_y = swapped(join_sum(here_y, along_z, ys, 1, chunk), "y")
+    sent = after(slots, (along_y, updated, second_y[1]))
+    sent_back = lax.all_to_all(sent, TY + TX, split_axis=0, concat_axis=0, tiled=True)
     global_grad = add_rows(send_rows, sent_back, global_latent.shape[0])
-    here_y, here_z = after((here["y"], here["z"]), slots)
     second_z = swapped(join_sum(here_z, along_y, zs, -1, chunk), "z")
-    second_y = swapped(join_sum(here_y, along_z, ys, 1, chunk), "y")
     total = jnp.concatenate([sum(piece.astype(F32) for piece in group) for group in (second_z, second_y)], axis=2)
     total = total.astype(BF16).reshape(-1, 4, chunk, width)
     place = lax.axis_index(X)

time: 232 us -> 230 us (level)
  starting transfers between devices: 93.9 us -> 83.1 us
  waiting for transfers between devices: 55.6 us -> 64.5 us
    ppermute x17, starting transfers between devices: 53.9 us -> 45.2 us  [shifted(): lax.ppermute(block, axis, [(i, (i + step) % count) for i in range(count)])]
    ppermute x17, waiting for transfers between devices: 22.7 us -> 28 us  [shifted(): lax.ppermute(block, axis, [(i, (i + step) % count) for i in range(count)])]
    ppermute x8, waiting for transfers between devices: 3.98 us -> 7.56 us  [passed_along(): return lax.ppermute(block, axis, route)]
    all_to_all x1, starting transfers between devices: 11.8 us -> 9.26 us  [body(): lax.all_to_all(sent, TY + TX, split_axis=0, concat_axis=0, tiled=True)]
  transfers between devices with their start and end apart: 27 -> 27, of which waited for: 7 -> 8; matrix products, arithmetic and copies ran while one was open for 2% -> 2% of each run, Pallas kernels for 12% -> 12%
where the time goes in v2:
time: 230 us; the launch traced here: 229 us
  starting transfers between devices  83.1 us (36%)
  Pallas kernels  72.4 us (31%)
  waiting for transfers between devices  64.5 us (28%)
  local copies, waits for them, and re-layouts  3.26 us (1%)
  matrix products  2.55 us (1%)
  other arithmetic  2.44 us (1%)
    ppermute x17, starting transfers between devices, shifted(): lax.ppermute(block, axis, [(i, (i + step) % count) for i in range(count)])  45.2 us
    pallas_call x1, Pallas kernels, attend(): pl.pallas_call(attend_kernel, grid=(steps,), in_specs=[flags(), flags()]...  39 us
    all_to_all x1, waiting for transfers between devices, body(): lax.all_to_all(outgoing, TY + TX, split_axis=0, concat_axis=0, tiled=True)  28.9 us
    ppermute x17, waiting for transfers between devices, shifted(): lax.ppermute(block, axis, [(i, (i + step) % count) for i in range(count)])  28 us
    ppermute x8, starting transfers between devices, passed_along(): return lax.ppermute(block, axis, route)  17.5 us
    all_to_all x1, starting transfers between devices, body(): lax.all_to_all(outgoing, TY + TX, split_axis=0, concat_axis=0, tiled=True)  11.1 us
    all_to_all x1, starting transfers between devices, body(): lax.all_to_all(sent, TY + TX, split_axis=0, concat_axis=0, tiled=True)  9.26 us
    ppermute x8, waiting for transfers between devices, passed_along(): return lax.ppermute(block, axis, route)  7.56 us
  transfers between devices with their start and end apart: 27, of which 8 were waited for; matrix products, arithmetic and copies ran while one was open for 2% of the time, Pallas kernels for 12%

profile of v2, /device:TPU:0, one launch (start us, length us, event | category | flops | bytes accessed | tf_op | source)
XLA Modules:
  0.0 229.2 jit_solution(9224686786005226665)
XLA Ops:
  0.6 4.5 %pick_rows.1 = bf16[1024,1024]{1,0:T(8,128)(2,1)} custom-call(s32[1,1024]{1,0:T(1,128)} %rows_ref.3, bf16[512,1024]{1,0:T(8,128)(2,1)} %table_ref.1), custom_call_target="tpu_custom_call" | custom-call | tf_op jit(solution)/shard_map/pick_rows/pallas_call | solution.py:36
  5.1 11.1 %all-to-all-start = ((bf16[128,8,1024]{2,1,0:T(8,128)(2,1)}), bf16[128,8,1024]{2,1,0:T(8,128)(2,1)S(1)}, u32[]{:S(2)}, u32[]{:S(2)}) async-start(bf16[128,8,1024]{2,1,0:T(8,128)(2,1)} %bitcast.31), calls=%async_computation | async-start | bytes 4194304 | tf_op jit(solution)/shard_map/all_to_all | solution.py:401
  17.8 28.9 %all-to-all-done = bf16[128,8,1024]{2,1,0:T(8,128)(2,1)S(1)} async-done(((bf16[128,8,1024]{2,1,0:T(8,128)(2,1)}), bf16[128,8,1024]{2,1,0:T(8,128)(2,1)S(1)}, u32[]{:S(2)}, u32[]{:S(2)}) %all-to-all-start) | async-done | bytes 2097184 | tf_op jit(solution)/shard_map/all_to_all | solution.py:401
  56.1 7.0 %project.1 = (bf16[256,1024]{1,0:T(8,128)(2,1)}, bf16[256,1024]{1,0:T(8,128)(2,1)}, bf16[256,1024]{1,0:T(8,128)(2,1)}, bf16[256,1024]{1,0:T(8,128)(2,1)}) custom-call(bf16[256,1024]{1,0:T(8,128)(2,1)} %copy-done.3, bf16[256,1024]{1,0:T(8,128)(2,1)} %bitcast.32, bf16[1024,1024]{1,0:T(8,128)(2,1)} %wq_ref.3, bf16[1024,1024]{1,0:T(8,128)(2,1)} %wk_ref.3, ...), custom_call_target="tpu_custom_call" | custom-call | flops 2100000000 | bytes 11000000 | tf_op jit(solution)/shard_map/project/pallas_call | solution.py:121
  63.1 2.8 %collective-permute-done.2.up_ref = bf16[256,1024]{1,0:T(8,128)(2,1)S(1)} collective-permute-done((bf16[256,1024]{1,0:T(8,128)(2,1)S(1)}, bf16[256,1024]{1,0:T(8,128)(2,1)S(1)}, u32[]{:S(2)}, u32[]{:S(2)}) %collective-permute-start.2) | collective-permute-done | bytes 524320 | tf_op jit(solution)/shard_map/ppermute | solution.py:374
  66.0 4.7 %collective-permute-done.3.down_ref = bf16[256,1024]{1,0:T(8,128)(2,1)S(1)} collective-permute-done((bf16[256,1024]{1,0:T(8,128)(2,1)S(1)}, bf16[256,1024]{1,0:T(8,128)(2,1)S(1)}, u32[]{:S(2)}, u32[]{:S(2)}) %collective-permute-start.3) | collective-permute-done | bytes 524320 | tf_op jit(solution)/shard_map/ppermute | solution.py:374
  71.5 39.0 %attend.1 = (bf16[4,2,4,128,256]{4,3,2,1,0:T(8,128)(2,1)}, bf16[4,2,4,128,256]{4,3,2,1,0:T(8,128)(2,1)}, bf16[4,2,4,128,256]{4,3,2,1,0:T(8,128)(2,1)}, bf16[4,2,...) custom-call(s32[1]{0:T(128)} %bitcast.1.core_ref, ...), custom_call_target="tpu_custom_call" | custom-call | flops 33999998976 | bytes 32000000 | tf_op jit(solution)/shard_map/attend/pallas_call | solution.py:230
  112.4 5.4 %collective-permute-start.7 = (bf16[256,1024]{1,0:T(8,128)(2,1)}, bf16[256,1024]{1,0:T(8,128)(2,1)}, u32[]{:S(2)}, u32[]{:S(2)}) collective-permute-start(bf16[256,1024]{1,0:T(8,128)(2,1)} %get-tuple-element.60), channel_id=1, source_target_pairs={{0,16},{16,32},{32,48},{48,64},{64,80},{80,96},{96,112},{1,17},{17... | collective-permute-start | bytes 1572872 | tf_op jit(solution)/shard_map/ppermute | solution.py:374
  119.0 3.9 %collective-permute-start.9 = (bf16[256,1024]{1,0:T(8,128)(2,1)}, bf16[256,1024]{1,0:T(8,128)(2,1)}, u32[]{:S(2)}, u32[]{:S(2)}) collective-permute-start(bf16[256,1024]{1,0:T(8,128)(2,1)} %get-tuple-element.62), channel_id=1, source_target_pairs={{0,1},{1,2},{2,3},{3,4},{4,5},{5,6},{6,7},{7,8},{8,9},{9,10},{10,1... | collective-permute-start | bytes 1572872 | tf_op jit(solution)/shard_map/ppermute | solution.py:374
  122.9 6.0 %split_sum.1 = (bf16[2,4,128,256]{3,2,1,0:T(8,128)(2,1)}, bf16[2,4,128,256]{3,2,1,0:T(8,128)(2,1)}, bf16[2,4,128,256]{3,2,1,0:T(8,128)(2,1)}, bf16[2,4,128,256]{...) custom-call(s32[1]{0:T(128)} %bitcast.7.refs_0_.here_ref, ...), custom_call_target="tpu_custom_call" | custom-call | flops 1000000 | bytes 12000000 | tf_op jit(solution)/shard_map/split_sum/pallas_call | solution.py:266
  134.7 11.4 %collective-permute-start.11 = (bf16[2,4,128,256]{3,2,1,0:T(8,128)(2,1)}, bf16[2,4,128,256]{3,2,1,0:T(8,128)(2,1)}, u32[]{:S(2)}, u32[]{:S(2)}) collective-permute-start(bf16[2,4,128,256]{3,2,1,0:T(8,128)(2,1)} %get-tuple-element.69), channel_id=1, source_target_pairs={{0,32},{16,48},{32,0},{48,16},{1,33},{17,49},{33,1},{49,17},{2,34}... | collective-permute-start | bytes 1572872 | tf_op jit(solution)/shard_map/ppermute | solution.py:364
  146.1 12.0 %collective-permute-start.12 = (bf16[2,4,128,256]{3,2,1,0:T(8,128)(2,1)}, bf16[2,4,128,256]{3,2,1,0:T(8,128)(2,1)}, u32[]{:S(2)}, u32[]{:S(2)}) collective-permute-start(bf16[2,4,128,256]{3,2,1,0:T(8,128)(2,1)} %get-tuple-element.70), channel_id=1, source_target_pairs={{0,48},{16,0},{32,16},{48,32},{1,49},{17,1},{33,17},{49,33},{2,50}... | collective-permute-start | bytes 1572872 | tf_op jit(solution)/shard_map/ppermute | solution.py:364
  158.1 6.9 %finish.1 = (bf16[256,1024]{1,0:T(8,128)(2,1)}, bf16[1024,1024]{1,0:T(8,128)(2,1)}) custom-call(f32[256,1024]{1,0:T(8,128)} %get-tuple-element.58.own_ref, bf16[256,1024]{1,0:T(8,128)(2,1)} %copy-done.11, bf16[256,1024]{1,0:T(8,128)(2,1)} %collective-permute-done.7.down_ref, bf16[256,1024]{1,0:T(8,128)(2,1)} %copy-done.12, ...), custom_call_target="tpu_custom_call" | custom-call | tf_op jit(solution)/shard_map/finish/pallas_call | solution.py:347
  164.9 2.5 %join_sum.2 = (bf16[2,2,2,8,1024]{4,3,2,1,0:T(8,128)(2,1)}, bf16[2,2,2,8,1024]{4,3,2,1,0:T(8,128)(2,1)}, bf16[2,2,2,8,1024]{4,3,2,1,0:T(8,128)(2,1)}, bf16[2,2,2,8,1024]{4,3,2,1,0:T(8,128)(2,1)}) custom-call(s32[1]{0:T(128)} %bitcast.7.refs_0_.here_ref, bf16[2,4,128,256]{3,2,1,0:T(8,128)(2,1)} %get-tuple-element.56.refs_0_, ...), custom_call_target="tpu_custom_call" | custom-call | flops 1000000 | bytes 6000000 | tf_op jit(solution)/shard_map/join_sum/pallas_call | solution.py:317
  167.5 2.5 %fusion = bf16[256,1024]{1,0:T(8,128)(2,1)} fusion(bf16[256,1024]{1,0:T(8,128)(2,1)} %get-tuple-element.66, bf16[1024,1024]{1,0:T(8,128)(2,1)S(1)} %copy-done.9, bf16[1,1,256,1024]{3,2,1,0:T(8,128)(2,1)S(1)} %copy-done.4), kind=kOutput, calls=%fused_computation.1 | convolution fusion | flops 537657344 | bytes 3670016 | tf_op jit(solution)/shard_map/dot_general | solution.py:429
  170.1 3.3 %collective-permute-done.12.refs_3_ = bf16[2,4,128,256]{3,2,1,0:T(8,128)(2,1)} collective-permute-done((bf16[2,4,128,256]{3,2,1,0:T(8,128)(2,1)}, bf16[2,4,128,256]{3,2,1,0:T(8,128)(2,1)}, u32[]{:S(2)}, u32[]{:S(2)}) %collective-permute-start.12) | collective-permute-done | bytes 524320 | tf_op jit(solution)/shard_map/ppermute | solution.py:364
  173.4 3.7 %collective-permute-done.16 = bf16[2,2,2,8,1024]{4,3,2,1,0:T(8,128)(2,1)S(1)} collective-permute-done((bf16[2,2,2,8,1024]{4,3,2,1,0:T(8,128)(2,1)}, bf16[2,2,2,8,1024]{4,3,2,1,0:T(8,128)(2,1)S(1)}, u32[]{:S(2)}, u32[]{:S(2)}) %collective-permute-start.16) | collective-permute-done | bytes 131104 | tf_op jit(solution)/shard_map/ppermute | solution.py:364
  177.1 9.3 %all-to-all-start.1 = ((bf16[128,8,1024]{2,1,0:T(8,128)(2,1)}), bf16[128,8,1024]{2,1,0:T(8,128)(2,1)S(1)}, u32[]{:S(2)}, u32[]{:S(2)}) async-start(bf16[128,8,1024]{2,1,0:T(8,128)(2,1)} %bitcast.35), calls=%async_computation.1 | async-start | bytes 4194304 | tf_op jit(solution)/shard_map/all_to_all | solution.py:434
  186.4 2.5 %collective-permute-start.20 = (bf16[2,2,2,8,1024]{4,3,2,1,0:T(8,128)(2,1)S(1)}, bf16[2,2,2,8,1024]{4,3,2,1,0:T(8,128)(2,1)S(1)}, u32[]{:S(2)}, u32[]{:S(2)}) collective-permute-start(bf16[2,2,2,8,1024]{4,3,2,1,0:T(8,128)(2,1)S(1)} %copy-done.23), channel_id=1, source_target_pairs={{0,32},{16,48},{32,0},{48,16},{1,33},{17,49},{33,1},{49,17},{2,34}... | collective-permute-start | bytes 393224 | tf_op jit(solution)/shard_map/ppermute | solution.py:364
  190.2 2.4 %join_sum.3 = (bf16[2,2,2,8,1024]{4,3,2,1,0:T(8,128)(2,1)}, bf16[2,2,2,8,1024]{4,3,2,1,0:T(8,128)(2,1)}, bf16[2,2,2,8,1024]{4,3,2,1,0:T(8,128)(2,1)}, bf16[2,2,2,8,1024]{4,3,2,1,0:T(8,128)(2,1)}) custom-call(s32[1]{0:T(128)} %bitcast.8.refs_1_.here_ref, bf16[2,4,128,256]{3,2,1,0:T(8,128)(2,1)} %get-tuple-element.57.refs_0_, ...), custom_call_target="tpu_custom_call" | custom-call | flops 1000000 | bytes 6000000 | tf_op jit(solution)/shard_map/join_sum/pallas_call | solution.py:317
  194.2 3.2 %collective-permute-start.18 = (bf16[2,2,2,8,1024]{4,3,2,1,0:T(8,128)(2,1)}, bf16[2,2,2,8,1024]{4,3,2,1,0:T(8,128)(2,1)S(1)}, u32[]{:S(2)}, u32[]{:S(2)}) collective-permute-start(bf16[2,2,2,8,1024]{4,3,2,1,0:T(8,128)(2,1)} %get-tuple-element.80), channel_id=1, source_target_pairs={{0,8},{4,12},{8,0},{12,4},{1,9},{5,13},{9,1},{13,5},{2,10},{6,14},... | collective-permute-start | bytes 393224 | tf_op jit(solution)/shard_map/ppermute | solution.py:364
  198.6 16.1 %collective-permute-done.20 = bf16[2,2,2,8,1024]{4,3,2,1,0:T(8,128)(2,1)S(1)} collective-permute-done((bf16[2,2,2,8,1024]{4,3,2,1,0:T(8,128)(2,1)S(1)}, bf16[2,2,2,8,1024]{4,3,2,1,0:T(8,128)(2,1)S(1)}, u32[]{:S(2)}, u32[]{:S(2)}) %collective-permute-start.20) | collective-permute-done | bytes 131104 | tf_op jit(solution)/shard_map/ppermute | solution.py:364
  215.9 3.7 %collective-permute-done.17 = bf16[2,2,2,8,1024]{4,3,2,1,0:T(8,128)(2,1)S(1)} collective-permute-done((bf16[2,2,2,8,1024]{4,3,2,1,0:T(8,128)(2,1)}, bf16[2,2,2,8,1024]{4,3,2,1,0:T(8,128)(2,1)S(1)}, u32[]{:S(2)}, u32[]{:S(2)}) %collective-permute-start.17) | collective-permute-done | bytes 131104 | tf_op jit(solution)/shard_map/ppermute | solution.py:364
  221.3 2.7 %collective-permute-start.23 = (bf16[4,8,1024]{2,1,0:T(8,128)(2,1)S(1)}, bf16[4,8,1024]{2,1,0:T(8,128)(2,1)S(1)}, u32[]{:S(2)}, u32[]{:S(2)}) collective-permute-start(bf16[4,8,1024]{2,1,0:T(8,128)(2,1)S(1)} %get-tuple-element.88), channel_id=1, source_target_pairs={{0,64},{2,66},{64,0},{66,2},{1,65},{3,67},{65,1},{67,3},{4,68},{6,... | collective-permute-start | bytes 196616 | tf_op jit(solution)/shard_map/ppermute | solution.py:364
  (97 shorter events, 32.7 us)
Async XLA Ops:
  5.1 41.6 %all-to-all-start = ((bf16[128,8,1024]{2,1,0:T(8,128)(2,1)}), bf16[128,8,1024]{2,1,0:T(8,128)(2,1)S(1)}, u32[]{:S(2)}, u32[]{:S(2)}) async-start(bf16[128,8,1024]{2,1,0:T(8,128)(2,1)} %bitcast.31), calls=%async_computation | async-start | bytes 4194304 | tf_op jit(solution)/shard_map/all_to_all | solution.py:401
  50.3 12.8 %collective-permute-start = (bf16[256,1024]{1,0:T(8,128)(2,1)S(1)}, bf16[256,1024]{1,0:T(8,128)(2,1)S(1)}, u32[]{:S(2)}, u32[]{:S(2)}) collective-permute-start(bf16[256,1024]{1,0:T(8,128)(2,1)S(1)} %get-tuple-element.45.in_ref.own_ref), channel_id=1, source_target_pairs={{0,1},{1,2},{2,3},{3,4},{4,5},{5,6},{6,7},{7,8},{8,9},{9,10},{10,1... | collective-permute-start | bytes 1572872 | tf_op jit(solution)/shard_map/ppermute | solution.py:374
  51.6 11.5 %collective-permute-start.1 = (bf16[256,1024]{1,0:T(8,128)(2,1)S(1)}, bf16[256,1024]{1,0:T(8,128)(2,1)S(1)}, u32[]{:S(2)}, u32[]{:S(2)}) collective-permute-start(bf16[256,1024]{1,0:T(8,128)(2,1)S(1)} %get-tuple-element.45.in_ref.own_ref), channel_id=1, source_target_pairs={{1,0},{2,1},{3,2},{4,3},{5,4},{6,5},{7,6},{8,7},{9,8},{10,9},{11,1... | collective-permute-start | bytes 1572872 | tf_op jit(solution)/shard_map/ppermute | solution.py:374
  52.9 13.0 %collective-permute-start.2 = (bf16[256,1024]{1,0:T(8,128)(2,1)S(1)}, bf16[256,1024]{1,0:T(8,128)(2,1)S(1)}, u32[]{:S(2)}, u32[]{:S(2)}) collective-permute-start(bf16[256,1024]{1,0:T(8,128)(2,1)S(1)} %get-tuple-element.45.in_ref.own_ref), channel_id=1, source_target_pairs={{0,16},{16,32},{32,48},{48,64},{64,80},{80,96},{96,112},{1,17},{17... | collective-permute-start | bytes 1572872 | tf_op jit(solution)/shard_map/ppermute | solution.py:374
  54.6 16.1 %collective-permute-start.3 = (bf16[256,1024]{1,0:T(8,128)(2,1)S(1)}, bf16[256,1024]{1,0:T(8,128)(2,1)S(1)}, u32[]{:S(2)}, u32[]{:S(2)}) collective-permute-start(bf16[256,1024]{1,0:T(8,128)(2,1)S(1)} %get-tuple-element.45.in_ref.own_ref), channel_id=1, source_target_pairs={{16,0},{32,16},{48,32},{64,48},{80,64},{96,80},{112,96},{17,1},{33... | collective-permute-start | bytes 1572872 | tf_op jit(solution)/shard_map/ppermute | solution.py:374
  110.5 8.5 %collective-permute-start.4 = (bf16[4,2,4,128,256]{4,3,2,1,0:T(8,128)(2,1)}, bf16[4,2,4,128,256]{4,3,2,1,0:T(8,128)(2,1)S(1)}, u32[]{:S(2)}, u32[]{:S(2)}) collective-permute-start(bf16[4,2,4,128,256]{4,3,2,1,0:T(8,128)(2,1)} %get-tuple-element.53), channel_id=1, source_target_pairs={{0,1},{1,0},{2,3},{3,2},{4,5},{5,4},{6,7},{7,6},{8,9},{9,8},{10,11... | collective-permute-start | bytes 6291464 | tf_op jit(solution)/shard_map/ppermute | solution.py:364
  111.0 11.9 %collective-permute-start.5 = (bf16[4,2,4,128,256]{4,3,2,1,0:T(8,128)(2,1)}, bf16[4,2,4,128,256]{4,3,2,1,0:T(8,128)(2,1)}, u32[]{:S(2)}, u32[]{:S(2)}) collective-permute-start(bf16[4,2,4,128,256]{4,3,2,1,0:T(8,128)(2,1)} %get-tuple-element.55), channel_id=1, source_target_pairs={{0,1},{1,0},{2,3},{3,2},{4,5},{5,4},{6,7},{7,6},{8,9},{9,8},{10,11... | collective-permute-start | bytes 6291464 | tf_op jit(solution)/shard_map/ppermute | solution.py:364
  111.1 18.9 %collective-permute-start.6 = (bf16[256,1024]{1,0:T(8,128)(2,1)}, bf16[256,1024]{1,0:T(8,128)(2,1)S(1)}, u32[]{:S(2)}, u32[]{:S(2)}) collective-permute-start(bf16[256,1024]{1,0:T(8,128)(2,1)} %get-tuple-element.59), channel_id=1, source_target_pairs={{16,0},{32,16},{48,32},{64,48},{80,64},{96,80},{112,96},{17,1},{33... | collective-permute-start | bytes 1572872 | tf_op jit(solution)/shard_map/ppermute | solution.py:374
  112.4 19.8 %collective-permute-start.7 = (bf16[256,1024]{1,0:T(8,128)(2,1)}, bf16[256,1024]{1,0:T(8,128)(2,1)}, u32[]{:S(2)}, u32[]{:S(2)}) collective-permute-start(bf16[256,1024]{1,0:T(8,128)(2,1)} %get-tuple-element.60), channel_id=1, source_target_pairs={{0,16},{16,32},{32,48},{48,64},{64,80},{80,96},{96,112},{1,17},{17... | collective-permute-start | bytes 1572872 | tf_op jit(solution)/shard_map/ppermute | solution.py:374
  117.7 16.4 %collective-permute-start.8 = (bf16[256,1024]{1,0:T(8,128)(2,1)}, bf16[256,1024]{1,0:T(8,128)(2,1)S(1)}, u32[]{:S(2)}, u32[]{:S(2)}) collective-permute-start(bf16[256,1024]{1,0:T(8,128)(2,1)} %get-tuple-element.61), channel_id=1, source_target_pairs={{1,0},{2,1},{3,2},{4,3},{5,4},{6,5},{7,6},{8,7},{9,8},{10,9},{11,1... | collective-permute-start | bytes 1572872 | tf_op jit(solution)/shard_map/ppermute | solution.py:374
  119.0 15.6 %collective-permute-start.9 = (bf16[256,1024]{1,0:T(8,128)(2,1)}, bf16[256,1024]{1,0:T(8,128)(2,1)}, u32[]{:S(2)}, u32[]{:S(2)}) collective-permute-start(bf16[256,1024]{1,0:T(8,128)(2,1)} %get-tuple-element.62), channel_id=1, source_target_pairs={{0,1},{1,2},{2,3},{3,4},{4,5},{5,6},{6,7},{7,8},{8,9},{9,10},{10,1... | collective-permute-start | bytes 1572872 | tf_op jit(solution)/shard_map/ppermute | solution.py:374
  128.9 17.2 %collective-permute-start.13 = (bf16[2,4,128,256]{3,2,1,0:T(8,128)(2,1)}, bf16[2,4,128,256]{3,2,1,0:T(8,128)(2,1)S(1)}, u32[]{:S(2)}, u32[]{:S(2)}) collective-permute-start(bf16[2,4,128,256]{3,2,1,0:T(8,128)(2,1)} %get-tuple-element.72), channel_id=1, source_target_pairs={{0,4},{4,8},{8,12},{12,0},{1,5},{5,9},{9,13},{13,1},{2,6},{6,10},{... | collective-permute-start | bytes 1572872 | tf_op jit(solution)/shard_map/ppermute | solution.py:364
  130.0 34.9 %collective-permute-start.14 = (bf16[2,4,128,256]{3,2,1,0:T(8,128)(2,1)}, bf16[2,4,128,256]{3,2,1,0:T(8,128)(2,1)}, u32[]{:S(2)}, u32[]{:S(2)}) collective-permute-start(bf16[2,4,128,256]{3,2,1,0:T(8,128)(2,1)} %get-tuple-element.73), channel_id=1, source_target_pairs={{0,8},{4,12},{8,0},{12,4},{1,9},{5,13},{9,1},{13,5},{2,10},{6,14},... | collective-permute-start | bytes 1572872 | tf_op jit(solution)/shard_map/ppermute | solution.py:364
  132.1 32.8 %collective-permute-start.15 = (bf16[2,4,128,256]{3,2,1,0:T(8,128)(2,1)}, bf16[2,4,128,256]{3,2,1,0:T(8,128)(2,1)}, u32[]{:S(2)}, u32[]{:S(2)}) collective-permute-start(bf16[2,4,128,256]{3,2,1,0:T(8,128)(2,1)} %get-tuple-element.74), channel_id=1, source_target_pairs={{0,12},{4,0},{8,4},{12,8},{1,13},{5,1},{9,5},{13,9},{2,14},{6,2},{... | collective-permute-start | bytes 1572872 | tf_op jit(solution)/shard_map/ppermute | solution.py:364
  134.1 35.9 %collective-permute-start.10 = (bf16[2,4,128,256]{3,2,1,0:T(8,128)(2,1)}, bf16[2,4,128,256]{3,2,1,0:T(8,128)(2,1)S(1)}, u32[]{:S(2)}, u32[]{:S(2)}) collective-permute-start(bf16[2,4,128,256]{3,2,1,0:T(8,128)(2,1)} %get-tuple-element.68), channel_id=1, source_target_pairs={{0,16},{16,32},{32,48},{48,0},{1,17},{17,33},{33,49},{49,1},{2,18}... | collective-permute-start | bytes 1572872 | tf_op jit(solution)/shard_map/ppermute | solution.py:364
  134.7 35.4 %collective-permute-start.11 = (bf16[2,4,128,256]{3,2,1,0:T(8,128)(2,1)}, bf16[2,4,128,256]{3,2,1,0:T(8,128)(2,1)}, u32[]{:S(2)}, u32[]{:S(2)}) collective-permute-start(bf16[2,4,128,256]{3,2,1,0:T(8,128)(2,1)} %get-tuple-element.69), channel_id=1, source_target_pairs={{0,32},{16,48},{32,0},{48,16},{1,33},{17,49},{33,1},{49,17},{2,34}... | collective-permute-start | bytes 1572872 | tf_op jit(solution)/shard_map/ppermute | solution.py:364
  146.1 27.4 %collective-permute-start.12 = (bf16[2,4,128,256]{3,2,1,0:T(8,128)(2,1)}, bf16[2,4,128,256]{3,2,1,0:T(8,128)(2,1)}, u32[]{:S(2)}, u32[]{:S(2)}) collective-permute-start(bf16[2,4,128,256]{3,2,1,0:T(8,128)(2,1)} %get-tuple-element.70), channel_id=1, source_target_pairs={{0,48},{16,0},{32,16},{48,32},{1,49},{17,1},{33,17},{49,33},{2,50}... | collective-permute-start | bytes 1572872 | tf_op jit(solution)/shard_map/ppermute | solution.py:364
  167.5 9.7 %collective-permute-start.16 = (bf16[2,2,2,8,1024]{4,3,2,1,0:T(8,128)(2,1)}, bf16[2,2,2,8,1024]{4,3,2,1,0:T(8,128)(2,1)S(1)}, u32[]{:S(2)}, u32[]{:S(2)}) collective-permute-start(bf16[2,2,2,8,1024]{4,3,2,1,0:T(8,128)(2,1)} %get-tuple-element.75), channel_id=1, source_target_pairs={{0,16},{16,32},{32,48},{48,0},{1,17},{17,33},{33,49},{49,1},{2,18}... | collective-permute-start | bytes 393224 | tf_op jit(solution)/shard_map/ppermute | solution.py:364
  177.1 49.1 %all-to-all-start.1 = ((bf16[128,8,1024]{2,1,0:T(8,128)(2,1)}), bf16[128,8,1024]{2,1,0:T(8,128)(2,1)S(1)}, u32[]{:S(2)}, u32[]{:S(2)}) async-start(bf16[128,8,1024]{2,1,0:T(8,128)(2,1)} %bitcast.35), calls=%async_computation.1 | async-start | bytes 4194304 | tf_op jit(solution)/shard_map/all_to_all | solution.py:434
  186.4 28.3 %collective-permute-start.20 = (bf16[2,2,2,8,1024]{4,3,2,1,0:T(8,128)(2,1)S(1)}, bf16[2,2,2,8,1024]{4,3,2,1,0:T(8,128)(2,1)S(1)}, u32[]{:S(2)}, u32[]{:S(2)}) collective-permute-start(bf16[2,2,2,8,1024]{4,3,2,1,0:T(8,128)(2,1)S(1)} %copy-done.23), channel_id=1, source_target_pairs={{0,32},{16,48},{32,0},{48,16},{1,33},{17,49},{33,1},{49,17},{2,34}... | collective-permute-start | bytes 393224 | tf_op jit(solution)/shard_map/ppermute | solution.py:364
  189.0 26.8 %collective-permute-start.21 = (bf16[2,2,2,8,1024]{4,3,2,1,0:T(8,128)(2,1)S(1)}, bf16[2,2,2,8,1024]{4,3,2,1,0:T(8,128)(2,1)S(1)}, u32[]{:S(2)}, u32[]{:S(2)}) collective-permute-start(bf16[2,2,2,8,1024]{4,3,2,1,0:T(8,128)(2,1)S(1)} %copy-done.22), channel_id=1, source_target_pairs={{0,48},{16,0},{32,16},{48,32},{1,49},{17,1},{33,17},{49,33},{2,50}... | collective-permute-start | bytes 393224 | tf_op jit(solution)/shard_map/ppermute | solution.py:364
  192.5 27.1 %collective-permute-start.17 = (bf16[2,2,2,8,1024]{4,3,2,1,0:T(8,128)(2,1)}, bf16[2,2,2,8,1024]{4,3,2,1,0:T(8,128)(2,1)S(1)}, u32[]{:S(2)}, u32[]{:S(2)}) collective-permute-start(bf16[2,2,2,8,1024]{4,3,2,1,0:T(8,128)(2,1)} %get-tuple-element.79), channel_id=1, source_target_pairs={{0,4},{4,8},{8,12},{12,0},{1,5},{5,9},{9,13},{13,1},{2,6},{6,10},{... | collective-permute-start | bytes 393224 | tf_op jit(solution)/shard_map/ppermute | solution.py:364
  194.2 25.4 %collective-permute-start.18 = (bf16[2,2,2,8,1024]{4,3,2,1,0:T(8,128)(2,1)}, bf16[2,2,2,8,1024]{4,3,2,1,0:T(8,128)(2,1)S(1)}, u32[]{:S(2)}, u32[]{:S(2)}) collective-permute-start(bf16[2,2,2,8,1024]{4,3,2,1,0:T(8,128)(2,1)} %get-tuple-element.80), channel_id=1, source_target_pairs={{0,8},{4,12},{8,0},{12,4},{1,9},{5,13},{9,1},{13,5},{2,10},{6,14},... | collective-permute-start | bytes 393224 | tf_op jit(solution)/shard_map/ppermute | solution.py:364
  197.4 22.2 %collective-permute-start.19 = (bf16[2,2,2,8,1024]{4,3,2,1,0:T(8,128)(2,1)}, bf16[2,2,2,8,1024]{4,3,2,1,0:T(8,128)(2,1)S(1)}, u32[]{:S(2)}, u32[]{:S(2)}) collective-permute-start(bf16[2,2,2,8,1024]{4,3,2,1,0:T(8,128)(2,1)} %get-tuple-element.81), channel_id=1, source_target_pairs={{0,12},{4,0},{8,4},{12,8},{1,13},{5,1},{9,5},{13,9},{2,14},{6,2},{... | collective-permute-start | bytes 393224 | tf_op jit(solution)/shard_map/ppermute | solution.py:364
  (27 other events, 406.0 us)

commit v3 on v2

--- a/solution.py
+++ b/solution.py
@@ -32,7 +32,7 @@
 
 
 def pick_rows(rows, table):
-    count, width, step = rows.shape[1], table.shape[1], 256
+    count, width, step = rows.shape[1], table.shape[1], 512
     return pl.pallas_call(
         pick_kernel,
         grid=(count // step,),
@@ -350,7 +350,7 @@
             jax.ShapeDtypeStruct((rows, width), BF16),
             jax.ShapeDtypeStruct((count, width), BF16),
         ),
-        compiler_params=params(60),
+        compiler_params=params(26),
         name="finish",
     )(own, *near, normed, inverse, gain, grad_out, slots, blend)
 

time: 230 us -> 229 us (level)
  Pallas kernels: 72.4 us -> 70 us
    pallas_call x1, Pallas kernels: 6.87 us -> 4.38 us  [finish(): pl.pallas_call(finish_kernel, out_shape=(jax.ShapeDtypeStruct((rows, widt...]
  transfers between devices with their start and end apart: 27 -> 27, of which waited for: 8 -> 8; matrix products, arithmetic and copies ran while one was open for 2% -> 2% of each run, Pallas kernels for 12% -> 11%
where the time goes in v3:
time: 229 us; the launch traced here: 228 us
  starting transfers between devices  81.9 us (36%)
  Pallas kernels  70 us (31%)
  waiting for transfers between devices  65.4 us (29%)
  local copies, waits for them, and re-layouts  4.03 us (2%)
  matrix products  3.1 us (1%)
  other arithmetic  2.44 us (1%)
    ppermute x17, starting transfers between devices, shifted(): lax.ppermute(block, axis, [(i, (i + step) % count) for i in range(count)])  45.9 us
    pallas_call x1, Pallas kernels, attend(): pl.pallas_call(attend_kernel, grid=(steps,), in_specs=[flags(), flags()]...  39 us
    all_to_all x1, waiting for transfers between devices, body(): lax.all_to_all(outgoing, TY + TX, split_axis=0, concat_axis=0, tiled=True)  28.9 us
    ppermute x17, waiting for transfers between devices, shifted(): lax.ppermute(block, axis, [(i, (i + step) % count) for i in range(count)])  28.6 us
    ppermute x8, starting transfers between devices, passed_along(): return lax.ppermute(block, axis, route)  16.7 us
    all_to_all x1, starting transfers between devices, body(): lax.all_to_all(outgoing, TY + TX, split_axis=0, concat_axis=0, tiled=True)  11.1 us
    all_to_all x1, starting transfers between devices, body(): lax.all_to_all(sent, TY + TX, split_axis=0, concat_axis=0, tiled=True)  8.12 us
    ppermute x8, waiting for transfers between devices, passed_along(): return lax.ppermute(block, axis, route)  7.84 us
  transfers between devices with their start and end apart: 27, of which 8 were waited for; matrix products, arithmetic and copies ran while one was open for 2% of the time, Pallas kernels for 11%

profile of v3, /device:TPU:0, one launch (start us, length us, event | category | flops | bytes accessed | tf_op | source)
XLA Modules:
  0.0 227.8 jit_solution(11619270422011249081)
XLA Ops:
  0.6 3.7 %pick_rows.1 = bf16[1024,1024]{1,0:T(8,128)(2,1)} custom-call(s32[1,1024]{1,0:T(1,128)} %rows_ref.3, bf16[512,1024]{1,0:T(8,128)(2,1)} %table_ref.1), custom_call_target="tpu_custom_call" | custom-call | tf_op jit(solution)/shard_map/pick_rows/pallas_call | solution.py:36
  4.4 11.1 %all-to-all-start = ((bf16[128,8,1024]{2,1,0:T(8,128)(2,1)}), bf16[128,8,1024]{2,1,0:T(8,128)(2,1)S(1)}, u32[]{:S(2)}, u32[]{:S(2)}) async-start(bf16[128,8,1024]{2,1,0:T(8,128)(2,1)} %bitcast.35), calls=%async_computation | async-start | bytes 4194304 | tf_op jit(solution)/shard_map/all_to_all | solution.py:401
  17.0 28.9 %all-to-all-done = bf16[128,8,1024]{2,1,0:T(8,128)(2,1)S(1)} async-done(((bf16[128,8,1024]{2,1,0:T(8,128)(2,1)}), bf16[128,8,1024]{2,1,0:T(8,128)(2,1)S(1)}, u32[]{:S(2)}, u32[]{:S(2)}) %all-to-all-start) | async-done | bytes 2097184 | tf_op jit(solution)/shard_map/all_to_all | solution.py:401
  47.0 2.8 %blend_norm.1 = (bf16[256,1024]{1,0:T(8,128)(2,1)}, f32[256,1024]{1,0:T(8,128)S(1)}, f32[256,128]{1,0:T(8,128)S(1)}) custom-call(s32[256,4]{1,0:T(8,128)S(1)} %reshape.30.slots_ref, f32[256,4]{1,0:T(8,128)S(1)} %bitcast.32, bf16[1024,1024]{1,0:T(8,128)(2,1)S(1)} %bitcast.27, bf16[256,1024]{1,0:T(8,128)(2,1)S(1)} %bitcast.34, ...), custom_call_target="tpu_custom_call" | custom-call | tf_op jit(solution)/shard_map/blend_norm/pallas_call | solution.py:96
  55.5 7.0 %project.1 = (bf16[256,1024]{1,0:T(8,128)(2,1)}, bf16[256,1024]{1,0:T(8,128)(2,1)}, bf16[256,1024]{1,0:T(8,128)(2,1)}, bf16[256,1024]{1,0:T(8,128)(2,1)}) custom-call(bf16[256,1024]{1,0:T(8,128)(2,1)} %get-tuple-element.45.in_ref.own_ref, bf16[256,1024]{1,0:T(8,128)(2,1)} %bitcast.28, bf16[1024,1024]{1,0:T(8,128)(2,1)} %wq_ref.3, bf16[1024,1024]{1,0:T(8,128)(2,1)} %wk_ref.3, ...), custom_call_target="tpu_custom_call" | custom-call | flops 2100000000 | bytes 11000000 | tf_op jit(solution)/shard_map/project/pallas_call | solution.py:121
  62.5 3.2 %collective-permute-done.2.up_ref = bf16[256,1024]{1,0:T(8,128)(2,1)S(1)} collective-permute-done((bf16[256,1024]{1,0:T(8,128)(2,1)}, bf16[256,1024]{1,0:T(8,128)(2,1)S(1)}, u32[]{:S(2)}, u32[]{:S(2)}) %collective-permute-start.2) | collective-permute-done | bytes 524320 | tf_op jit(solution)/shard_map/ppermute | solution.py:374
  65.7 4.6 %collective-permute-done.3.down_ref = bf16[256,1024]{1,0:T(8,128)(2,1)S(1)} collective-permute-done((bf16[256,1024]{1,0:T(8,128)(2,1)}, bf16[256,1024]{1,0:T(8,128)(2,1)S(1)}, u32[]{:S(2)}, u32[]{:S(2)}) %collective-permute-start.3) | collective-permute-done | bytes 524320 | tf_op jit(solution)/shard_map/ppermute | solution.py:374
  71.2 39.0 %attend.1 = (bf16[4,2,4,128,256]{4,3,2,1,0:T(8,128)(2,1)}, bf16[4,2,4,128,256]{4,3,2,1,0:T(8,128)(2,1)}, bf16[4,2,4,128,256]{4,3,2,1,0:T(8,128)(2,1)}, bf16[4,2,...) custom-call(s32[1]{0:T(128)} %bitcast.1.core_ref, ...), custom_call_target="tpu_custom_call" | custom-call | flops 33999998976 | bytes 32000000 | tf_op jit(solution)/shard_map/attend/pallas_call | solution.py:230
  112.1 4.6 %collective-permute-start.7 = (bf16[256,1024]{1,0:T(8,128)(2,1)}, bf16[256,1024]{1,0:T(8,128)(2,1)S(1)}, u32[]{:S(2)}, u32[]{:S(2)}) collective-permute-start(bf16[256,1024]{1,0:T(8,128)(2,1)} %get-tuple-element.60), channel_id=1, source_target_pairs={{0,16},{16,32},{32,48},{48,64},{64,80},{80,96},{96,112},{1,17},{17... | collective-permute-start | bytes 1572872 | tf_op jit(solution)/shard_map/ppermute | solution.py:374
  118.0 3.8 %collective-permute-start.9 = (bf16[256,1024]{1,0:T(8,128)(2,1)}, bf16[256,1024]{1,0:T(8,128)(2,1)}, u32[]{:S(2)}, u32[]{:S(2)}) collective-permute-start(bf16[256,1024]{1,0:T(8,128)(2,1)} %get-tuple-element.62), channel_id=1, source_target_pairs={{0,1},{1,2},{2,3},{3,4},{4,5},{5,6},{6,7},{7,8},{8,9},{9,10},{10,1... | collective-permute-start | bytes 1572872 | tf_op jit(solution)/shard_map/ppermute | solution.py:374
  121.8 6.1 %split_sum.1 = (bf16[2,4,128,256]{3,2,1,0:T(8,128)(2,1)}, bf16[2,4,128,256]{3,2,1,0:T(8,128)(2,1)}, bf16[2,4,128,256]{3,2,1,0:T(8,128)(2,1)}, bf16[2,4,128,256]{...) custom-call(s32[1]{0:T(128)} %bitcast.7.refs_0_.here_ref, ...), custom_call_target="tpu_custom_call" | custom-call | flops 1000000 | bytes 12000000 | tf_op jit(solution)/shard_map/split_sum/pallas_call | solution.py:266
  134.4 11.4 %collective-permute-start.11 = (bf16[2,4,128,256]{3,2,1,0:T(8,128)(2,1)}, bf16[2,4,128,256]{3,2,1,0:T(8,128)(2,1)}, u32[]{:S(2)}, u32[]{:S(2)}) collective-permute-start(bf16[2,4,128,256]{3,2,1,0:T(8,128)(2,1)} %get-tuple-element.69), channel_id=1, source_target_pairs={{0,32},{16,48},{32,0},{48,16},{1,33},{17,49},{33,1},{49,17},{2,34}... | collective-permute-start | bytes 1572872 | tf_op jit(solution)/shard_map/ppermute | solution.py:364
  145.8 12.0 %collective-permute-start.12 = (bf16[2,4,128,256]{3,2,1,0:T(8,128)(2,1)}, bf16[2,4,128,256]{3,2,1,0:T(8,128)(2,1)}, u32[]{:S(2)}, u32[]{:S(2)}) collective-permute-start(bf16[2,4,128,256]{3,2,1,0:T(8,128)(2,1)} %get-tuple-element.70), channel_id=1, source_target_pairs={{0,48},{16,0},{32,16},{48,32},{1,49},{17,1},{33,17},{49,33},{2,50}... | collective-permute-start | bytes 1572872 | tf_op jit(solution)/shard_map/ppermute | solution.py:364
  157.8 4.4 %finish.1 = (bf16[256,1024]{1,0:T(8,128)(2,1)}, bf16[1024,1024]{1,0:T(8,128)(2,1)S(1)}) custom-call(f32[256,1024]{1,0:T(8,128)S(1)} %copy-done.2, bf16[256,1024]{1,0:T(8,128)(2,1)S(1)} %collective-permute-done.6.up_ref, bf16[256,1024]{1,0:T(8,128)(2,1)S(1)} %collective-permute-done.7.down_ref, bf16[256,1024]{1,0:T(8,128)(2,1)} %collective-permute-done.8.left_ref, ...), custom_call_target="tpu_custom_call" | custom-call | tf_op jit(solution)/shard_map/finish/pallas_call | solution.py:347
  163.6 2.5 %join_sum.2 = (bf16[2,2,2,8,1024]{4,3,2,1,0:T(8,128)(2,1)}, bf16[2,2,2,8,1024]{4,3,2,1,0:T(8,128)(2,1)}, bf16[2,2,2,8,1024]{4,3,2,1,0:T(8,128)(2,1)}, bf16[2,2,2,8,1024]{4,3,2,1,0:T(8,128)(2,1)}) custom-call(s32[1]{0:T(128)} %bitcast.7.refs_0_.here_ref, bf16[2,4,128,256]{3,2,1,0:T(8,128)(2,1)} %get-tuple-element.56.refs_0_, ...), custom_call_target="tpu_custom_call" | custom-call | flops 1000000 | bytes 6000000 | tf_op jit(solution)/shard_map/join_sum/pallas_call | solution.py:317
  166.1 3.1 %fusion = bf16[256,1024]{1,0:T(8,128)(2,1)} fusion(bf16[256,1024]{1,0:T(8,128)(2,1)S(1)} %copy-done.17, bf16[1024,1024]{1,0:T(8,128)(2,1)} %wo_ref.1, bf16[1,1,256,1024]{3,2,1,0:T(8,128)(2,1)S(1)} %copy-done.4), kind=kOutput, calls=%fused_computation.1 | convolution fusion | flops 537657344 | bytes 3670016 | tf_op jit(solution)/shard_map/dot_general | solution.py:429
  169.2 3.8 %collective-permute-done.12.refs_3_ = bf16[2,4,128,256]{3,2,1,0:T(8,128)(2,1)} collective-permute-done((bf16[2,4,128,256]{3,2,1,0:T(8,128)(2,1)}, bf16[2,4,128,256]{3,2,1,0:T(8,128)(2,1)}, u32[]{:S(2)}, u32[]{:S(2)}) %collective-permute-start.12) | collective-permute-done | bytes 524320 | tf_op jit(solution)/shard_map/ppermute | solution.py:364
  173.0 3.9 %collective-permute-done.16 = bf16[2,2,2,8,1024]{4,3,2,1,0:T(8,128)(2,1)S(1)} collective-permute-done((bf16[2,2,2,8,1024]{4,3,2,1,0:T(8,128)(2,1)}, bf16[2,2,2,8,1024]{4,3,2,1,0:T(8,128)(2,1)S(1)}, u32[]{:S(2)}, u32[]{:S(2)}) %collective-permute-start.16) | collective-permute-done | bytes 131104 | tf_op jit(solution)/shard_map/ppermute | solution.py:364
  176.9 8.1 %all-to-all-start.1 = ((bf16[128,8,1024]{2,1,0:T(8,128)(2,1)}), bf16[128,8,1024]{2,1,0:T(8,128)(2,1)S(1)}, u32[]{:S(2)}, u32[]{:S(2)}) async-start(bf16[128,8,1024]{2,1,0:T(8,128)(2,1)} %bitcast.31), calls=%async_computation.1 | async-start | bytes 4194304 | tf_op jit(solution)/shard_map/all_to_all | solution.py:434
  185.1 2.5 %collective-permute-start.20 = (bf16[2,2,2,8,1024]{4,3,2,1,0:T(8,128)(2,1)S(1)}, bf16[2,2,2,8,1024]{4,3,2,1,0:T(8,128)(2,1)S(1)}, u32[]{:S(2)}, u32[]{:S(2)}) collective-permute-start(bf16[2,2,2,8,1024]{4,3,2,1,0:T(8,128)(2,1)S(1)} %copy-done.16), channel_id=1, source_target_pairs={{0,32},{16,48},{32,0},{48,16},{1,33},{17,49},{33,1},{49,17},{2,34}... | collective-permute-start | bytes 393224 | tf_op jit(solution)/shard_map/ppermute | solution.py:364
  192.8 3.2 %collective-permute-start.18 = (bf16[2,2,2,8,1024]{4,3,2,1,0:T(8,128)(2,1)}, bf16[2,2,2,8,1024]{4,3,2,1,0:T(8,128)(2,1)S(1)}, u32[]{:S(2)}, u32[]{:S(2)}) collective-permute-start(bf16[2,2,2,8,1024]{4,3,2,1,0:T(8,128)(2,1)} %get-tuple-element.80), channel_id=1, source_target_pairs={{0,8},{4,12},{8,0},{12,4},{1,9},{5,13},{9,1},{13,5},{2,10},{6,14},... | collective-permute-start | bytes 393224 | tf_op jit(solution)/shard_map/ppermute | solution.py:364
  197.2 16.1 %collective-permute-done.20 = bf16[2,2,2,8,1024]{4,3,2,1,0:T(8,128)(2,1)S(1)} collective-permute-done((bf16[2,2,2,8,1024]{4,3,2,1,0:T(8,128)(2,1)S(1)}, bf16[2,2,2,8,1024]{4,3,2,1,0:T(8,128)(2,1)S(1)}, u32[]{:S(2)}, u32[]{:S(2)}) %collective-permute-start.20) | collective-permute-done | bytes 131104 | tf_op jit(solution)/shard_map/ppermute | solution.py:364
  214.5 3.7 %collective-permute-done.17 = bf16[2,2,2,8,1024]{4,3,2,1,0:T(8,128)(2,1)S(1)} collective-permute-done((bf16[2,2,2,8,1024]{4,3,2,1,0:T(8,128)(2,1)}, bf16[2,2,2,8,1024]{4,3,2,1,0:T(8,128)(2,1)S(1)}, u32[]{:S(2)}, u32[]{:S(2)}) %collective-permute-start.17) | collective-permute-done | bytes 131104 | tf_op jit(solution)/shard_map/ppermute | solution.py:364
  219.9 2.7 %collective-permute-start.23 = (bf16[4,8,1024]{2,1,0:T(8,128)(2,1)S(1)}, bf16[4,8,1024]{2,1,0:T(8,128)(2,1)S(1)}, u32[]{:S(2)}, u32[]{:S(2)}) collective-permute-start(bf16[4,8,1024]{2,1,0:T(8,128)(2,1)S(1)} %get-tuple-element.88), channel_id=1, source_target_pairs={{0,64},{2,66},{64,0},{66,2},{1,65},{3,67},{65,1},{67,3},{4,68},{6,... | collective-permute-start | bytes 196616 | tf_op jit(solution)/shard_map/ppermute | solution.py:364
  (85 shorter events, 34.6 us)
Async XLA Ops:
  4.4 41.6 %all-to-all-start = ((bf16[128,8,1024]{2,1,0:T(8,128)(2,1)}), bf16[128,8,1024]{2,1,0:T(8,128)(2,1)S(1)}, u32[]{:S(2)}, u32[]{:S(2)}) async-start(bf16[128,8,1024]{2,1,0:T(8,128)(2,1)} %bitcast.35), calls=%async_computation | async-start | bytes 4194304 | tf_op jit(solution)/shard_map/all_to_all | solution.py:401
  49.8 12.7 %collective-permute-start = (bf16[256,1024]{1,0:T(8,128)(2,1)}, bf16[256,1024]{1,0:T(8,128)(2,1)S(1)}, u32[]{:S(2)}, u32[]{:S(2)}) collective-permute-start(bf16[256,1024]{1,0:T(8,128)(2,1)} %get-tuple-element.45.in_ref.own_ref), channel_id=1, source_target_pairs={{0,1},{1,2},{2,3},{3,4},{4,5},{5,6},{6,7},{7,8},{8,9},{9,10},{10,1... | collective-permute-start | bytes 1572872 | tf_op jit(solution)/shard_map/ppermute | solution.py:374
  51.1 11.4 %collective-permute-start.1 = (bf16[256,1024]{1,0:T(8,128)(2,1)}, bf16[256,1024]{1,0:T(8,128)(2,1)S(1)}, u32[]{:S(2)}, u32[]{:S(2)}) collective-permute-start(bf16[256,1024]{1,0:T(8,128)(2,1)} %get-tuple-element.45.in_ref.own_ref), channel_id=1, source_target_pairs={{1,0},{2,1},{3,2},{4,3},{5,4},{6,5},{7,6},{8,7},{9,8},{10,9},{11,1... | collective-permute-start | bytes 1572872 | tf_op jit(solution)/shard_map/ppermute | solution.py:374
  52.4 13.3 %collective-permute-start.2 = (bf16[256,1024]{1,0:T(8,128)(2,1)}, bf16[256,1024]{1,0:T(8,128)(2,1)S(1)}, u32[]{:S(2)}, u32[]{:S(2)}) collective-permute-start(bf16[256,1024]{1,0:T(8,128)(2,1)} %get-tuple-element.45.in_ref.own_ref), channel_id=1, source_target_pairs={{0,16},{16,32},{32,48},{48,64},{64,80},{80,96},{96,112},{1,17},{17... | collective-permute-start | bytes 1572872 | tf_op jit(solution)/shard_map/ppermute | solution.py:374
  54.0 16.3 %collective-permute-start.3 = (bf16[256,1024]{1,0:T(8,128)(2,1)}, bf16[256,1024]{1,0:T(8,128)(2,1)S(1)}, u32[]{:S(2)}, u32[]{:S(2)}) collective-permute-start(bf16[256,1024]{1,0:T(8,128)(2,1)} %get-tuple-element.45.in_ref.own_ref), channel_id=1, source_target_pairs={{16,0},{32,16},{48,32},{64,48},{80,64},{96,80},{112,96},{17,1},{33... | collective-permute-start | bytes 1572872 | tf_op jit(solution)/shard_map/ppermute | solution.py:374
  110.7 11.2 %collective-permute-start.5 = (bf16[4,2,4,128,256]{4,3,2,1,0:T(8,128)(2,1)}, bf16[4,2,4,128,256]{4,3,2,1,0:T(8,128)(2,1)}, u32[]{:S(2)}, u32[]{:S(2)}) collective-permute-start(bf16[4,2,4,128,256]{4,3,2,1,0:T(8,128)(2,1)} %get-tuple-element.55), channel_id=1, source_target_pairs={{0,1},{1,0},{2,3},{3,2},{4,5},{5,4},{6,7},{7,6},{8,9},{9,8},{10,11... | collective-permute-start | bytes 6291464 | tf_op jit(solution)/shard_map/ppermute | solution.py:364
  110.8 18.3 %collective-permute-start.6 = (bf16[256,1024]{1,0:T(8,128)(2,1)}, bf16[256,1024]{1,0:T(8,128)(2,1)S(1)}, u32[]{:S(2)}, u32[]{:S(2)}) collective-permute-start(bf16[256,1024]{1,0:T(8,128)(2,1)} %get-tuple-element.59), channel_id=1, source_target_pairs={{16,0},{32,16},{48,32},{64,48},{80,64},{96,80},{112,96},{17,1},{33... | collective-permute-start | bytes 1572872 | tf_op jit(solution)/shard_map/ppermute | solution.py:374
  112.1 19.1 %collective-permute-start.7 = (bf16[256,1024]{1,0:T(8,128)(2,1)}, bf16[256,1024]{1,0:T(8,128)(2,1)S(1)}, u32[]{:S(2)}, u32[]{:S(2)}) collective-permute-start(bf16[256,1024]{1,0:T(8,128)(2,1)} %get-tuple-element.60), channel_id=1, source_target_pairs={{0,16},{16,32},{32,48},{48,64},{64,80},{80,96},{96,112},{1,17},{17... | collective-permute-start | bytes 1572872 | tf_op jit(solution)/shard_map/ppermute | solution.py:374
  116.7 16.5 %collective-permute-start.8 = (bf16[256,1024]{1,0:T(8,128)(2,1)}, bf16[256,1024]{1,0:T(8,128)(2,1)}, u32[]{:S(2)}, u32[]{:S(2)}) collective-permute-start(bf16[256,1024]{1,0:T(8,128)(2,1)} %get-tuple-element.61), channel_id=1, source_target_pairs={{1,0},{2,1},{3,2},{4,3},{5,4},{6,5},{7,6},{8,7},{9,8},{10,9},{11,1... | collective-permute-start | bytes 1572872 | tf_op jit(solution)/shard_map/ppermute | solution.py:374
  118.0 16.4 %collective-permute-start.9 = (bf16[256,1024]{1,0:T(8,128)(2,1)}, bf16[256,1024]{1,0:T(8,128)(2,1)}, u32[]{:S(2)}, u32[]{:S(2)}) collective-permute-start(bf16[256,1024]{1,0:T(8,128)(2,1)} %get-tuple-element.62), channel_id=1, source_target_pairs={{0,1},{1,2},{2,3},{3,4},{4,5},{5,6},{6,7},{7,8},{8,9},{9,10},{10,1... | collective-permute-start | bytes 1572872 | tf_op jit(solution)/shard_map/ppermute | solution.py:374
  127.9 17.9 %collective-permute-start.13 = (bf16[2,4,128,256]{3,2,1,0:T(8,128)(2,1)}, bf16[2,4,128,256]{3,2,1,0:T(8,128)(2,1)S(1)}, u32[]{:S(2)}, u32[]{:S(2)}) collective-permute-start(bf16[2,4,128,256]{3,2,1,0:T(8,128)(2,1)} %get-tuple-element.72), channel_id=1, source_target_pairs={{0,4},{4,8},{8,12},{12,0},{1,5},{5,9},{9,13},{13,1},{2,6},{6,10},{... | collective-permute-start | bytes 1572872 | tf_op jit(solution)/shard_map/ppermute | solution.py:364
  129.1 34.5 %collective-permute-start.14 = (bf16[2,4,128,256]{3,2,1,0:T(8,128)(2,1)}, bf16[2,4,128,256]{3,2,1,0:T(8,128)(2,1)}, u32[]{:S(2)}, u32[]{:S(2)}) collective-permute-start(bf16[2,4,128,256]{3,2,1,0:T(8,128)(2,1)} %get-tuple-element.73), channel_id=1, source_target_pairs={{0,8},{4,12},{8,0},{12,4},{1,9},{5,13},{9,1},{13,5},{2,10},{6,14},... | collective-permute-start | bytes 1572872 | tf_op jit(solution)/shard_map/ppermute | solution.py:364
  131.2 32.4 %collective-permute-start.15 = (bf16[2,4,128,256]{3,2,1,0:T(8,128)(2,1)}, bf16[2,4,128,256]{3,2,1,0:T(8,128)(2,1)}, u32[]{:S(2)}, u32[]{:S(2)}) collective-permute-start(bf16[2,4,128,256]{3,2,1,0:T(8,128)(2,1)} %get-tuple-element.74), channel_id=1, source_target_pairs={{0,12},{4,0},{8,4},{12,8},{1,13},{5,1},{9,5},{13,9},{2,14},{6,2},{... | collective-permute-start | bytes 1572872 | tf_op jit(solution)/shard_map/ppermute | solution.py:364
  133.2 36.0 %collective-permute-start.10 = (bf16[2,4,128,256]{3,2,1,0:T(8,128)(2,1)}, bf16[2,4,128,256]{3,2,1,0:T(8,128)(2,1)}, u32[]{:S(2)}, u32[]{:S(2)}) collective-permute-start(bf16[2,4,128,256]{3,2,1,0:T(8,128)(2,1)} %get-tuple-element.68), channel_id=1, source_target_pairs={{0,16},{16,32},{32,48},{48,0},{1,17},{17,33},{33,49},{49,1},{2,18}... | collective-permute-start | bytes 1572872 | tf_op jit(solution)/shard_map/ppermute | solution.py:364
  134.4 34.8 %collective-permute-start.11 = (bf16[2,4,128,256]{3,2,1,0:T(8,128)(2,1)}, bf16[2,4,128,256]{3,2,1,0:T(8,128)(2,1)}, u32[]{:S(2)}, u32[]{:S(2)}) collective-permute-start(bf16[2,4,128,256]{3,2,1,0:T(8,128)(2,1)} %get-tuple-element.69), channel_id=1, source_target_pairs={{0,32},{16,48},{32,0},{48,16},{1,33},{17,49},{33,1},{49,17},{2,34}... | collective-permute-start | bytes 1572872 | tf_op jit(solution)/shard_map/ppermute | solution.py:364
  145.8 27.2 %collective-permute-start.12 = (bf16[2,4,128,256]{3,2,1,0:T(8,128)(2,1)}, bf16[2,4,128,256]{3,2,1,0:T(8,128)(2,1)}, u32[]{:S(2)}, u32[]{:S(2)}) collective-permute-start(bf16[2,4,128,256]{3,2,1,0:T(8,128)(2,1)} %get-tuple-element.70), channel_id=1, source_target_pairs={{0,48},{16,0},{32,16},{48,32},{1,49},{17,1},{33,17},{49,33},{2,50}... | collective-permute-start | bytes 1572872 | tf_op jit(solution)/shard_map/ppermute | solution.py:364
  166.0 10.9 %collective-permute-start.16 = (bf16[2,2,2,8,1024]{4,3,2,1,0:T(8,128)(2,1)}, bf16[2,2,2,8,1024]{4,3,2,1,0:T(8,128)(2,1)S(1)}, u32[]{:S(2)}, u32[]{:S(2)}) collective-permute-start(bf16[2,2,2,8,1024]{4,3,2,1,0:T(8,128)(2,1)} %get-tuple-element.75), channel_id=1, source_target_pairs={{0,16},{16,32},{32,48},{48,0},{1,17},{17,33},{33,49},{49,1},{2,18}... | collective-permute-start | bytes 393224 | tf_op jit(solution)/shard_map/ppermute | solution.py:364
  176.9 48.0 %all-to-all-start.1 = ((bf16[128,8,1024]{2,1,0:T(8,128)(2,1)}), bf16[128,8,1024]{2,1,0:T(8,128)(2,1)S(1)}, u32[]{:S(2)}, u32[]{:S(2)}) async-start(bf16[128,8,1024]{2,1,0:T(8,128)(2,1)} %bitcast.31), calls=%async_computation.1 | async-start | bytes 4194304 | tf_op jit(solution)/shard_map/all_to_all | solution.py:434
  185.1 28.3 %collective-permute-start.20 = (bf16[2,2,2,8,1024]{4,3,2,1,0:T(8,128)(2,1)S(1)}, bf16[2,2,2,8,1024]{4,3,2,1,0:T(8,128)(2,1)S(1)}, u32[]{:S(2)}, u32[]{:S(2)}) collective-permute-start(bf16[2,2,2,8,1024]{4,3,2,1,0:T(8,128)(2,1)S(1)} %copy-done.16), channel_id=1, source_target_pairs={{0,32},{16,48},{32,0},{48,16},{1,33},{17,49},{33,1},{49,17},{2,34}... | collective-permute-start | bytes 393224 | tf_op jit(solution)/shard_map/ppermute | solution.py:364
  187.6 26.8 %collective-permute-start.21 = (bf16[2,2,2,8,1024]{4,3,2,1,0:T(8,128)(2,1)S(1)}, bf16[2,2,2,8,1024]{4,3,2,1,0:T(8,128)(2,1)S(1)}, u32[]{:S(2)}, u32[]{:S(2)}) collective-permute-start(bf16[2,2,2,8,1024]{4,3,2,1,0:T(8,128)(2,1)S(1)} %copy-done.15), channel_id=1, source_target_pairs={{0,48},{16,0},{32,16},{48,32},{1,49},{17,1},{33,17},{49,33},{2,50}... | collective-permute-start | bytes 393224 | tf_op jit(solution)/shard_map/ppermute | solution.py:364
  191.1 27.1 %collective-permute-start.17 = (bf16[2,2,2,8,1024]{4,3,2,1,0:T(8,128)(2,1)}, bf16[2,2,2,8,1024]{4,3,2,1,0:T(8,128)(2,1)S(1)}, u32[]{:S(2)}, u32[]{:S(2)}) collective-permute-start(bf16[2,2,2,8,1024]{4,3,2,1,0:T(8,128)(2,1)} %get-tuple-element.79), channel_id=1, source_target_pairs={{0,4},{4,8},{8,12},{12,0},{1,5},{5,9},{9,13},{13,1},{2,6},{6,10},{... | collective-permute-start | bytes 393224 | tf_op jit(solution)/shard_map/ppermute | solution.py:364
  192.8 25.4 %collective-permute-start.18 = (bf16[2,2,2,8,1024]{4,3,2,1,0:T(8,128)(2,1)}, bf16[2,2,2,8,1024]{4,3,2,1,0:T(8,128)(2,1)S(1)}, u32[]{:S(2)}, u32[]{:S(2)}) collective-permute-start(bf16[2,2,2,8,1024]{4,3,2,1,0:T(8,128)(2,1)} %get-tuple-element.80), channel_id=1, source_target_pairs={{0,8},{4,12},{8,0},{12,4},{1,9},{5,13},{9,1},{13,5},{2,10},{6,14},... | collective-permute-start | bytes 393224 | tf_op jit(solution)/shard_map/ppermute | solution.py:364
  196.0 22.2 %collective-permute-start.19 = (bf16[2,2,2,8,1024]{4,3,2,1,0:T(8,128)(2,1)}, bf16[2,2,2,8,1024]{4,3,2,1,0:T(8,128)(2,1)S(1)}, u32[]{:S(2)}, u32[]{:S(2)}) collective-permute-start(bf16[2,2,2,8,1024]{4,3,2,1,0:T(8,128)(2,1)} %get-tuple-element.81), channel_id=1, source_target_pairs={{0,12},{4,0},{8,4},{12,8},{1,13},{5,1},{9,5},{13,9},{2,14},{6,2},{... | collective-permute-start | bytes 393224 | tf_op jit(solution)/shard_map/ppermute | solution.py:364
  219.3 7.8 %collective-permute-start.22 = (bf16[4,8,1024]{2,1,0:T(8,128)(2,1)S(1)}, bf16[4,8,1024]{2,1,0:T(8,128)(2,1)S(1)}, u32[]{:S(2)}, u32[]{:S(2)}) collective-permute-start(bf16[4,8,1024]{2,1,0:T(8,128)(2,1)S(1)} %get-tuple-element.87), channel_id=1, source_target_pairs={{0,2},{2,64},{64,66},{66,0},{1,3},{3,65},{65,67},{67,1},{4,6},{6,6... | collective-permute-start | bytes 196616 | tf_op jit(solution)/shard_map/ppermute | solution.py:364
  (21 other events, 256.9 us)

commit v4 on v3

--- a/solution.py
+++ b/solution.py
@@ -130,9 +130,33 @@
     )(normed_in, grad_out, w_query, w_key, w_value, w_out)
 
 
+def sides_kernel(left_ref, right_ref, wk_ref, wv_ref, key_ref, value_ref):
+    rows = left_ref.shape[0]
+    for at, ref in ((0, left_ref), (rows, right_ref)):
+        key_ref[at : at + rows] = mm(ref[...], wk_ref[...]).astype(BF16)
+        value_ref[at : at + rows] = mm(ref[...], wv_ref[...]).astype(BF16)
+
+
+def sides(left, right, w_key, w_value):
+    rows, width = left.shape
+    lanes = 2 * HEAD_SIZE
+    whole = lambda: pl.BlockSpec((rows, width), lambda h: (0, 0), pipeline_mode=pl.Buffered(1))
+    columns = lambda n: pl.BlockSpec((n, lanes), lambda h: (0, h))
+    return pl.pallas_call(
+        sides_kernel,
+        grid=(width // lanes,),
+        in_specs=[whole(), whole(), columns(width), columns(width)],
+        out_specs=[columns(2 * rows)] * 2,
+        out_shape=(jax.ShapeDtypeStruct((2 * rows, width), BF16),) * 2,
+        compiler_params=params(60),
+        cost_estimate=pl.CostEstimate(flops=21 * 10**8, bytes_accessed=8 * 10**6, transcendentals=0),
+        name="sides",
+    )(left, right, w_key, w_value)
+
+
 def attend_kernel(
     core_ref, mask_ref, own_ref, left_ref, right_ref, up_ref, down_ref, grad_ref,
-    query_ref, own_key_ref, own_value_ref, g_ref, wq_ref, wk_ref, wv_ref,
+    query_ref, own_key_ref, own_value_ref, g_ref, side_key_ref, side_value_ref, wq_ref, wk_ref, wv_ref,
     keep_y, send_y, keep_z, send_z, attended_ref, up_grad, down_grad, left_grad, right_grad, own_grad, x_all, x_turned, grads,
 ):
     step = pl.program_id(0)
@@ -152,9 +176,9 @@
     width = grad_out.shape[1]
     scale = HEAD_SIZE ** (-0.5)
     query, g = query_ref[...], g_ref[...]
-    near = x_all[rows:]
-    key = jnp.concatenate([own_key_ref[...], mm(near, wk_ref[...]).astype(BF16)], axis=0)
-    value = jnp.concatenate([own_value_ref[...], mm(near, wv_ref[...]).astype(BF16)], axis=0)
+    near = x_all[rows : 3 * rows]
+    key = jnp.concatenate([own_key_ref[...], mm(near, wk_ref[...]).astype(BF16), side_key_ref[...]], axis=0)
+    value = jnp.concatenate([own_value_ref[...], mm(near, wv_ref[...]).astype(BF16), side_value_ref[...]], axis=0)
     query_t, g_t = query.T, g.T
     attended_t, dquery_t, dkey, dvalue = [], [], [], []
     for h in range(lanes // HEAD_SIZE):
@@ -233,6 +257,7 @@
         in_specs=[flags(), flags()]
         + [whole() for _ in range(near + 1)]
         + [out(rows)] * 4
+        + [out(2 * rows)] * 2
         + [columns()] * 3,
         out_specs=[parts(ys), parts(ys), parts(zs), parts(zs), out(rows)]
         + [whole() for _ in range(near)],
@@ -409,6 +434,7 @@
         passed_along(normed_in, TX, -1),
     )
     projected = project(normed_in, grad_out, w_query, w_key, w_value, w_out)
+    projected += sides(tiles[3], tiles[4], w_key, w_value)
     here = {axis: lax.axis_index(axis).reshape(1) for axis in ("z", "y", "core", "x_hi", "x_lo")}
     chunk = width // devices
     ys, zs = lax.axis_size("y"), lax.axis_size("z")

time: 229 us -> 227 us (level)
  waiting for transfers between devices: 65.4 us -> 57.8 us
  Pallas kernels: 70 us -> 74 us
    ppermute x8, waiting for transfers between devices: 7.84 us -> 0.24 us  [passed_along(): return lax.ppermute(block, axis, route)]
    pallas_call x0 -> x1, Pallas kernels: none -> 6 us  [sides(): pl.pallas_call(sides_kernel, grid=(width // lanes,), in_specs=[whole(), w...]
  transfers between devices with their start and end apart: 27 -> 27, of which waited for: 8 -> 7; matrix products, arithmetic and copies ran while one was open for 2% -> 2% of each run, Pallas kernels for 11% -> 14%
where the time goes in v4:
time: 227 us; the launch traced here: 226 us
  starting transfers between devices  81.9 us (36%)
  Pallas kernels  74 us (33%)
  waiting for transfers between devices  57.8 us (25%)
  local copies, waits for them, and re-layouts  5.58 us (2%)
  matrix products  3.1 us (1%)
  other arithmetic  2.44 us (1%)
    ppermute x17, starting transfers between devices, shifted(): lax.ppermute(block, axis, [(i, (i + step) % count) for i in range(count)])  45.6 us
    pallas_call x1, Pallas kernels, attend(): pl.pallas_call(attend_kernel, grid=(steps,), in_specs=[flags(), flags()]...  37 us
    all_to_all x1, waiting for transfers between devices, body(): lax.all_to_all(outgoing, TY + TX, split_axis=0, concat_axis=0, tiled=True)  28.9 us
    ppermute x17, waiting for transfers between devices, shifted(): lax.ppermute(block, axis, [(i, (i + step) % count) for i in range(count)])  28.6 us
    ppermute x8, starting transfers between devices, passed_along(): return lax.ppermute(block, axis, route)  17 us
    all_to_all x1, starting transfers between devices, body(): lax.all_to_all(outgoing, TY + TX, split_axis=0, concat_axis=0, tiled=True)  11.1 us
    all_to_all x1, starting transfers between devices, body(): lax.all_to_all(sent, TY + TX, split_axis=0, concat_axis=0, tiled=True)  8.12 us
    pallas_call x1, Pallas kernels, project(): pl.pallas_call(project_kernel, grid=(width // lanes,), in_specs=[whole(),...  6.98 us
  transfers between devices with their start and end apart: 27, of which 7 were waited for; matrix products, arithmetic and copies ran while one was open for 2% of the time, Pallas kernels for 14%

profile of v4, /device:TPU:0, one launch (start us, length us, event | category | flops | bytes accessed | tf_op | source)
XLA Modules:
  0.0 225.7 jit_solution(4672409450587278469)
XLA Ops:
  0.6 3.7 %pick_rows.1 = bf16[1024,1024]{1,0:T(8,128)(2,1)} custom-call(s32[1,1024]{1,0:T(1,128)} %rows_ref.3, bf16[512,1024]{1,0:T(8,128)(2,1)} %table_ref.1), custom_call_target="tpu_custom_call" | custom-call | tf_op jit(solution)/shard_map/pick_rows/pallas_call | solution.py:36
  4.4 11.1 %all-to-all-start = ((bf16[128,8,1024]{2,1,0:T(8,128)(2,1)}), bf16[128,8,1024]{2,1,0:T(8,128)(2,1)S(1)}, u32[]{:S(2)}, u32[]{:S(2)}) async-start(bf16[128,8,1024]{2,1,0:T(8,128)(2,1)} %bitcast.35), calls=%async_computation | async-start | bytes 4194304 | tf_op jit(solution)/shard_map/all_to_all | solution.py:426
  17.0 28.9 %all-to-all-done = bf16[128,8,1024]{2,1,0:T(8,128)(2,1)S(1)} async-done(((bf16[128,8,1024]{2,1,0:T(8,128)(2,1)}), bf16[128,8,1024]{2,1,0:T(8,128)(2,1)S(1)}, u32[]{:S(2)}, u32[]{:S(2)}) %all-to-all-start) | async-done | bytes 2097184 | tf_op jit(solution)/shard_map/all_to_all | solution.py:426
  47.0 2.8 %blend_norm.1 = (bf16[256,1024]{1,0:T(8,128)(2,1)}, f32[256,1024]{1,0:T(8,128)S(1)}, f32[256,128]{1,0:T(8,128)S(1)}) custom-call(s32[256,4]{1,0:T(8,128)S(1)} %reshape.30.slots_ref, f32[256,4]{1,0:T(8,128)S(1)} %bitcast.32, bf16[1024,1024]{1,0:T(8,128)(2,1)S(1)} %bitcast.27, bf16[256,1024]{1,0:T(8,128)(2,1)S(1)} %bitcast.34, ...), custom_call_target="tpu_custom_call" | custom-call | tf_op jit(solution)/shard_map/blend_norm/pallas_call | solution.py:96
  55.5 7.0 %project.1 = (bf16[256,1024]{1,0:T(8,128)(2,1)}, bf16[256,1024]{1,0:T(8,128)(2,1)}, bf16[256,1024]{1,0:T(8,128)(2,1)}, bf16[256,1024]{1,0:T(8,128)(2,1)}) custom-call(bf16[256,1024]{1,0:T(8,128)(2,1)} %get-tuple-element.47.in_ref.own_ref, bf16[256,1024]{1,0:T(8,128)(2,1)} %bitcast.28, bf16[1024,1024]{1,0:T(8,128)(2,1)} %wq_ref.3, bf16[1024,1024]{1,0:T(8,128)(2,1)} %wk_ref.5, ...), custom_call_target="tpu_custom_call" | custom-call | flops 2100000000 | bytes 11000000 | tf_op jit(solution)/shard_map/project/pallas_call | solution.py:121
  64.1 6.0 %sides.1 = (bf16[512,1024]{1,0:T(8,128)(2,1)}, bf16[512,1024]{1,0:T(8,128)(2,1)}) custom-call(bf16[256,1024]{1,0:T(8,128)(2,1)} %copy-done.11, bf16[256,1024]{1,0:T(8,128)(2,1)} %copy-done.12, bf16[1024,1024]{1,0:T(8,128)(2,1)} %wk_ref.5, bf16[1024,1024]{1,0:T(8,128)(2,1)} %wv_ref.5), custom_call_target="tpu_custom_call" | custom-call | flops 2100000000 | bytes 8000000 | tf_op jit(solution)/shard_map/sides/pallas_call | solution.py:145
  71.1 37.0 %attend.1 = (bf16[4,2,4,128,256]{4,3,2,1,0:T(8,128)(2,1)}, bf16[4,2,4,128,256]{4,3,2,1,0:T(8,128)(2,1)}, bf16[4,2,4,128,256]{4,3,2,1,0:T(8,128)(2,1)}, bf16[4,2,...) custom-call(s32[1]{0:T(128)} %bitcast.1.core_ref, ...), custom_call_target="tpu_custom_call" | custom-call | flops 33999998976 | bytes 32000000 | tf_op jit(solution)/shard_map/attend/pallas_call | solution.py:254
  111.1 4.9 %collective-permute-start.7 = (bf16[256,1024]{1,0:T(8,128)(2,1)}, bf16[256,1024]{1,0:T(8,128)(2,1)S(1)}, u32[]{:S(2)}, u32[]{:S(2)}) collective-permute-start(bf16[256,1024]{1,0:T(8,128)(2,1)} %get-tuple-element.64), channel_id=1, source_target_pairs={{0,16},{16,32},{32,48},{48,64},{64,80},{80,96},{96,112},{1,17},{17... | collective-permute-start | bytes 1572872 | tf_op jit(solution)/shard_map/ppermute | solution.py:399
  117.4 3.8 %collective-permute-start.9 = (bf16[256,1024]{1,0:T(8,128)(2,1)}, bf16[256,1024]{1,0:T(8,128)(2,1)}, u32[]{:S(2)}, u32[]{:S(2)}) collective-permute-start(bf16[256,1024]{1,0:T(8,128)(2,1)} %get-tuple-element.66), channel_id=1, source_target_pairs={{0,1},{1,2},{2,3},{3,4},{4,5},{5,6},{6,7},{7,8},{8,9},{9,10},{10,1... | collective-permute-start | bytes 1572872 | tf_op jit(solution)/shard_map/ppermute | solution.py:399
  121.2 6.1 %split_sum.1 = (bf16[2,4,128,256]{3,2,1,0:T(8,128)(2,1)}, bf16[2,4,128,256]{3,2,1,0:T(8,128)(2,1)}, bf16[2,4,128,256]{3,2,1,0:T(8,128)(2,1)}, bf16[2,4,128,256]{...) custom-call(s32[1]{0:T(128)} %bitcast.7.refs_0_.here_ref, ...), custom_call_target="tpu_custom_call" | custom-call | flops 1000000 | bytes 12000000 | tf_op jit(solution)/shard_map/split_sum/pallas_call | solution.py:291
  135.3 8.4 %collective-permute-start.11 = (bf16[2,4,128,256]{3,2,1,0:T(8,128)(2,1)}, bf16[2,4,128,256]{3,2,1,0:T(8,128)(2,1)}, u32[]{:S(2)}, u32[]{:S(2)}) collective-permute-start(bf16[2,4,128,256]{3,2,1,0:T(8,128)(2,1)} %get-tuple-element.73), channel_id=1, source_target_pairs={{0,32},{16,48},{32,0},{48,16},{1,33},{17,49},{33,1},{49,17},{2,34}... | collective-permute-start | bytes 1572872 | tf_op jit(solution)/shard_map/ppermute | solution.py:389
  143.7 12.0 %collective-permute-start.12 = (bf16[2,4,128,256]{3,2,1,0:T(8,128)(2,1)}, bf16[2,4,128,256]{3,2,1,0:T(8,128)(2,1)}, u32[]{:S(2)}, u32[]{:S(2)}) collective-permute-start(bf16[2,4,128,256]{3,2,1,0:T(8,128)(2,1)} %get-tuple-element.74), channel_id=1, source_target_pairs={{0,48},{16,0},{32,16},{48,32},{1,49},{17,1},{33,17},{49,33},{2,50}... | collective-permute-start | bytes 1572872 | tf_op jit(solution)/shard_map/ppermute | solution.py:389
  155.8 4.4 %finish.1 = (bf16[256,1024]{1,0:T(8,128)(2,1)}, bf16[1024,1024]{1,0:T(8,128)(2,1)S(1)}) custom-call(f32[256,1024]{1,0:T(8,128)S(1)} %copy-done.2, bf16[256,1024]{1,0:T(8,128)(2,1)S(1)} %collective-permute-done.6.up_ref, bf16[256,1024]{1,0:T(8,128)(2,1)S(1)} %collective-permute-done.7.down_ref, bf16[256,1024]{1,0:T(8,128)(2,1)} %collective-permute-done.8.left_ref, ...), custom_call_target="tpu_custom_call" | custom-call | tf_op jit(solution)/shard_map/finish/pallas_call | solution.py:372
  161.5 2.5 %join_sum.2 = (bf16[2,2,2,8,1024]{4,3,2,1,0:T(8,128)(2,1)}, bf16[2,2,2,8,1024]{4,3,2,1,0:T(8,128)(2,1)}, bf16[2,2,2,8,1024]{4,3,2,1,0:T(8,128)(2,1)}, bf16[2,2,2,8,1024]{4,3,2,1,0:T(8,128)(2,1)}) custom-call(s32[1]{0:T(128)} %bitcast.7.refs_0_.here_ref, bf16[2,4,128,256]{3,2,1,0:T(8,128)(2,1)} %get-tuple-element.60.refs_0_, ...), custom_call_target="tpu_custom_call" | custom-call | flops 1000000 | bytes 6000000 | tf_op jit(solution)/shard_map/join_sum/pallas_call | solution.py:342
  164.0 3.1 %fusion = bf16[256,1024]{1,0:T(8,128)(2,1)} fusion(bf16[256,1024]{1,0:T(8,128)(2,1)S(1)} %copy-done.17, bf16[1024,1024]{1,0:T(8,128)(2,1)} %wo_ref.1, bf16[1,1,256,1024]{3,2,1,0:T(8,128)(2,1)S(1)} %copy-done.4), kind=kOutput, calls=%fused_computation.1 | convolution fusion | flops 537657344 | bytes 3670016 | tf_op jit(solution)/shard_map/dot_general | solution.py:455
  167.1 3.8 %collective-permute-done.12.refs_3_ = bf16[2,4,128,256]{3,2,1,0:T(8,128)(2,1)} collective-permute-done((bf16[2,4,128,256]{3,2,1,0:T(8,128)(2,1)}, bf16[2,4,128,256]{3,2,1,0:T(8,128)(2,1)}, u32[]{:S(2)}, u32[]{:S(2)}) %collective-permute-start.12) | collective-permute-done | bytes 524320 | tf_op jit(solution)/shard_map/ppermute | solution.py:389
  170.9 3.9 %collective-permute-done.16 = bf16[2,2,2,8,1024]{4,3,2,1,0:T(8,128)(2,1)S(1)} collective-permute-done((bf16[2,2,2,8,1024]{4,3,2,1,0:T(8,128)(2,1)}, bf16[2,2,2,8,1024]{4,3,2,1,0:T(8,128)(2,1)S(1)}, u32[]{:S(2)}, u32[]{:S(2)}) %collective-permute-start.16) | collective-permute-done | bytes 131104 | tf_op jit(solution)/shard_map/ppermute | solution.py:389
  174.8 8.1 %all-to-all-start.1 = ((bf16[128,8,1024]{2,1,0:T(8,128)(2,1)}), bf16[128,8,1024]{2,1,0:T(8,128)(2,1)S(1)}, u32[]{:S(2)}, u32[]{:S(2)}) async-start(bf16[128,8,1024]{2,1,0:T(8,128)(2,1)} %bitcast.31), calls=%async_computation.1 | async-start | bytes 4194304 | tf_op jit(solution)/shard_map/all_to_all | solution.py:460
  183.0 2.5 %collective-permute-start.20 = (bf16[2,2,2,8,1024]{4,3,2,1,0:T(8,128)(2,1)S(1)}, bf16[2,2,2,8,1024]{4,3,2,1,0:T(8,128)(2,1)S(1)}, u32[]{:S(2)}, u32[]{:S(2)}) collective-permute-start(bf16[2,2,2,8,1024]{4,3,2,1,0:T(8,128)(2,1)S(1)} %copy-done.16), channel_id=1, source_target_pairs={{0,32},{16,48},{32,0},{48,16},{1,33},{17,49},{33,1},{49,17},{2,34}... | collective-permute-start | bytes 393224 | tf_op jit(solution)/shard_map/ppermute | solution.py:389
  186.7 2.4 %join_sum.3 = (bf16[2,2,2,8,1024]{4,3,2,1,0:T(8,128)(2,1)}, bf16[2,2,2,8,1024]{4,3,2,1,0:T(8,128)(2,1)}, bf16[2,2,2,8,1024]{4,3,2,1,0:T(8,128)(2,1)}, bf16[2,2,2,8,1024]{4,3,2,1,0:T(8,128)(2,1)}) custom-call(s32[1]{0:T(128)} %bitcast.8.refs_1_.here_ref, bf16[2,4,128,256]{3,2,1,0:T(8,128)(2,1)} %get-tuple-element.61.refs_0_, ...), custom_call_target="tpu_custom_call" | custom-call | flops 1000000 | bytes 6000000 | tf_op jit(solution)/shard_map/join_sum/pallas_call | solution.py:342
  190.8 3.2 %collective-permute-start.18 = (bf16[2,2,2,8,1024]{4,3,2,1,0:T(8,128)(2,1)}, bf16[2,2,2,8,1024]{4,3,2,1,0:T(8,128)(2,1)S(1)}, u32[]{:S(2)}, u32[]{:S(2)}) collective-permute-start(bf16[2,2,2,8,1024]{4,3,2,1,0:T(8,128)(2,1)} %get-tuple-element.84), channel_id=1, source_target_pairs={{0,8},{4,12},{8,0},{12,4},{1,9},{5,13},{9,1},{13,5},{2,10},{6,14},... | collective-permute-start | bytes 393224 | tf_op jit(solution)/shard_map/ppermute | solution.py:389
  195.2 16.1 %collective-permute-done.20 = bf16[2,2,2,8,1024]{4,3,2,1,0:T(8,128)(2,1)S(1)} collective-permute-done((bf16[2,2,2,8,1024]{4,3,2,1,0:T(8,128)(2,1)S(1)}, bf16[2,2,2,8,1024]{4,3,2,1,0:T(8,128)(2,1)S(1)}, u32[]{:S(2)}, u32[]{:S(2)}) %collective-permute-start.20) | collective-permute-done | bytes 131104 | tf_op jit(solution)/shard_map/ppermute | solution.py:389
  212.4 3.7 %collective-permute-done.17 = bf16[2,2,2,8,1024]{4,3,2,1,0:T(8,128)(2,1)S(1)} collective-permute-done((bf16[2,2,2,8,1024]{4,3,2,1,0:T(8,128)(2,1)}, bf16[2,2,2,8,1024]{4,3,2,1,0:T(8,128)(2,1)S(1)}, u32[]{:S(2)}, u32[]{:S(2)}) %collective-permute-start.17) | collective-permute-done | bytes 131104 | tf_op jit(solution)/shard_map/ppermute | solution.py:389
  217.9 2.7 %collective-permute-start.23 = (bf16[4,8,1024]{2,1,0:T(8,128)(2,1)S(1)}, bf16[4,8,1024]{2,1,0:T(8,128)(2,1)S(1)}, u32[]{:S(2)}, u32[]{:S(2)}) collective-permute-start(bf16[4,8,1024]{2,1,0:T(8,128)(2,1)S(1)} %get-tuple-element.92), channel_id=1, source_target_pairs={{0,64},{2,66},{64,0},{66,2},{1,65},{3,67},{65,1},{67,3},{4,68},{6,... | collective-permute-start | bytes 196616 | tf_op jit(solution)/shard_map/ppermute | solution.py:389
  (86 shorter events, 36.6 us)
Async XLA Ops:
  4.4 41.6 %all-to-all-start = ((bf16[128,8,1024]{2,1,0:T(8,128)(2,1)}), bf16[128,8,1024]{2,1,0:T(8,128)(2,1)S(1)}, u32[]{:S(2)}, u32[]{:S(2)}) async-start(bf16[128,8,1024]{2,1,0:T(8,128)(2,1)} %bitcast.35), calls=%async_computation | async-start | bytes 4194304 | tf_op jit(solution)/shard_map/all_to_all | solution.py:426
  49.8 12.7 %collective-permute-start = (bf16[256,1024]{1,0:T(8,128)(2,1)}, bf16[256,1024]{1,0:T(8,128)(2,1)S(1)}, u32[]{:S(2)}, u32[]{:S(2)}) collective-permute-start(bf16[256,1024]{1,0:T(8,128)(2,1)} %get-tuple-element.47.in_ref.own_ref), channel_id=1, source_target_pairs={{0,1},{1,2},{2,3},{3,4},{4,5},{5,6},{6,7},{7,8},{8,9},{9,10},{10,1... | collective-permute-start | bytes 1572872 | tf_op jit(solution)/shard_map/ppermute | solution.py:399
  51.1 11.4 %collective-permute-start.1 = (bf16[256,1024]{1,0:T(8,128)(2,1)}, bf16[256,1024]{1,0:T(8,128)(2,1)S(1)}, u32[]{:S(2)}, u32[]{:S(2)}) collective-permute-start(bf16[256,1024]{1,0:T(8,128)(2,1)} %get-tuple-element.47.in_ref.own_ref), channel_id=1, source_target_pairs={{1,0},{2,1},{3,2},{4,3},{5,4},{6,5},{7,6},{8,7},{9,8},{10,9},{11,1... | collective-permute-start | bytes 1572872 | tf_op jit(solution)/shard_map/ppermute | solution.py:399
  52.4 17.7 %collective-permute-start.2 = (bf16[256,1024]{1,0:T(8,128)(2,1)}, bf16[256,1024]{1,0:T(8,128)(2,1)S(1)}, u32[]{:S(2)}, u32[]{:S(2)}) collective-permute-start(bf16[256,1024]{1,0:T(8,128)(2,1)} %get-tuple-element.47.in_ref.own_ref), channel_id=1, source_target_pairs={{0,16},{16,32},{32,48},{48,64},{64,80},{80,96},{96,112},{1,17},{17... | collective-permute-start | bytes 1572872 | tf_op jit(solution)/shard_map/ppermute | solution.py:399
  54.0 16.3 %collective-permute-start.3 = (bf16[256,1024]{1,0:T(8,128)(2,1)}, bf16[256,1024]{1,0:T(8,128)(2,1)S(1)}, u32[]{:S(2)}, u32[]{:S(2)}) collective-permute-start(bf16[256,1024]{1,0:T(8,128)(2,1)} %get-tuple-element.47.in_ref.own_ref), channel_id=1, source_target_pairs={{16,0},{32,16},{48,32},{64,48},{80,64},{96,80},{112,96},{17,1},{33... | collective-permute-start | bytes 1572872 | tf_op jit(solution)/shard_map/ppermute | solution.py:399
  108.1 9.3 %collective-permute-start.4 = (bf16[4,2,4,128,256]{4,3,2,1,0:T(8,128)(2,1)}, bf16[4,2,4,128,256]{4,3,2,1,0:T(8,128)(2,1)}, u32[]{:S(2)}, u32[]{:S(2)}) collective-permute-start(bf16[4,2,4,128,256]{4,3,2,1,0:T(8,128)(2,1)} %get-tuple-element.57), channel_id=1, source_target_pairs={{0,1},{1,0},{2,3},{3,2},{4,5},{5,4},{6,7},{7,6},{8,9},{9,8},{10,11... | collective-permute-start | bytes 6291464 | tf_op jit(solution)/shard_map/ppermute | solution.py:389
  109.8 11.5 %collective-permute-start.5 = (bf16[4,2,4,128,256]{4,3,2,1,0:T(8,128)(2,1)}, bf16[4,2,4,128,256]{4,3,2,1,0:T(8,128)(2,1)}, u32[]{:S(2)}, u32[]{:S(2)}) collective-permute-start(bf16[4,2,4,128,256]{4,3,2,1,0:T(8,128)(2,1)} %get-tuple-element.59), channel_id=1, source_target_pairs={{0,1},{1,0},{2,3},{3,2},{4,5},{5,4},{6,7},{7,6},{8,9},{9,8},{10,11... | collective-permute-start | bytes 6291464 | tf_op jit(solution)/shard_map/ppermute | solution.py:389
  109.9 19.5 %collective-permute-start.6 = (bf16[256,1024]{1,0:T(8,128)(2,1)}, bf16[256,1024]{1,0:T(8,128)(2,1)S(1)}, u32[]{:S(2)}, u32[]{:S(2)}) collective-permute-start(bf16[256,1024]{1,0:T(8,128)(2,1)} %get-tuple-element.63), channel_id=1, source_target_pairs={{16,0},{32,16},{48,32},{64,48},{80,64},{96,80},{112,96},{17,1},{33... | collective-permute-start | bytes 1572872 | tf_op jit(solution)/shard_map/ppermute | solution.py:399
  111.1 20.2 %collective-permute-start.7 = (bf16[256,1024]{1,0:T(8,128)(2,1)}, bf16[256,1024]{1,0:T(8,128)(2,1)S(1)}, u32[]{:S(2)}, u32[]{:S(2)}) collective-permute-start(bf16[256,1024]{1,0:T(8,128)(2,1)} %get-tuple-element.64), channel_id=1, source_target_pairs={{0,16},{16,32},{32,48},{48,64},{64,80},{80,96},{96,112},{1,17},{17... | collective-permute-start | bytes 1572872 | tf_op jit(solution)/shard_map/ppermute | solution.py:399
  116.1 17.2 %collective-permute-start.8 = (bf16[256,1024]{1,0:T(8,128)(2,1)}, bf16[256,1024]{1,0:T(8,128)(2,1)}, u32[]{:S(2)}, u32[]{:S(2)}) collective-permute-start(bf16[256,1024]{1,0:T(8,128)(2,1)} %get-tuple-element.65), channel_id=1, source_target_pairs={{1,0},{2,1},{3,2},{4,3},{5,4},{6,5},{7,6},{8,7},{9,8},{10,9},{11,1... | collective-permute-start | bytes 1572872 | tf_op jit(solution)/shard_map/ppermute | solution.py:399
  117.4 17.9 %collective-permute-start.9 = (bf16[256,1024]{1,0:T(8,128)(2,1)}, bf16[256,1024]{1,0:T(8,128)(2,1)}, u32[]{:S(2)}, u32[]{:S(2)}) collective-permute-start(bf16[256,1024]{1,0:T(8,128)(2,1)} %get-tuple-element.66), channel_id=1, source_target_pairs={{0,1},{1,2},{2,3},{3,4},{4,5},{5,6},{6,7},{7,8},{8,9},{9,10},{10,1... | collective-permute-start | bytes 1572872 | tf_op jit(solution)/shard_map/ppermute | solution.py:399
  127.3 16.4 %collective-permute-start.13 = (bf16[2,4,128,256]{3,2,1,0:T(8,128)(2,1)}, bf16[2,4,128,256]{3,2,1,0:T(8,128)(2,1)S(1)}, u32[]{:S(2)}, u32[]{:S(2)}) collective-permute-start(bf16[2,4,128,256]{3,2,1,0:T(8,128)(2,1)} %get-tuple-element.76), channel_id=1, source_target_pairs={{0,4},{4,8},{8,12},{12,0},{1,5},{5,9},{9,13},{13,1},{2,6},{6,10},{... | collective-permute-start | bytes 1572872 | tf_op jit(solution)/shard_map/ppermute | solution.py:389
  129.3 32.2 %collective-permute-start.14 = (bf16[2,4,128,256]{3,2,1,0:T(8,128)(2,1)}, bf16[2,4,128,256]{3,2,1,0:T(8,128)(2,1)}, u32[]{:S(2)}, u32[]{:S(2)}) collective-permute-start(bf16[2,4,128,256]{3,2,1,0:T(8,128)(2,1)} %get-tuple-element.77), channel_id=1, source_target_pairs={{0,8},{4,12},{8,0},{12,4},{1,9},{5,13},{9,1},{13,5},{2,10},{6,14},... | collective-permute-start | bytes 1572872 | tf_op jit(solution)/shard_map/ppermute | solution.py:389
  131.3 30.1 %collective-permute-start.15 = (bf16[2,4,128,256]{3,2,1,0:T(8,128)(2,1)}, bf16[2,4,128,256]{3,2,1,0:T(8,128)(2,1)}, u32[]{:S(2)}, u32[]{:S(2)}) collective-permute-start(bf16[2,4,128,256]{3,2,1,0:T(8,128)(2,1)} %get-tuple-element.78), channel_id=1, source_target_pairs={{0,12},{4,0},{8,4},{12,8},{1,13},{5,1},{9,5},{13,9},{2,14},{6,2},{... | collective-permute-start | bytes 1572872 | tf_op jit(solution)/shard_map/ppermute | solution.py:389
  133.3 33.8 %collective-permute-start.10 = (bf16[2,4,128,256]{3,2,1,0:T(8,128)(2,1)}, bf16[2,4,128,256]{3,2,1,0:T(8,128)(2,1)}, u32[]{:S(2)}, u32[]{:S(2)}) collective-permute-start(bf16[2,4,128,256]{3,2,1,0:T(8,128)(2,1)} %get-tuple-element.72), channel_id=1, source_target_pairs={{0,16},{16,32},{32,48},{48,0},{1,17},{17,33},{33,49},{49,1},{2,18}... | collective-permute-start | bytes 1572872 | tf_op jit(solution)/shard_map/ppermute | solution.py:389
  135.3 31.8 %collective-permute-start.11 = (bf16[2,4,128,256]{3,2,1,0:T(8,128)(2,1)}, bf16[2,4,128,256]{3,2,1,0:T(8,128)(2,1)}, u32[]{:S(2)}, u32[]{:S(2)}) collective-permute-start(bf16[2,4,128,256]{3,2,1,0:T(8,128)(2,1)} %get-tuple-element.73), channel_id=1, source_target_pairs={{0,32},{16,48},{32,0},{48,16},{1,33},{17,49},{33,1},{49,17},{2,34}... | collective-permute-start | bytes 1572872 | tf_op jit(solution)/shard_map/ppermute | solution.py:389
  143.7 27.2 %collective-permute-start.12 = (bf16[2,4,128,256]{3,2,1,0:T(8,128)(2,1)}, bf16[2,4,128,256]{3,2,1,0:T(8,128)(2,1)}, u32[]{:S(2)}, u32[]{:S(2)}) collective-permute-start(bf16[2,4,128,256]{3,2,1,0:T(8,128)(2,1)} %get-tuple-element.74), channel_id=1, source_target_pairs={{0,48},{16,0},{32,16},{48,32},{1,49},{17,1},{33,17},{49,33},{2,50}... | collective-permute-start | bytes 1572872 | tf_op jit(solution)/shard_map/ppermute | solution.py:389
  163.9 10.9 %collective-permute-start.16 = (bf16[2,2,2,8,1024]{4,3,2,1,0:T(8,128)(2,1)}, bf16[2,2,2,8,1024]{4,3,2,1,0:T(8,128)(2,1)S(1)}, u32[]{:S(2)}, u32[]{:S(2)}) collective-permute-start(bf16[2,2,2,8,1024]{4,3,2,1,0:T(8,128)(2,1)} %get-tuple-element.79), channel_id=1, source_target_pairs={{0,16},{16,32},{32,48},{48,0},{1,17},{17,33},{33,49},{49,1},{2,18}... | collective-permute-start | bytes 393224 | tf_op jit(solution)/shard_map/ppermute | solution.py:389
  174.8 47.9 %all-to-all-start.1 = ((bf16[128,8,1024]{2,1,0:T(8,128)(2,1)}), bf16[128,8,1024]{2,1,0:T(8,128)(2,1)S(1)}, u32[]{:S(2)}, u32[]{:S(2)}) async-start(bf16[128,8,1024]{2,1,0:T(8,128)(2,1)} %bitcast.31), calls=%async_computation.1 | async-start | bytes 4194304 | tf_op jit(solution)/shard_map/all_to_all | solution.py:460
  183.0 28.3 %collective-permute-start.20 = (bf16[2,2,2,8,1024]{4,3,2,1,0:T(8,128)(2,1)S(1)}, bf16[2,2,2,8,1024]{4,3,2,1,0:T(8,128)(2,1)S(1)}, u32[]{:S(2)}, u32[]{:S(2)}) collective-permute-start(bf16[2,2,2,8,1024]{4,3,2,1,0:T(8,128)(2,1)S(1)} %copy-done.16), channel_id=1, source_target_pairs={{0,32},{16,48},{32,0},{48,16},{1,33},{17,49},{33,1},{49,17},{2,34}... | collective-permute-start | bytes 393224 | tf_op jit(solution)/shard_map/ppermute | solution.py:389
  185.5 26.8 %collective-permute-start.21 = (bf16[2,2,2,8,1024]{4,3,2,1,0:T(8,128)(2,1)S(1)}, bf16[2,2,2,8,1024]{4,3,2,1,0:T(8,128)(2,1)S(1)}, u32[]{:S(2)}, u32[]{:S(2)}) collective-permute-start(bf16[2,2,2,8,1024]{4,3,2,1,0:T(8,128)(2,1)S(1)} %copy-done.15), channel_id=1, source_target_pairs={{0,48},{16,0},{32,16},{48,32},{1,49},{17,1},{33,17},{49,33},{2,50}... | collective-permute-start | bytes 393224 | tf_op jit(solution)/shard_map/ppermute | solution.py:389
  189.1 27.1 %collective-permute-start.17 = (bf16[2,2,2,8,1024]{4,3,2,1,0:T(8,128)(2,1)}, bf16[2,2,2,8,1024]{4,3,2,1,0:T(8,128)(2,1)S(1)}, u32[]{:S(2)}, u32[]{:S(2)}) collective-permute-start(bf16[2,2,2,8,1024]{4,3,2,1,0:T(8,128)(2,1)} %get-tuple-element.83), channel_id=1, source_target_pairs={{0,4},{4,8},{8,12},{12,0},{1,5},{5,9},{9,13},{13,1},{2,6},{6,10},{... | collective-permute-start | bytes 393224 | tf_op jit(solution)/shard_map/ppermute | solution.py:389
  190.8 25.4 %collective-permute-start.18 = (bf16[2,2,2,8,1024]{4,3,2,1,0:T(8,128)(2,1)}, bf16[2,2,2,8,1024]{4,3,2,1,0:T(8,128)(2,1)S(1)}, u32[]{:S(2)}, u32[]{:S(2)}) collective-permute-start(bf16[2,2,2,8,1024]{4,3,2,1,0:T(8,128)(2,1)} %get-tuple-element.84), channel_id=1, source_target_pairs={{0,8},{4,12},{8,0},{12,4},{1,9},{5,13},{9,1},{13,5},{2,10},{6,14},... | collective-permute-start | bytes 393224 | tf_op jit(solution)/shard_map/ppermute | solution.py:389
  194.0 22.2 %collective-permute-start.19 = (bf16[2,2,2,8,1024]{4,3,2,1,0:T(8,128)(2,1)}, bf16[2,2,2,8,1024]{4,3,2,1,0:T(8,128)(2,1)S(1)}, u32[]{:S(2)}, u32[]{:S(2)}) collective-permute-start(bf16[2,2,2,8,1024]{4,3,2,1,0:T(8,128)(2,1)} %get-tuple-element.85), channel_id=1, source_target_pairs={{0,12},{4,0},{8,4},{12,8},{1,13},{5,1},{9,5},{13,9},{2,14},{6,2},{... | collective-permute-start | bytes 393224 | tf_op jit(solution)/shard_map/ppermute | solution.py:389
  (21 other events, 236.0 us)

commit v5 on v4

--- a/solution.py
+++ b/solution.py
@@ -456,12 +456,13 @@
     updated = (state.astype(F32) + term).astype(BF16)
     here_y, here_z = after((here["y"], here["z"]), slots)
     second_y = swapped(join_sum(here_y, along_z, ys, 1, chunk), "y")
-    sent = after(slots, (along_y, updated, second_y[1]))
+    sent = after(slots, (along_y, second_y[1]))
     sent_back = lax.all_to_all(sent, TY + TX, split_axis=0, concat_axis=0, tiled=True)
     global_grad = add_rows(send_rows, sent_back, global_latent.shape[0])
     second_z = swapped(join_sum(here_z, along_y, zs, -1, chunk), "z")
     total = jnp.concatenate([sum(piece.astype(F32) for piece in group) for group in (second_z, second_y)], axis=2)
     total = total.astype(BF16).reshape(-1, 4, chunk, width)
+    total = after(total, updated)
     place = lax.axis_index(X)
     along_x = swapped([lax.dynamic_index_in_dim(total, (place + k) % total.shape[0], 0, keepdims=False) for k in range(total.shape[0])], X)
     weight_grads = sum(piece.astype(F32) for piece in after(along_x[:1], global_grad) + along_x[1:])

time: 227 us -> 228 us (level)
  transfers between devices with their start and end apart: 27 -> 27, of which waited for: 7 -> 8; matrix products, arithmetic and copies ran while one was open for 2% -> 2% of each run, Pallas kernels for 14% -> 13%
where the time goes in v5:
time: 228 us; the launch traced here: 226 us
  starting transfers between devices  82.3 us (36%)
  Pallas kernels  73.9 us (32%)
  waiting for transfers between devices  58 us (25%)
  local copies, waits for them, and re-layouts  5.6 us (2%)
  matrix products  3.1 us (1%)
  other arithmetic  2.43 us (1%)
    ppermute x17, starting transfers between devices, shifted(): lax.ppermute(block, axis, [(i, (i + step) % count) for i in range(count)])  46 us
    pallas_call x1, Pallas kernels, attend(): pl.pallas_call(attend_kernel, grid=(steps,), in_specs=[flags(), flags()]...  37 us
    all_to_all x1, waiting for transfers between devices, body(): lax.all_to_all(outgoing, TY + TX, split_axis=0, concat_axis=0, tiled=True)  28.9 us
    ppermute x17, waiting for transfers between devices, shifted(): lax.ppermute(block, axis, [(i, (i + step) % count) for i in range(count)])  28.9 us
    ppermute x8, starting transfers between devices, passed_along(): return lax.ppermute(block, axis, route)  17 us
    all_to_all x1, starting transfers between devices, body(): lax.all_to_all(outgoing, TY + TX, split_axis=0, concat_axis=0, tiled=True)  11.1 us
    all_to_all x1, starting transfers between devices, body(): lax.all_to_all(sent, TY + TX, split_axis=0, concat_axis=0, tiled=True)  8.13 us
    pallas_call x1, Pallas kernels, project(): pl.pallas_call(project_kernel, grid=(width // lanes,), in_specs=[whole(),...  6.98 us
  transfers between devices with their start and end apart: 27, of which 8 were waited for; matrix products, arithmetic and copies ran while one was open for 2% of the time, Pallas kernels for 13%

profile of v5, /device:TPU:0, one launch (start us, length us, event | category | flops | bytes accessed | tf_op | source)
XLA Modules:
  0.0 226.4 jit_solution(16526694743307924453)
XLA Ops:
  0.6 3.7 %pick_rows.1 = bf16[1024,1024]{1,0:T(8,128)(2,1)} custom-call(s32[1,1024]{1,0:T(1,128)} %rows_ref.3, bf16[512,1024]{1,0:T(8,128)(2,1)} %table_ref.1), custom_call_target="tpu_custom_call" | custom-call | tf_op jit(solution)/shard_map/pick_rows/pallas_call | solution.py:36
  4.4 11.1 %all-to-all-start = ((bf16[128,8,1024]{2,1,0:T(8,128)(2,1)}), bf16[128,8,1024]{2,1,0:T(8,128)(2,1)S(1)}, u32[]{:S(2)}, u32[]{:S(2)}) async-start(bf16[128,8,1024]{2,1,0:T(8,128)(2,1)} %bitcast.35), calls=%async_computation | async-start | bytes 4194304 | tf_op jit(solution)/shard_map/all_to_all | solution.py:426
  17.0 28.9 %all-to-all-done = bf16[128,8,1024]{2,1,0:T(8,128)(2,1)S(1)} async-done(((bf16[128,8,1024]{2,1,0:T(8,128)(2,1)}), bf16[128,8,1024]{2,1,0:T(8,128)(2,1)S(1)}, u32[]{:S(2)}, u32[]{:S(2)}) %all-to-all-start) | async-done | bytes 2097184 | tf_op jit(solution)/shard_map/all_to_all | solution.py:426
  47.0 2.8 %blend_norm.1 = (bf16[256,1024]{1,0:T(8,128)(2,1)}, f32[256,1024]{1,0:T(8,128)S(1)}, f32[256,128]{1,0:T(8,128)S(1)}) custom-call(s32[256,4]{1,0:T(8,128)S(1)} %reshape.30.slots_ref, f32[256,4]{1,0:T(8,128)S(1)} %bitcast.32, bf16[1024,1024]{1,0:T(8,128)(2,1)S(1)} %bitcast.27, bf16[256,1024]{1,0:T(8,128)(2,1)S(1)} %bitcast.34, ...), custom_call_target="tpu_custom_call" | custom-call | tf_op jit(solution)/shard_map/blend_norm/pallas_call | solution.py:96
  55.5 7.0 %project.1 = (bf16[256,1024]{1,0:T(8,128)(2,1)}, bf16[256,1024]{1,0:T(8,128)(2,1)}, bf16[256,1024]{1,0:T(8,128)(2,1)}, bf16[256,1024]{1,0:T(8,128)(2,1)}) custom-call(bf16[256,1024]{1,0:T(8,128)(2,1)} %get-tuple-element.48.in_ref.own_ref, bf16[256,1024]{1,0:T(8,128)(2,1)} %bitcast.28, bf16[1024,1024]{1,0:T(8,128)(2,1)} %wq_ref.3, bf16[1024,1024]{1,0:T(8,128)(2,1)} %wk_ref.5, ...), custom_call_target="tpu_custom_call" | custom-call | flops 2100000000 | bytes 11000000 | tf_op jit(solution)/shard_map/project/pallas_call | solution.py:121
  64.1 6.0 %sides.1 = (bf16[512,1024]{1,0:T(8,128)(2,1)}, bf16[512,1024]{1,0:T(8,128)(2,1)}) custom-call(bf16[256,1024]{1,0:T(8,128)(2,1)} %copy-done.11, bf16[256,1024]{1,0:T(8,128)(2,1)} %copy-done.12, bf16[1024,1024]{1,0:T(8,128)(2,1)} %wk_ref.5, bf16[1024,1024]{1,0:T(8,128)(2,1)} %wv_ref.5), custom_call_target="tpu_custom_call" | custom-call | flops 2100000000 | bytes 8000000 | tf_op jit(solution)/shard_map/sides/pallas_call | solution.py:145
  71.1 37.0 %attend.1 = (bf16[4,2,4,128,256]{4,3,2,1,0:T(8,128)(2,1)}, bf16[4,2,4,128,256]{4,3,2,1,0:T(8,128)(2,1)}, bf16[4,2,4,128,256]{4,3,2,1,0:T(8,128)(2,1)}, bf16[4,2,...) custom-call(s32[1]{0:T(128)} %bitcast.1.core_ref, ...), custom_call_target="tpu_custom_call" | custom-call | flops 33999998976 | bytes 32000000 | tf_op jit(solution)/shard_map/attend/pallas_call | solution.py:254
  111.1 4.9 %collective-permute-start.7 = (bf16[256,1024]{1,0:T(8,128)(2,1)}, bf16[256,1024]{1,0:T(8,128)(2,1)S(1)}, u32[]{:S(2)}, u32[]{:S(2)}) collective-permute-start(bf16[256,1024]{1,0:T(8,128)(2,1)} %get-tuple-element.65), channel_id=1, source_target_pairs={{0,16},{16,32},{32,48},{48,64},{64,80},{80,96},{96,112},{1,17},{17... | collective-permute-start | bytes 1572872 | tf_op jit(solution)/shard_map/ppermute | solution.py:399
  117.4 3.8 %collective-permute-start.9 = (bf16[256,1024]{1,0:T(8,128)(2,1)}, bf16[256,1024]{1,0:T(8,128)(2,1)}, u32[]{:S(2)}, u32[]{:S(2)}) collective-permute-start(bf16[256,1024]{1,0:T(8,128)(2,1)} %get-tuple-element.67), channel_id=1, source_target_pairs={{0,1},{1,2},{2,3},{3,4},{4,5},{5,6},{6,7},{7,8},{8,9},{9,10},{10,1... | collective-permute-start | bytes 1572872 | tf_op jit(solution)/shard_map/ppermute | solution.py:399
  121.2 6.1 %split_sum.1 = (bf16[2,4,128,256]{3,2,1,0:T(8,128)(2,1)}, bf16[2,4,128,256]{3,2,1,0:T(8,128)(2,1)}, bf16[2,4,128,256]{3,2,1,0:T(8,128)(2,1)}, bf16[2,4,128,256]{...) custom-call(s32[1]{0:T(128)} %bitcast.7.refs_0_.here_ref, ...), custom_call_target="tpu_custom_call" | custom-call | flops 1000000 | bytes 12000000 | tf_op jit(solution)/shard_map/split_sum/pallas_call | solution.py:291
  135.3 8.4 %collective-permute-start.11 = (bf16[2,4,128,256]{3,2,1,0:T(8,128)(2,1)}, bf16[2,4,128,256]{3,2,1,0:T(8,128)(2,1)}, u32[]{:S(2)}, u32[]{:S(2)}) collective-permute-start(bf16[2,4,128,256]{3,2,1,0:T(8,128)(2,1)} %get-tuple-element.74), channel_id=1, source_target_pairs={{0,32},{16,48},{32,0},{48,16},{1,33},{17,49},{33,1},{49,17},{2,34}... | collective-permute-start | bytes 1572872 | tf_op jit(solution)/shard_map/ppermute | solution.py:389
  143.7 12.0 %collective-permute-start.12 = (bf16[2,4,128,256]{3,2,1,0:T(8,128)(2,1)}, bf16[2,4,128,256]{3,2,1,0:T(8,128)(2,1)}, u32[]{:S(2)}, u32[]{:S(2)}) collective-permute-start(bf16[2,4,128,256]{3,2,1,0:T(8,128)(2,1)} %get-tuple-element.75), channel_id=1, source_target_pairs={{0,48},{16,0},{32,16},{48,32},{1,49},{17,1},{33,17},{49,33},{2,50}... | collective-permute-start | bytes 1572872 | tf_op jit(solution)/shard_map/ppermute | solution.py:389
  155.8 4.4 %finish.1 = (bf16[256,1024]{1,0:T(8,128)(2,1)}, bf16[1024,1024]{1,0:T(8,128)(2,1)S(1)}) custom-call(f32[256,1024]{1,0:T(8,128)S(1)} %copy-done.2, bf16[256,1024]{1,0:T(8,128)(2,1)S(1)} %collective-permute-done.6.up_ref, bf16[256,1024]{1,0:T(8,128)(2,1)S(1)} %collective-permute-done.7.down_ref, bf16[256,1024]{1,0:T(8,128)(2,1)} %collective-permute-done.8.left_ref, ...), custom_call_target="tpu_custom_call" | custom-call | tf_op jit(solution)/shard_map/finish/pallas_call | solution.py:372
  161.5 2.4 %join_sum.2 = (bf16[2,2,2,8,1024]{4,3,2,1,0:T(8,128)(2,1)}, bf16[2,2,2,8,1024]{4,3,2,1,0:T(8,128)(2,1)}, bf16[2,2,2,8,1024]{4,3,2,1,0:T(8,128)(2,1)}, bf16[2,2,2,8,1024]{4,3,2,1,0:T(8,128)(2,1)}) custom-call(s32[1]{0:T(128)} %bitcast.7.refs_0_.here_ref, bf16[2,4,128,256]{3,2,1,0:T(8,128)(2,1)} %get-tuple-element.61.refs_0_, ...), custom_call_target="tpu_custom_call" | custom-call | flops 1000000 | bytes 6000000 | tf_op jit(solution)/shard_map/join_sum/pallas_call | solution.py:342
  163.9 7.0 %collective-permute-done.12.refs_3_ = bf16[2,4,128,256]{3,2,1,0:T(8,128)(2,1)} collective-permute-done((bf16[2,4,128,256]{3,2,1,0:T(8,128)(2,1)}, bf16[2,4,128,256]{3,2,1,0:T(8,128)(2,1)}, u32[]{:S(2)}, u32[]{:S(2)}) %collective-permute-start.12) | collective-permute-done | bytes 524320 | tf_op jit(solution)/shard_map/ppermute | solution.py:389
  170.9 3.9 %collective-permute-done.16 = bf16[2,2,2,8,1024]{4,3,2,1,0:T(8,128)(2,1)S(1)} collective-permute-done((bf16[2,2,2,8,1024]{4,3,2,1,0:T(8,128)(2,1)}, bf16[2,2,2,8,1024]{4,3,2,1,0:T(8,128)(2,1)S(1)}, u32[]{:S(2)}, u32[]{:S(2)}) %collective-permute-start.16) | collective-permute-done | bytes 131104 | tf_op jit(solution)/shard_map/ppermute | solution.py:389
  174.8 8.1 %all-to-all-start.1 = ((bf16[128,8,1024]{2,1,0:T(8,128)(2,1)}), bf16[128,8,1024]{2,1,0:T(8,128)(2,1)S(1)}, u32[]{:S(2)}, u32[]{:S(2)}) async-start(bf16[128,8,1024]{2,1,0:T(8,128)(2,1)} %bitcast.31), calls=%async_computation.1 | async-start | bytes 4194304 | tf_op jit(solution)/shard_map/all_to_all | solution.py:460
  183.0 2.5 %collective-permute-start.20 = (bf16[2,2,2,8,1024]{4,3,2,1,0:T(8,128)(2,1)S(1)}, bf16[2,2,2,8,1024]{4,3,2,1,0:T(8,128)(2,1)S(1)}, u32[]{:S(2)}, u32[]{:S(2)}) collective-permute-start(bf16[2,2,2,8,1024]{4,3,2,1,0:T(8,128)(2,1)S(1)} %copy-done.16), channel_id=1, source_target_pairs={{0,32},{16,48},{32,0},{48,16},{1,33},{17,49},{33,1},{49,17},{2,34}... | collective-permute-start | bytes 393224 | tf_op jit(solution)/shard_map/ppermute | solution.py:389
  186.8 3.1 %fusion = bf16[256,1024]{1,0:T(8,128)(2,1)} fusion(bf16[256,1024]{1,0:T(8,128)(2,1)S(1)} %copy-done.17, bf16[1024,1024]{1,0:T(8,128)(2,1)} %wo_ref.1, bf16[1,1,256,1024]{3,2,1,0:T(8,128)(2,1)S(1)} %copy-done.4), kind=kOutput, calls=%fused_computation.1 | convolution fusion | flops 537657344 | bytes 3670016 | tf_op jit(solution)/shard_map/dot_general | solution.py:455
  189.9 2.4 %join_sum.3 = (bf16[2,2,2,8,1024]{4,3,2,1,0:T(8,128)(2,1)}, bf16[2,2,2,8,1024]{4,3,2,1,0:T(8,128)(2,1)}, bf16[2,2,2,8,1024]{4,3,2,1,0:T(8,128)(2,1)}, bf16[2,2,2,8,1024]{4,3,2,1,0:T(8,128)(2,1)}) custom-call(s32[1]{0:T(128)} %bitcast.8.refs_1_.here_ref, bf16[2,4,128,256]{3,2,1,0:T(8,128)(2,1)} %get-tuple-element.62.refs_0_, ...), custom_call_target="tpu_custom_call" | custom-call | flops 1000000 | bytes 6000000 | tf_op jit(solution)/shard_map/join_sum/pallas_call | solution.py:342
  193.9 3.2 %collective-permute-start.18 = (bf16[2,2,2,8,1024]{4,3,2,1,0:T(8,128)(2,1)}, bf16[2,2,2,8,1024]{4,3,2,1,0:T(8,128)(2,1)S(1)}, u32[]{:S(2)}, u32[]{:S(2)}) collective-permute-start(bf16[2,2,2,8,1024]{4,3,2,1,0:T(8,128)(2,1)} %get-tuple-element.85), channel_id=1, source_target_pairs={{0,8},{4,12},{8,0},{12,4},{1,9},{5,13},{9,1},{13,5},{2,10},{6,14},... | collective-permute-start | bytes 393224 | tf_op jit(solution)/shard_map/ppermute | solution.py:389
  198.4 12.9 %collective-permute-done.20 = bf16[2,2,2,8,1024]{4,3,2,1,0:T(8,128)(2,1)S(1)} collective-permute-done((bf16[2,2,2,8,1024]{4,3,2,1,0:T(8,128)(2,1)S(1)}, bf16[2,2,2,8,1024]{4,3,2,1,0:T(8,128)(2,1)S(1)}, u32[]{:S(2)}, u32[]{:S(2)}) %collective-permute-start.20) | collective-permute-done | bytes 131104 | tf_op jit(solution)/shard_map/ppermute | solution.py:389
  213.4 2.9 %collective-permute-done.18 = bf16[2,2,2,8,1024]{4,3,2,1,0:T(8,128)(2,1)S(1)} collective-permute-done((bf16[2,2,2,8,1024]{4,3,2,1,0:T(8,128)(2,1)}, bf16[2,2,2,8,1024]{4,3,2,1,0:T(8,128)(2,1)S(1)}, u32[]{:S(2)}, u32[]{:S(2)}) %collective-permute-start.18) | collective-permute-done | bytes 131104 | tf_op jit(solution)/shard_map/ppermute | solution.py:389
  221.0 2.5 %collective-permute-start.24 = (bf16[4,8,1024]{2,1,0:T(8,128)(2,1)S(1)}, bf16[4,8,1024]{2,1,0:T(8,128)(2,1)S(1)}, u32[]{:S(2)}, u32[]{:S(2)}) collective-permute-start(bf16[4,8,1024]{2,1,0:T(8,128)(2,1)S(1)} %get-tuple-element.93), channel_id=1, source_target_pairs={{0,66},{2,0},{64,2},{66,64},{1,67},{3,1},{65,3},{67,65},{4,70},{6,... | collective-permute-start | bytes 196616 | tf_op jit(solution)/shard_map/ppermute | solution.py:389
  (87 shorter events, 38.2 us)
Async XLA Ops:
  4.4 41.6 %all-to-all-start = ((bf16[128,8,1024]{2,1,0:T(8,128)(2,1)}), bf16[128,8,1024]{2,1,0:T(8,128)(2,1)S(1)}, u32[]{:S(2)}, u32[]{:S(2)}) async-start(bf16[128,8,1024]{2,1,0:T(8,128)(2,1)} %bitcast.35), calls=%async_computation | async-start | bytes 4194304 | tf_op jit(solution)/shard_map/all_to_all | solution.py:426
  49.8 12.7 %collective-permute-start = (bf16[256,1024]{1,0:T(8,128)(2,1)}, bf16[256,1024]{1,0:T(8,128)(2,1)S(1)}, u32[]{:S(2)}, u32[]{:S(2)}) collective-permute-start(bf16[256,1024]{1,0:T(8,128)(2,1)} %get-tuple-element.48.in_ref.own_ref), channel_id=1, source_target_pairs={{0,1},{1,2},{2,3},{3,4},{4,5},{5,6},{6,7},{7,8},{8,9},{9,10},{10,1... | collective-permute-start | bytes 1572872 | tf_op jit(solution)/shard_map/ppermute | solution.py:399
  51.1 11.4 %collective-permute-start.1 = (bf16[256,1024]{1,0:T(8,128)(2,1)}, bf16[256,1024]{1,0:T(8,128)(2,1)S(1)}, u32[]{:S(2)}, u32[]{:S(2)}) collective-permute-start(bf16[256,1024]{1,0:T(8,128)(2,1)} %get-tuple-element.48.in_ref.own_ref), channel_id=1, source_target_pairs={{1,0},{2,1},{3,2},{4,3},{5,4},{6,5},{7,6},{8,7},{9,8},{10,9},{11,1... | collective-permute-start | bytes 1572872 | tf_op jit(solution)/shard_map/ppermute | solution.py:399
  52.4 17.7 %collective-permute-start.2 = (bf16[256,1024]{1,0:T(8,128)(2,1)}, bf16[256,1024]{1,0:T(8,128)(2,1)S(1)}, u32[]{:S(2)}, u32[]{:S(2)}) collective-permute-start(bf16[256,1024]{1,0:T(8,128)(2,1)} %get-tuple-element.48.in_ref.own_ref), channel_id=1, source_target_pairs={{0,16},{16,32},{32,48},{48,64},{64,80},{80,96},{96,112},{1,17},{17... | collective-permute-start | bytes 1572872 | tf_op jit(solution)/shard_map/ppermute | solution.py:399
  54.0 16.3 %collective-permute-start.3 = (bf16[256,1024]{1,0:T(8,128)(2,1)}, bf16[256,1024]{1,0:T(8,128)(2,1)S(1)}, u32[]{:S(2)}, u32[]{:S(2)}) collective-permute-start(bf16[256,1024]{1,0:T(8,128)(2,1)} %get-tuple-element.48.in_ref.own_ref), channel_id=1, source_target_pairs={{16,0},{32,16},{48,32},{64,48},{80,64},{96,80},{112,96},{17,1},{33... | collective-permute-start | bytes 1572872 | tf_op jit(solution)/shard_map/ppermute | solution.py:399
  108.1 9.3 %collective-permute-start.4 = (bf16[4,2,4,128,256]{4,3,2,1,0:T(8,128)(2,1)}, bf16[4,2,4,128,256]{4,3,2,1,0:T(8,128)(2,1)}, u32[]{:S(2)}, u32[]{:S(2)}) collective-permute-start(bf16[4,2,4,128,256]{4,3,2,1,0:T(8,128)(2,1)} %get-tuple-element.58), channel_id=1, source_target_pairs={{0,1},{1,0},{2,3},{3,2},{4,5},{5,4},{6,7},{7,6},{8,9},{9,8},{10,11... | collective-permute-start | bytes 6291464 | tf_op jit(solution)/shard_map/ppermute | solution.py:389
  109.8 11.5 %collective-permute-start.5 = (bf16[4,2,4,128,256]{4,3,2,1,0:T(8,128)(2,1)}, bf16[4,2,4,128,256]{4,3,2,1,0:T(8,128)(2,1)}, u32[]{:S(2)}, u32[]{:S(2)}) collective-permute-start(bf16[4,2,4,128,256]{4,3,2,1,0:T(8,128)(2,1)} %get-tuple-element.60), channel_id=1, source_target_pairs={{0,1},{1,0},{2,3},{3,2},{4,5},{5,4},{6,7},{7,6},{8,9},{9,8},{10,11... | collective-permute-start | bytes 6291464 | tf_op jit(solution)/shard_map/ppermute | solution.py:389
  109.9 19.5 %collective-permute-start.6 = (bf16[256,1024]{1,0:T(8,128)(2,1)}, bf16[256,1024]{1,0:T(8,128)(2,1)S(1)}, u32[]{:S(2)}, u32[]{:S(2)}) collective-permute-start(bf16[256,1024]{1,0:T(8,128)(2,1)} %get-tuple-element.64), channel_id=1, source_target_pairs={{16,0},{32,16},{48,32},{64,48},{80,64},{96,80},{112,96},{17,1},{33... | collective-permute-start | bytes 1572872 | tf_op jit(solution)/shard_map/ppermute | solution.py:399
  111.1 20.2 %collective-permute-start.7 = (bf16[256,1024]{1,0:T(8,128)(2,1)}, bf16[256,1024]{1,0:T(8,128)(2,1)S(1)}, u32[]{:S(2)}, u32[]{:S(2)}) collective-permute-start(bf16[256,1024]{1,0:T(8,128)(2,1)} %get-tuple-element.65), channel_id=1, source_target_pairs={{0,16},{16,32},{32,48},{48,64},{64,80},{80,96},{96,112},{1,17},{17... | collective-permute-start | bytes 1572872 | tf_op jit(solution)/shard_map/ppermute | solution.py:399
  116.1 17.2 %collective-permute-start.8 = (bf16[256,1024]{1,0:T(8,128)(2,1)}, bf16[256,1024]{1,0:T(8,128)(2,1)}, u32[]{:S(2)}, u32[]{:S(2)}) collective-permute-start(bf16[256,1024]{1,0:T(8,128)(2,1)} %get-tuple-element.66), channel_id=1, source_target_pairs={{1,0},{2,1},{3,2},{4,3},{5,4},{6,5},{7,6},{8,7},{9,8},{10,9},{11,1... | collective-permute-start | bytes 1572872 | tf_op jit(solution)/shard_map/ppermute | solution.py:399
  117.4 17.9 %collective-permute-start.9 = (bf16[256,1024]{1,0:T(8,128)(2,1)}, bf16[256,1024]{1,0:T(8,128)(2,1)}, u32[]{:S(2)}, u32[]{:S(2)}) collective-permute-start(bf16[256,1024]{1,0:T(8,128)(2,1)} %get-tuple-element.67), channel_id=1, source_target_pairs={{0,1},{1,2},{2,3},{3,4},{4,5},{5,6},{6,7},{7,8},{8,9},{9,10},{10,1... | collective-permute-start | bytes 1572872 | tf_op jit(solution)/shard_map/ppermute | solution.py:399
  127.3 16.4 %collective-permute-start.13 = (bf16[2,4,128,256]{3,2,1,0:T(8,128)(2,1)}, bf16[2,4,128,256]{3,2,1,0:T(8,128)(2,1)S(1)}, u32[]{:S(2)}, u32[]{:S(2)}) collective-permute-start(bf16[2,4,128,256]{3,2,1,0:T(8,128)(2,1)} %get-tuple-element.77), channel_id=1, source_target_pairs={{0,4},{4,8},{8,12},{12,0},{1,5},{5,9},{9,13},{13,1},{2,6},{6,10},{... | collective-permute-start | bytes 1572872 | tf_op jit(solution)/shard_map/ppermute | solution.py:389
  129.3 32.2 %collective-permute-start.14 = (bf16[2,4,128,256]{3,2,1,0:T(8,128)(2,1)}, bf16[2,4,128,256]{3,2,1,0:T(8,128)(2,1)}, u32[]{:S(2)}, u32[]{:S(2)}) collective-permute-start(bf16[2,4,128,256]{3,2,1,0:T(8,128)(2,1)} %get-tuple-element.78), channel_id=1, source_target_pairs={{0,8},{4,12},{8,0},{12,4},{1,9},{5,13},{9,1},{13,5},{2,10},{6,14},... | collective-permute-start | bytes 1572872 | tf_op jit(solution)/shard_map/ppermute | solution.py:389
  131.3 30.1 %collective-permute-start.15 = (bf16[2,4,128,256]{3,2,1,0:T(8,128)(2,1)}, bf16[2,4,128,256]{3,2,1,0:T(8,128)(2,1)}, u32[]{:S(2)}, u32[]{:S(2)}) collective-permute-start(bf16[2,4,128,256]{3,2,1,0:T(8,128)(2,1)} %get-tuple-element.79), channel_id=1, source_target_pairs={{0,12},{4,0},{8,4},{12,8},{1,13},{5,1},{9,5},{13,9},{2,14},{6,2},{... | collective-permute-start | bytes 1572872 | tf_op jit(solution)/shard_map/ppermute | solution.py:389
  133.3 30.6 %collective-permute-start.10 = (bf16[2,4,128,256]{3,2,1,0:T(8,128)(2,1)}, bf16[2,4,128,256]{3,2,1,0:T(8,128)(2,1)}, u32[]{:S(2)}, u32[]{:S(2)}) collective-permute-start(bf16[2,4,128,256]{3,2,1,0:T(8,128)(2,1)} %get-tuple-element.73), channel_id=1, source_target_pairs={{0,16},{16,32},{32,48},{48,0},{1,17},{17,33},{33,49},{49,1},{2,18}... | collective-permute-start | bytes 1572872 | tf_op jit(solution)/shard_map/ppermute | solution.py:389
  135.3 28.6 %collective-permute-start.11 = (bf16[2,4,128,256]{3,2,1,0:T(8,128)(2,1)}, bf16[2,4,128,256]{3,2,1,0:T(8,128)(2,1)}, u32[]{:S(2)}, u32[]{:S(2)}) collective-permute-start(bf16[2,4,128,256]{3,2,1,0:T(8,128)(2,1)} %get-tuple-element.74), channel_id=1, source_target_pairs={{0,32},{16,48},{32,0},{48,16},{1,33},{17,49},{33,1},{49,17},{2,34}... | collective-permute-start | bytes 1572872 | tf_op jit(solution)/shard_map/ppermute | solution.py:389
  143.7 27.2 %collective-permute-start.12 = (bf16[2,4,128,256]{3,2,1,0:T(8,128)(2,1)}, bf16[2,4,128,256]{3,2,1,0:T(8,128)(2,1)}, u32[]{:S(2)}, u32[]{:S(2)}) collective-permute-start(bf16[2,4,128,256]{3,2,1,0:T(8,128)(2,1)} %get-tuple-element.75), channel_id=1, source_target_pairs={{0,48},{16,0},{32,16},{48,32},{1,49},{17,1},{33,17},{49,33},{2,50}... | collective-permute-start | bytes 1572872 | tf_op jit(solution)/shard_map/ppermute | solution.py:389
  163.9 11.0 %collective-permute-start.16 = (bf16[2,2,2,8,1024]{4,3,2,1,0:T(8,128)(2,1)}, bf16[2,2,2,8,1024]{4,3,2,1,0:T(8,128)(2,1)S(1)}, u32[]{:S(2)}, u32[]{:S(2)}) collective-permute-start(bf16[2,2,2,8,1024]{4,3,2,1,0:T(8,128)(2,1)} %get-tuple-element.80), channel_id=1, source_target_pairs={{0,16},{16,32},{32,48},{48,0},{1,17},{17,33},{33,49},{49,1},{2,18}... | collective-permute-start | bytes 393224 | tf_op jit(solution)/shard_map/ppermute | solution.py:389
  174.8 48.6 %all-to-all-start.1 = ((bf16[128,8,1024]{2,1,0:T(8,128)(2,1)}), bf16[128,8,1024]{2,1,0:T(8,128)(2,1)S(1)}, u32[]{:S(2)}, u32[]{:S(2)}) async-start(bf16[128,8,1024]{2,1,0:T(8,128)(2,1)} %bitcast.31), calls=%async_computation.1 | async-start | bytes 4194304 | tf_op jit(solution)/shard_map/all_to_all | solution.py:460
  183.0 28.2 %collective-permute-start.20 = (bf16[2,2,2,8,1024]{4,3,2,1,0:T(8,128)(2,1)S(1)}, bf16[2,2,2,8,1024]{4,3,2,1,0:T(8,128)(2,1)S(1)}, u32[]{:S(2)}, u32[]{:S(2)}) collective-permute-start(bf16[2,2,2,8,1024]{4,3,2,1,0:T(8,128)(2,1)S(1)} %copy-done.16), channel_id=1, source_target_pairs={{0,32},{16,48},{32,0},{48,16},{1,33},{17,49},{33,1},{49,17},{2,34}... | collective-permute-start | bytes 393224 | tf_op jit(solution)/shard_map/ppermute | solution.py:389
  185.6 26.8 %collective-permute-start.21 = (bf16[2,2,2,8,1024]{4,3,2,1,0:T(8,128)(2,1)S(1)}, bf16[2,2,2,8,1024]{4,3,2,1,0:T(8,128)(2,1)S(1)}, u32[]{:S(2)}, u32[]{:S(2)}) collective-permute-start(bf16[2,2,2,8,1024]{4,3,2,1,0:T(8,128)(2,1)S(1)} %copy-done.15), channel_id=1, source_target_pairs={{0,48},{16,0},{32,16},{48,32},{1,49},{17,1},{33,17},{49,33},{2,50}... | collective-permute-start | bytes 393224 | tf_op jit(solution)/shard_map/ppermute | solution.py:389
  192.3 21.2 %collective-permute-start.17 = (bf16[2,2,2,8,1024]{4,3,2,1,0:T(8,128)(2,1)}, bf16[2,2,2,8,1024]{4,3,2,1,0:T(8,128)(2,1)S(1)}, u32[]{:S(2)}, u32[]{:S(2)}) collective-permute-start(bf16[2,2,2,8,1024]{4,3,2,1,0:T(8,128)(2,1)} %get-tuple-element.84), channel_id=1, source_target_pairs={{0,4},{4,8},{8,12},{12,0},{1,5},{5,9},{9,13},{13,1},{2,6},{6,10},{... | collective-permute-start | bytes 393224 | tf_op jit(solution)/shard_map/ppermute | solution.py:389
  193.9 22.4 %collective-permute-start.18 = (bf16[2,2,2,8,1024]{4,3,2,1,0:T(8,128)(2,1)}, bf16[2,2,2,8,1024]{4,3,2,1,0:T(8,128)(2,1)S(1)}, u32[]{:S(2)}, u32[]{:S(2)}) collective-permute-start(bf16[2,2,2,8,1024]{4,3,2,1,0:T(8,128)(2,1)} %get-tuple-element.85), channel_id=1, source_target_pairs={{0,8},{4,12},{8,0},{12,4},{1,9},{5,13},{9,1},{13,5},{2,10},{6,14},... | collective-permute-start | bytes 393224 | tf_op jit(solution)/shard_map/ppermute | solution.py:389
  197.2 19.2 %collective-permute-start.19 = (bf16[2,2,2,8,1024]{4,3,2,1,0:T(8,128)(2,1)}, bf16[2,2,2,8,1024]{4,3,2,1,0:T(8,128)(2,1)S(1)}, u32[]{:S(2)}, u32[]{:S(2)}) collective-permute-start(bf16[2,2,2,8,1024]{4,3,2,1,0:T(8,128)(2,1)} %get-tuple-element.86), channel_id=1, source_target_pairs={{0,12},{4,0},{8,4},{12,8},{1,13},{5,1},{9,5},{13,9},{2,14},{6,2},{... | collective-permute-start | bytes 393224 | tf_op jit(solution)/shard_map/ppermute | solution.py:389
  (21 other events, 246.6 us)
